TPU v7x, 32 devices: a whole 2x2x4 slice. The times are simulated.
32 devices in a mesh: groups: 2 (over y), seq: 16 (over z, x, core).
Axes of the slice: x: 2, y: 2, z: 4, core: 2. Of those that a mesh axis runs over, the one named last changes fastest.
Arguments:
- queries: bfloat16 [12288, 2048], P(('groups', 'seq')), parts along dimension 0, may hold values from -6 to 6
- keys: bfloat16 [12288, 2048], P(('groups', 'seq')), parts along dimension 0, may hold values from -6 to 6
- values: bfloat16 [12288, 2048], P(('groups', 'seq')), parts along dimension 0, may hold values from -6 to 6
- out_grad: bfloat16 [12288, 2048], P(('groups', 'seq')), parts along dimension 0, may hold values from -6 to 6
Outputs:
- grad_queries: bfloat16 [12288, 2048], P(('groups', 'seq')), parts along dimension 0
- grad_keys: bfloat16 [12288, 2048], P(('groups', 'seq')), parts along dimension 0
- grad_values: bfloat16 [12288, 2048], P(('groups', 'seq')), parts along dimension 0
There are 2 independent parts, one for each index of `groups`. A program takes and returns all parts, laid end to end along the dimension named above; each array names one. Nothing has to cross between parts.
All inputs are finite; a program needn't handle non-finite values.
Results may differ from a plain program's by a relative error of at most 0.0049.
Values sent between devices are 32-bit elements; how exact they have to be, the bound alone decides.
No kernel may reach another device: no remote copies, remote signals or barrier semaphores. Data moves between devices by JAX's collectives and lax.ppermute only.
A program may use at most 64 MiB of HBM per device.

v0:
```python
import jax
import jax.numpy as jnp
from jax import lax
from jax.sharding import PartitionSpec as P

HD = 128


def passed_along(value, axis, by):
    size = lax.axis_size(axis)
    pairs = [(i, i + by) for i in range(size) if 0 <= i + by < size]
    return lax.ppermute(value, axis, pairs)


def local(queries, keys, values, out_grad):
    rows = queries.shape[0]
    heads = queries.shape[1] // HD
    devices_seq = lax.axis_size("seq")
    scale = 1.0 / jnp.sqrt(jnp.float32(HD * rows * devices_seq))
    qb = queries.reshape(rows, heads, HD)
    kb = keys.reshape(rows, heads, HD)
    vb = values.reshape(rows, heads, HD)
    gb = out_grad.reshape(rows, heads, HD)
    kv_local = jnp.einsum("shd,she->hde", kb, vb, preferred_element_type=jnp.float32)
    qg_local = jnp.einsum("shd,she->hde", qb, gb, preferred_element_type=jnp.float32)
    kv_upto = kv_local
    qg_from = qg_local
    for level in range(devices_seq.bit_length()):
        stride = 1 << level
        if stride < devices_seq:
            kv_upto = kv_upto + passed_along(kv_upto, "seq", stride)
            qg_from = qg_from + passed_along(qg_from, "seq", -stride)
    kv_state = kv_upto - kv_local
    qg_state = qg_from - qg_local
    kvs = kv_state.astype(jnp.bfloat16)
    qgs = qg_state.astype(jnp.bfloat16)
    lower = jnp.tril(jnp.ones((rows, rows), jnp.float32))
    weights = (
        jnp.einsum("thd,shd->hts", qb, kb, preferred_element_type=jnp.float32) * scale * lower
    ).astype(jnp.bfloat16)
    grad_scores = (
        jnp.einsum("thd,shd->hts", gb, vb, preferred_element_type=jnp.float32) * scale * lower
    ).astype(jnp.bfloat16)
    grad_q = jnp.einsum(
        "hts,shd->thd", grad_scores, kb, preferred_element_type=jnp.float32
    ) + scale * jnp.einsum("the,hde->thd", gb, kvs, preferred_element_type=jnp.float32)
    grad_k = jnp.einsum(
        "hts,thd->shd", grad_scores, qb, preferred_element_type=jnp.float32
    ) + scale * jnp.einsum("she,hde->shd", vb, qgs, preferred_element_type=jnp.float32)
    grad_v = jnp.einsum(
        "hts,the->she", weights, gb, preferred_element_type=jnp.float32
    ) + scale * jnp.einsum("shd,hde->she", kb, qgs, preferred_element_type=jnp.float32)
    width = heads * HD
    return (
        grad_q.astype(jnp.bfloat16).reshape(rows, width),
        grad_k.astype(jnp.bfloat16).reshape(rows, width),
        grad_v.astype(jnp.bfloat16).reshape(rows, width),
    )


def solution(mesh):
    in_specs = (
        P(("groups", "seq"), None),
        P(("groups", "seq"), None),
        P(("groups", "seq"), None),
        P(("groups", "seq"), None),
    )
    out_specs = (P(("groups", "seq"), None), P(("groups", "seq"), None), P(("groups", "seq"), None))
    return jax.shard_map(local, mesh=mesh, in_specs=in_specs, out_specs=out_specs, check_vma=False)
```

profile of v0, /device:TPU:0, one launch (start us, length us, event | category | flops | bytes accessed | tf_op | source)
XLA Modules:
  0.0 176.8 jit_solution(15084737286757852154)
XLA Ops:
  0.6 1.4 copy-done
  2.0 3.1 %fusion.15 = f32[16,128,128]{2,1,0:T(8,128)} fusion(bf16[384,2048]{1,0:T(8,128)(2,1)} %param.5, bf16[384,2048]{1,0:T(8,128)(2,1)S(1)} %copy-done), kind=kOutput, calls=%fused_computation.17 | convolution fusion | flops 201326592 | bytes 4194304 | tf_op jit(solution)/shard_map/shd,she->hde/dot_general | solution.py:24
  5.1 3.3 %collective-permute-start = (f32[16,128,128]{2,1,0:T(8,128)}, f32[16,128,128]{2,1,0:T(8,128)}, u32[]{:S(2)}, u32[]{:S(2)}) collective-permute-start(f32[16,128,128]{2,1,0:T(8,128)} %fusion.15), channel_id=1, source_target_pairs={{0,1},{1,2},{2,3},{3,4},{4,5},{5,6},{6,7},{7,8},{8,9},{9,10},{10,1... | collective-permute-start | bytes 3145736 | tf_op jit(solution)/shard_map/ppermute | solution.py:12
  8.5 1.9 %copy.25 = bf16[384,2048]{0,1:T(8,128)(2,1)S(1)} copy(bf16[384,2048]{1,0:T(8,128)(2,1)} %param.7) | data formatting | bytes 3145728 | tf_op jit(solution)/shard_map/reshape | solution.py:23
  10.3 2.2 %fusion.7 = f32[16,128,128]{2,1,0:T(8,128)S(1)} fusion(bf16[384,16,128]{0,2,1:T(8,128)(2,1)S(1)} %bitcast.90, bf16[384,2048]{1,0:T(8,128)(2,1)} %param.4), kind=kOutput, calls=%fused_computation.11 | convolution fusion | flops 201326592 | bytes 4194304 | tf_op jit(solution)/shard_map/shd,she->hde/dot_general | solution.py:25
  12.5 1.3 collective-permute-start.4
  13.8 1.7 add.33
  15.5 23.9 %collective-permute-start.1 = (f32[16,128,128]{2,1,0:T(8,128)S(1)}, f32[16,128,128]{2,1,0:T(8,128)S(1)}, u32[]{:S(2)}, u32[]{:S(2)}) collective-permute-start(f32[16,128,128]{2,1,0:T(8,128)S(1)} %add.33), channel_id=1, source_target_pairs={{0,2},{1,3},{2,4},{3,5},{4,6},{5,7},{6,8},{7,9},{8,10},{9,11},{10,... | collective-permute-start | bytes 3145736 | tf_op jit(solution)/shard_map/ppermute | solution.py:12
  39.5 1.3 collective-permute-start.5
  40.8 40.8 %collective-permute-done.1 = f32[16,128,128]{2,1,0:T(8,128)S(1)} collective-permute-done((f32[16,128,128]{2,1,0:T(8,128)S(1)}, f32[16,128,128]{2,1,0:T(8,128)S(1)}, u32[]{:S(2)}, u32[]{:S(2)}) %collective-permute-start.1) | collective-permute-done | bytes 1048608 | tf_op jit(solution)/shard_map/ppermute | solution.py:12
  81.8 4.2 %collective-permute-start.2 = (f32[16,128,128]{2,1,0:T(8,128)S(1)}, f32[16,128,128]{2,1,0:T(8,128)S(1)}, u32[]{:S(2)}, u32[]{:S(2)}) collective-permute-start(f32[16,128,128]{2,1,0:T(8,128)S(1)} %add.34), channel_id=1, source_target_pairs={{0,4},{1,5},{2,6},{3,7},{4,8},{5,9},{6,10},{7,11},{8,12},{9,13},{1... | collective-permute-start | bytes 3145736 | tf_op jit(solution)/shard_map/ppermute | solution.py:12
  86.0 0.2 add.39
  86.1 1.3 collective-permute-start.6
  87.5 0.8 copy-done.8
  88.3 1.7 multiply_convert_fusion.1
  90.0 15.4 %collective-permute-done.2 = f32[16,128,128]{2,1,0:T(8,128)S(1)} collective-permute-done((f32[16,128,128]{2,1,0:T(8,128)S(1)}, f32[16,128,128]{2,1,0:T(8,128)S(1)}, u32[]{:S(2)}, u32[]{:S(2)}) %collective-permute-start.2) | collective-permute-done | bytes 1048608 | tf_op jit(solution)/shard_map/ppermute | solution.py:12
  105.4 1.1 add.35
  106.5 6.4 %collective-permute-start.3 = (f32[16,128,128]{2,1,0:T(8,128)}, f32[16,128,128]{2,1,0:T(8,128)}, u32[]{:S(2)}, u32[]{:S(2)}) collective-permute-start(f32[16,128,128]{2,1,0:T(8,128)} %add.35), channel_id=1, source_target_pairs={{0,8},{1,9},{2,10},{3,11},{4,12},{5,13},{6,14},{7,15},{16,24},{17,... | collective-permute-start | bytes 3145736 | tf_op jit(solution)/shard_map/ppermute | solution.py:12
  113.0 3.3 %fusion.17 = f32[16,384,128]{1,2,0:T(8,128)} fusion(bf16[16,384,384]{2,1,0:T(8,128)(2,1)S(1)} %multiply_convert_fusion.1, bf16[384,2048]{1,0:T(8,128)(2,1)S(1)} %copy-done.1), kind=kOutput, calls=%fused_computation.19 | convolution fusion | flops 603979776 | bytes 9437184 | tf_op jit(solution)/shard_map/hts,shd->thd/dot_general | solution.py:44
  116.3 1.1 add.40
  117.4 1.5 collective-permute-start.7
  118.8 2.9 %fusion.9 = f32[16,384,128]{1,2,0:T(8,128)} fusion(bf16[16,384,384]{2,1,0:T(8,128)(2,1)S(1)} %multiply_convert_fusion.1, bf16[384,2048]{1,0:T(8,128)(2,1)S(1)} %copy-done.6), kind=kOutput, calls=%fused_computation.13 | convolution fusion | flops 603979776 | bytes 9437184 | tf_op jit(solution)/shard_map/hts,thd->shd/dot_general | solution.py:47
  121.8 6.1 %fusion = f32[16,384,128]{1,2,0:T(8,128)} fusion(bf16[384,16,128]{0,2,1:T(8,128)(2,1)S(1)} %bitcast.92, f32[384,384]{1,0:T(8,128)} %copy-done.8, bf16[384,2048]{1,0:T(8,128)(2,1)} %param.4, bf16[384,2048]{1,0:T(8,128)(2,1)} %param.5), kind=kOutput, calls=%fused_computation.2 | convolution fusion | flops 1212678144 | bytes 8454144 | tf_op jit(solution)/shard_map/hts,the->she/dot_general | solution.py:50
  127.9 3.1 %collective-permute-done.3 = f32[16,128,128]{2,1,0:T(8,128)} collective-permute-done((f32[16,128,128]{2,1,0:T(8,128)}, f32[16,128,128]{2,1,0:T(8,128)}, u32[]{:S(2)}, u32[]{:S(2)}) %collective-permute-start.3) | collective-permute-done | bytes 1048608 | tf_op jit(solution)/shard_map/ppermute | solution.py:12
  130.9 4.6 %fusion.6 = bf16[384,16,128]{0,2,1:T(8,128)(2,1)} fusion(f32[16,384,128]{1,2,0:T(8,128)} %fusion.17, bf16[384,16,128]{0,2,1:T(8,128)(2,1)S(1)} %bitcast.93, f32[16,128,128]{2,1,0:T(8,128)} %fusion.15, f32[16,128,128]{2,1,0:T(8,128)} %add.35, f32[16,128,128]{2,1,0:T(8,128)} %collective-permute-done.3), kind=kOutput, calls=%fused_computation.10 | convolution fusion | flops 204472320 | bytes 9437184 | tf_op jit(solution)/shard_map/the,hde->thd/dot_general | solution.py:46
  135.5 2.7 %copy.20 = bf16[384,2048]{1,0:T(8,128)(2,1)} copy(bf16[384,2048]{0,1:T(8,128)(2,1)} %bitcast.94) | data formatting | bytes 3145728
  138.2 25.6 %collective-permute-done.7 = f32[16,128,128]{2,1,0:T(8,128)} collective-permute-done((f32[16,128,128]{2,1,0:T(8,128)}, f32[16,128,128]{2,1,0:T(8,128)}, u32[]{:S(2)}, u32[]{:S(2)}) %collective-permute-start.7) | collective-permute-done | bytes 1048608 | tf_op jit(solution)/shard_map/ppermute | solution.py:12
  163.8 1.7 subtract_convert_fusion
  165.5 2.0 %fusion.5 = bf16[384,16,128]{0,2,1:T(8,128)(2,1)} fusion(f32[16,384,128]{1,2,0:T(8,128)S(1)} %copy-done.3, bf16[16,128,128]{2,1,0:T(8,128)(2,1)S(1)} %subtract_convert_fusion, bf16[384,2048]{1,0:T(8,128)(2,1)S(1)} %copy-done), kind=kOutput, calls=%fused_computation.8 | convolution fusion | flops 203685888 | bytes 6815744 | tf_op jit(solution)/shard_map/she,hde->shd/dot_general | solution.py:49
  167.5 2.7 %copy.21 = bf16[384,2048]{1,0:T(8,128)(2,1)} copy(bf16[384,2048]{0,1:T(8,128)(2,1)} %bitcast.96) | data formatting | bytes 3145728
  170.2 4.0 %fusion.4 = bf16[384,16,128]{0,2,1:T(8,128)(2,1)} fusion(f32[16,384,128]{1,2,0:T(8,128)} %fusion, bf16[16,128,128]{2,1,0:T(8,128)(2,1)} %copy-done.7, bf16[384,2048]{1,0:T(8,128)(2,1)S(1)} %copy-done.2), kind=kOutput, calls=%fused_computation.6 | convolution fusion | flops 203685888 | bytes 6815744 | tf_op jit(solution)/shard_map/shd,hde->she/dot_general | solution.py:52
  174.2 2.6 %copy.22 = bf16[384,2048]{1,0:T(8,128)(2,1)} copy(bf16[384,2048]{0,1:T(8,128)(2,1)} %bitcast.95) | data formatting | bytes 3145728
  (23 shorter events, 0.3 us)
Async XLA Ops:
  0.6 1.4 copy-start
  5.1 8.7 %collective-permute-start = (f32[16,128,128]{2,1,0:T(8,128)}, f32[16,128,128]{2,1,0:T(8,128)}, u32[]{:S(2)}, u32[]{:S(2)}) collective-permute-start(f32[16,128,128]{2,1,0:T(8,128)} %fusion.15), channel_id=1, source_target_pairs={{0,1},{1,2},{2,3},{3,4},{4,5},{5,6},{6,7},{7,8},{8,9},{9,10},{10,1... | collective-permute-start | bytes 3145736 | tf_op jit(solution)/shard_map/ppermute | solution.py:12
  12.5 26.9 %copy-start.4 = (f32[16,128,128]{2,1,0:T(8,128)}, f32[16,128,128]{2,1,0:T(8,128)S(1)}, u32[]{:S(2)}) copy-start(f32[16,128,128]{2,1,0:T(8,128)S(1)} %fusion.7) | copy-start | bytes 3145732
  12.5 26.9 %collective-permute-start.4 = (f32[16,128,128]{2,1,0:T(8,128)S(1)}, f32[16,128,128]{2,1,0:T(8,128)S(1)}, u32[]{:S(2)}, u32[]{:S(2)}) collective-permute-start(f32[16,128,128]{2,1,0:T(8,128)S(1)} %fusion.7), channel_id=1, source_target_pairs={{1,0},{2,1},{3,2},{4,3},{5,4},{6,5},{7,6},{8,7},{9,8},{10,9},{11,1... | collective-permute-start | bytes 3145736 | tf_op jit(solution)/shard_map/ppermute | solution.py:12
  15.5 66.2 %collective-permute-start.1 = (f32[16,128,128]{2,1,0:T(8,128)S(1)}, f32[16,128,128]{2,1,0:T(8,128)S(1)}, u32[]{:S(2)}, u32[]{:S(2)}) collective-permute-start(f32[16,128,128]{2,1,0:T(8,128)S(1)} %add.33), channel_id=1, source_target_pairs={{0,2},{1,3},{2,4},{3,5},{4,6},{5,7},{6,8},{7,9},{8,10},{9,11},{10,... | collective-permute-start | bytes 3145736 | tf_op jit(solution)/shard_map/ppermute | solution.py:12
  39.5 46.4 %collective-permute-start.5 = (f32[16,128,128]{2,1,0:T(8,128)S(1)}, f32[16,128,128]{2,1,0:T(8,128)S(1)}, u32[]{:S(2)}, u32[]{:S(2)}) collective-permute-start(f32[16,128,128]{2,1,0:T(8,128)S(1)} %add.38), channel_id=1, source_target_pairs={{2,0},{3,1},{4,2},{5,3},{6,4},{7,5},{8,6},{9,7},{10,8},{11,9},{12,... | collective-permute-start | bytes 3145736 | tf_op jit(solution)/shard_map/ppermute | solution.py:12
  81.8 23.7 %collective-permute-start.2 = (f32[16,128,128]{2,1,0:T(8,128)S(1)}, f32[16,128,128]{2,1,0:T(8,128)S(1)}, u32[]{:S(2)}, u32[]{:S(2)}) collective-permute-start(f32[16,128,128]{2,1,0:T(8,128)S(1)} %add.34), channel_id=1, source_target_pairs={{0,4},{1,5},{2,6},{3,7},{4,8},{5,9},{6,10},{7,11},{8,12},{9,13},{1... | collective-permute-start | bytes 3145736 | tf_op jit(solution)/shard_map/ppermute | solution.py:12
  86.1 30.1 %collective-permute-start.6 = (f32[16,128,128]{2,1,0:T(8,128)S(1)}, f32[16,128,128]{2,1,0:T(8,128)S(1)}, u32[]{:S(2)}, u32[]{:S(2)}) collective-permute-start(f32[16,128,128]{2,1,0:T(8,128)S(1)} %add.39), channel_id=1, source_target_pairs={{4,0},{5,1},{6,2},{7,3},{8,4},{9,5},{10,6},{11,7},{12,8},{13,9},{1... | collective-permute-start | bytes 3145736 | tf_op jit(solution)/shard_map/ppermute | solution.py:12
  87.5 0.8 copy-start.8
  90.0 23.0 %copy-start.1 = (bf16[384,2048]{1,0:T(8,128)(2,1)S(1)}, bf16[384,2048]{1,0:T(8,128)(2,1)}, u32[]{:S(2)}) copy-start(bf16[384,2048]{1,0:T(8,128)(2,1)} %param.5) | copy-start | bytes 4718596
  106.5 24.4 %collective-permute-start.3 = (f32[16,128,128]{2,1,0:T(8,128)}, f32[16,128,128]{2,1,0:T(8,128)}, u32[]{:S(2)}, u32[]{:S(2)}) collective-permute-start(f32[16,128,128]{2,1,0:T(8,128)} %add.35), channel_id=1, source_target_pairs={{0,8},{1,9},{2,10},{3,11},{4,12},{5,13},{6,14},{7,15},{16,24},{17,... | collective-permute-start | bytes 3145736 | tf_op jit(solution)/shard_map/ppermute | solution.py:12
  116.3 2.6 %copy-start.6 = (bf16[384,2048]{1,0:T(8,128)(2,1)S(1)}, bf16[384,2048]{1,0:T(8,128)(2,1)}, u32[]{:S(2)}) copy-start(bf16[384,2048]{1,0:T(8,128)(2,1)} %param.4) | copy-start | bytes 4718596
  117.4 46.4 %collective-permute-start.7 = (f32[16,128,128]{2,1,0:T(8,128)}, f32[16,128,128]{2,1,0:T(8,128)}, u32[]{:S(2)}, u32[]{:S(2)}) collective-permute-start(f32[16,128,128]{2,1,0:T(8,128)} %add.40), channel_id=1, source_target_pairs={{8,0},{9,1},{10,2},{11,3},{12,4},{13,5},{14,6},{15,7},{24,16},{25,... | collective-permute-start | bytes 3145736 | tf_op jit(solution)/shard_map/ppermute | solution.py:12
  135.5 28.3 %copy-start.5 = (f32[16,128,128]{2,1,0:T(8,128)S(1)}, f32[16,128,128]{2,1,0:T(8,128)}, u32[]{:S(2)}) copy-start(f32[16,128,128]{2,1,0:T(8,128)} %copy-done.4) | copy-start | bytes 3145732
  138.2 27.3 %copy-start.3 = (f32[16,384,128]{1,2,0:T(8,128)S(1)}, f32[16,384,128]{1,2,0:T(8,128)}, u32[]{:S(2)}) copy-start(f32[16,384,128]{1,2,0:T(8,128)} %fusion.9) | copy-start | bytes 9437188
  165.5 2.0 %copy-start.7 = (bf16[16,128,128]{2,1,0:T(8,128)(2,1)}, bf16[16,128,128]{2,1,0:T(8,128)(2,1)S(1)}, u32[]{:S(2)}) copy-start(bf16[16,128,128]{2,1,0:T(8,128)(2,1)S(1)} %subtract_convert_fusion) | copy-start | bytes 1572868
  167.5 2.7 %copy-start.2 = (bf16[384,2048]{1,0:T(8,128)(2,1)S(1)}, bf16[384,2048]{1,0:T(8,128)(2,1)}, u32[]{:S(2)}) copy-start(bf16[384,2048]{1,0:T(8,128)(2,1)} %param.5) | copy-start | bytes 4718596
where the time goes:
time: 177 us
  waiting for transfers between devices  84.9 us (48%)
  starting transfers between devices  43.2 us (24%)
  matrix products  29.9 us (17%)
  local copies, waits for them, and re-layouts  12 us (7%)
  other arithmetic  6 us (3%)
    ppermute x8, waiting for transfers between devices, passed_along(): return lax.ppermute(value, axis, pairs)  84.9 us
    ppermute x8, starting transfers between devices, passed_along(): return lax.ppermute(value, axis, pairs)  43.2 us
    unnamed x21, local copies, waits for them, and re-layouts  10.2 us
    dot_general x1, matrix products, local(): jnp.einsum('hts,the->she', weights, gb, preferred_element_type=jnp.float32)  6.11 us
    dot_general x1, matrix products, local(): jnp.einsum('the,hde->thd', gb, kvs, preferred_element_type=jnp.float32)  4.6 us
    dot_general x1, matrix products, local(): jnp.einsum('shd,hde->she', kb, qgs, preferred_element_type=jnp.float32)  4.02 us
  transfers between devices with their start and end apart: 8, of which 4 were waited for; matrix products, arithmetic and copies ran while one was open for 17% of the time, Pallas kernels for 0%

commit v1 on v0

v1 whole, which is shorter than its diff:
```python
import functools

import jax
import jax.numpy as jnp
from jax import lax
from jax.experimental import pallas as pl
from jax.experimental.pallas import tpu as pltpu
from jax.sharding import PartitionSpec as P

HD = 128
CHUNKS = 2
F32 = jnp.float32
BF16 = jnp.bfloat16
VMEM_LIMIT = 40 * 1024 * 1024


def dot(a, b, dims):
    return lax.dot_general(a, b, (dims, ((), ())), preferred_element_type=F32)


def params():
    return pltpu.CompilerParams(vmem_limit_bytes=VMEM_LIMIT)


def state_kernel(heads, a_ref, b_ref, out_ref):
    for h in range(heads):
        cols = slice(h * HD, (h + 1) * HD)
        out_ref[h] = dot(a_ref[:, cols], b_ref[:, cols], ((0,), (0,)))


def local_state(a, b, first, heads):
    rows = a.shape[0]
    per = min(heads, 4)
    block = pl.BlockSpec((rows, per * HD), lambda i: (0, first // per + i))
    return pl.pallas_call(
        functools.partial(state_kernel, per),
        grid=(heads // per,),
        out_shape=jax.ShapeDtypeStruct((heads, HD, HD), F32),
        in_specs=[block, block],
        out_specs=pl.BlockSpec((per, HD, HD), lambda i: (i, 0, 0)),
        compiler_params=params(),
        cost_estimate=pl.CostEstimate(
            flops=2 * heads * rows * HD * HD, bytes_accessed=4 * heads * rows * HD, transcendentals=0
        ),
    )(a, b)


def within_kernel(heads, scale, q_ref, k_ref, v_ref, g_ref, dq_ref, dk_ref, dv_ref):
    rows = q_ref.shape[0]
    at = lax.broadcasted_iota(jnp.int32, (rows, rows), 0)
    upto = lax.broadcasted_iota(jnp.int32, (rows, rows), 1) <= at
    for h in range(heads):
        cols = slice(h * HD, (h + 1) * HD)
        q, k, v, g = q_ref[:, cols], k_ref[:, cols], v_ref[:, cols], g_ref[:, cols]
        weights = jnp.where(upto, dot(q, k, ((1,), (1,))) * scale, 0.0).astype(BF16)
        scores = jnp.where(upto, dot(g, v, ((1,), (1,))) * scale, 0.0).astype(BF16)
        dq_ref[:, cols] = dot(scores, k, ((1,), (0,))).astype(BF16)
        dk_ref[:, cols] = dot(scores, q, ((0,), (0,))).astype(BF16)
        dv_ref[:, cols] = dot(weights, g, ((0,), (0,))).astype(BF16)


def within(q, k, v, g, first, heads, scale):
    rows = q.shape[0]
    per = min(heads, 2)
    block = pl.BlockSpec((rows, per * HD), lambda i: (0, first // per + i))
    out = pl.BlockSpec((rows, per * HD), lambda i: (0, i))
    return pl.pallas_call(
        functools.partial(within_kernel, per, scale),
        grid=(heads // per,),
        out_shape=[jax.ShapeDtypeStruct((rows, heads * HD), BF16)] * 3,
        in_specs=[block] * 4,
        out_specs=[out] * 3,
        compiler_params=params(),
        cost_estimate=pl.CostEstimate(
            flops=10 * heads * rows * rows * HD, bytes_accessed=14 * heads * rows * HD, transcendentals=0
        ),
    )(q, k, v, g)


def final_kernel(heads, scale, k_ref, v_ref, g_ref, kv_ref, qg_ref, pq_ref, pk_ref, pv_ref, dq_ref, dk_ref, dv_ref):
    for h in range(heads):
        cols = slice(h * HD, (h + 1) * HD)
        kv, qg = kv_ref[h].astype(BF16), qg_ref[h].astype(BF16)
        dq_ref[:, cols] = (pq_ref[:, cols].astype(F32) + scale * dot(g_ref[:, cols], kv, ((1,), (1,)))).astype(BF16)
        dk_ref[:, cols] = (pk_ref[:, cols].astype(F32) + scale * dot(v_ref[:, cols], qg, ((1,), (1,)))).astype(BF16)
        dv_ref[:, cols] = (pv_ref[:, cols].astype(F32) + scale * dot(k_ref[:, cols], qg, ((1,), (0,)))).astype(BF16)


def final(k, v, g, kv, qg, partials, scale):
    rows = k.shape[0]
    heads = kv.shape[0]
    per = min(heads, 2)
    block = pl.BlockSpec((rows, per * HD), lambda i: (0, i))
    state = pl.BlockSpec((per, HD, HD), lambda i: (i, 0, 0))
    return pl.pallas_call(
        functools.partial(final_kernel, per, scale),
        grid=(heads // per,),
        out_shape=[jax.ShapeDtypeStruct((rows, heads * HD), BF16)] * 3,
        in_specs=[block] * 3 + [state] * 2 + [block] * 3,
        out_specs=[block] * 3,
        compiler_params=params(),
        cost_estimate=pl.CostEstimate(
            flops=6 * heads * rows * HD * HD, bytes_accessed=18 * heads * rows * HD, transcendentals=0
        ),
    )(k, v, g, kv, qg, *partials)


def local(seq, queries, keys, values, out_grad):
    rows = queries.shape[0]
    heads = queries.shape[1] // HD
    scale = float(1.0 / (HD * rows * seq) ** 0.5)
    at = lax.axis_index("seq")
    later = at % 2 == 1
    second = (at // 2 + at) % 2 == 0
    second = jnp.where(later, (at // 2) % 2 == 1, (at // 2) % 2 == 0)

    core_pairs = [(i, i ^ 1) for i in range(seq)]
    chip_pairs = [(i, i ^ 2) for i in range(seq)]

    def shift(value, by):
        pairs = []
        for i in range(seq):
            j = i + 4 * by if i % 2 else i - 4 * by
            if 0 <= j < seq:
                pairs.append((i, j))
        return lax.ppermute(value, "seq", pairs)

    size = heads // CHUNKS
    half = size // 2
    kvs, qgs = [], []
    for chunk in range(CHUNKS):
        first = chunk * size
        kv = local_state(keys, values, first, size)
        qg = local_state(queries, out_grad, first, size)
        mine = jnp.where(later, kv, qg)
        other = lax.ppermute(jnp.where(later, qg, kv), "seq", core_pairs)
        chip = mine + other
        kept = jnp.where(second, chip[half:], chip[:half])
        partner = lax.ppermute(jnp.where(second, chip[:half], chip[half:]), "seq", chip_pairs)
        plane = kept + partner
        before = shift(plane, 1)
        window = plane + before
        by = 2
        while 4 * by < seq:
            more = shift(window, by)
            before = before + more
            window = window + more
            by *= 2
        swapped = lax.ppermute(jnp.where(second, before, before + kept), "seq", chip_pairs)
        upto = jnp.concatenate(
            [jnp.where(second, swapped, before), jnp.where(second, before + partner, swapped)]
        )
        given = lax.ppermute(upto, "seq", core_pairs)
        here = upto + other
        kvs.append(jnp.where(later, here, given))
        qgs.append(jnp.where(later, given, here))

    partials = within(queries, keys, values, out_grad, 0, heads, scale)
    kv = jnp.concatenate(kvs)
    qg = jnp.concatenate(qgs)
    return tuple(final(keys, values, out_grad, kv, qg, partials, scale))


def solution(mesh):
    spec = P(("groups", "seq"), None)
    return jax.shard_map(
        functools.partial(local, mesh.shape["seq"]),
        mesh=mesh,
        in_specs=(spec,) * 4,
        out_specs=(spec,) * 3,
        check_vma=False,
    )
```

time: 177 us -> 73.7 us (0.42)
  waiting for transfers between devices: 84.9 us -> 28.3 us
  starting transfers between devices: 43.2 us -> 13.3 us
  matrix products: 29.9 us -> 0 us
  Pallas kernels: 0 us -> 19.2 us
  local copies, waits for them, and re-layouts: 12 us -> 4 us
    ppermute x8 -> x12, waiting for transfers between devices: 84.9 us -> 28.3 us  [the longest x4 15 us: shift(): return lax.ppermute(value, 'seq', pairs)]
    ppermute x8 -> x12, starting transfers between devices: 43.2 us -> 13.3 us  [the longest x4 5.17 us: shift(): return lax.ppermute(value, 'seq', pairs)]
    dot_general x9 -> x0, matrix products: 29.9 us -> none  [the longest x1 6.11 us: local(): jnp.einsum('hts,the->she', weights, gb, preferred_element_type=jnp.float32)]
    pallas_call x0 -> x6, Pallas kernels: none -> 19.2 us  [the longest x1 10.3 us: within(): pl.pallas_call(functools.partial(within_kernel, per, scale), grid=(heads...]
    unnamed x21 -> x24, local copies, waits for them, and re-layouts: 10.2 us -> 4 us
    select_n x0 -> x10, other arithmetic: none -> 4.57 us  [the longest x2 2.3 us: local(): qgs.append(jnp.where(later, given, here))]
    reshape x1 -> x0, local copies, waits for them, and re-layouts: 1.87 us -> none  [local(): gb = out_grad.reshape(rows, heads, HD)]
  transfers between devices with their start and end apart: 8 -> 12, of which waited for: 4 -> 7; matrix products, arithmetic and copies ran while one was open for 17% -> 7% of each run, Pallas kernels for 0% -> 16%
where the time goes in v1:
time: 73.7 us; the launch traced here: 73.2 us
  waiting for transfers between devices  28.3 us (38%)
  Pallas kernels  19.2 us (26%)
  starting transfers between devices  13.3 us (18%)
  other arithmetic  7.5 us (10%)
  local copies, waits for them, and re-layouts  4 us (5%)
  between operations  0.92 us (1%)
    ppermute x4, waiting for transfers between devices, shift(): return lax.ppermute(value, 'seq', pairs)  15 us
    pallas_call x1, Pallas kernels, within(): pl.pallas_call(functools.partial(within_kernel, per, scale), grid=(heads...  10.3 us
    ppermute x2, waiting for transfers between devices, local(): lax.ppermute(jnp.where(second, chip[:half], chip[half:]), 'seq', chip_pairs)  9.11 us
    pallas_call x1, Pallas kernels, final(): pl.pallas_call(functools.partial(final_kernel, per, scale), grid=(heads /...  5.72 us
    ppermute x4, starting transfers between devices, shift(): return lax.ppermute(value, 'seq', pairs)  5.17 us
    ppermute x2, waiting for transfers between devices, local(): lax.ppermute(jnp.where(second, before, before + kept), 'seq', chip_pairs)  4.24 us
    unnamed x24, local copies, waits for them, and re-layouts  4 us
    ppermute x2, starting transfers between devices, local(): lax.ppermute(jnp.where(second, before, before + kept), 'seq', chip_pairs)  3.98 us
  transfers between devices with their start and end apart: 12, of which 7 were waited for; matrix products, arithmetic and copies ran while one was open for 7% of the time, Pallas kernels for 16%

profile of v1, /device:TPU:0, one launch (start us, length us, event | category | flops | bytes accessed | tf_op | source)
XLA Modules:
  0.0 73.2 jit_solution(12949654673535413918)
XLA Ops:
  0.7 1.4 %copy-done.2 = bf16[384,2048]{1,0:T(8,128)(2,1)S(1)} copy-done((bf16[384,2048]{1,0:T(8,128)(2,1)S(1)}, bf16[384,2048]{1,0:T(8,128)(2,1)}, u32[]{:S(2)}) %copy-start.2) | copy-done | bytes 1572888
  2.1 1.4 %copy-done.4 = bf16[384,2048]{1,0:T(8,128)(2,1)S(1)} copy-done((bf16[384,2048]{1,0:T(8,128)(2,1)S(1)}, bf16[384,2048]{1,0:T(8,128)(2,1)}, u32[]{:S(2)}) %copy-start.4) | copy-done | bytes 1572888
  3.5 0.8 %shard_map.70 = f32[8,128,128]{2,1,0:T(8,128)S(1)} custom-call(bf16[384,2048]{1,0:T(8,128)(2,1)S(1)} %copy-done.4, bf16[384,2048]{1,0:T(8,128)(2,1)S(1)} %copy-done.2), custom_call_target="tpu_custom_call" | custom-call | flops 100663296 | bytes 1572864 | tf_op jit(solution)/shard_map/pallas_call | solution.py:35
  4.3 0.6 copy-done
  4.9 0.5 copy-done.1
  5.3 0.8 %shard_map.69 = f32[8,128,128]{2,1,0:T(8,128)S(1)} custom-call(bf16[384,2048]{1,0:T(8,128)(2,1)S(1)} %copy-done, bf16[384,2048]{1,0:T(8,128)(2,1)S(1)} %copy-done.1), custom_call_target="tpu_custom_call" | custom-call | flops 100663296 | bytes 1572864 | tf_op jit(solution)/shard_map/pallas_call | solution.py:35
  6.2 0.9 %broadcast_select_fusion.3 = f32[8,128,128]{2,1,0:T(8,128)} fusion(f32[8,128,128]{2,1,0:T(8,128)S(1)} %shard_map.70, f32[8,128,128]{2,1,0:T(8,128)S(1)} %shard_map.69, pred[]{:T(512)S(6)} %eq.13), kind=kLoop, calls=%fused_computation.13 | loop fusion | flops 131072 | bytes 1572865 | tf_op jit(solution)/shard_map/jit(_where)/select_n | solution.py:136
  7.1 0.5 collective-permute-start.6
  7.6 0.8 %shard_map.68 = f32[8,128,128]{2,1,0:T(8,128)S(1)} custom-call(bf16[384,2048]{1,0:T(8,128)(2,1)S(1)} %copy-done.4, bf16[384,2048]{1,0:T(8,128)(2,1)S(1)} %copy-done.2), custom_call_target="tpu_custom_call" | custom-call | flops 100663296 | bytes 1572864 | tf_op jit(solution)/shard_map/pallas_call | solution.py:35
  8.4 0.8 %shard_map.67 = f32[8,128,128]{2,1,0:T(8,128)S(1)} custom-call(bf16[384,2048]{1,0:T(8,128)(2,1)S(1)} %copy-done, bf16[384,2048]{1,0:T(8,128)(2,1)S(1)} %copy-done.1), custom_call_target="tpu_custom_call" | custom-call | flops 100663296 | bytes 1572864 | tf_op jit(solution)/shard_map/pallas_call | solution.py:35
  9.2 1.0 %broadcast_select_fusion.5 = f32[8,128,128]{2,1,0:T(8,128)} fusion(f32[8,128,128]{2,1,0:T(8,128)S(1)} %shard_map.68, f32[8,128,128]{2,1,0:T(8,128)S(1)} %shard_map.67, pred[]{:T(512)S(6)} %eq.13), kind=kLoop, calls=%fused_computation.15 | loop fusion | flops 131072 | bytes 1572865 | tf_op jit(solution)/shard_map/jit(_where)/select_n | solution.py:136
  10.3 1.4 %select_add_fusion = f32[8,128,128]{2,1,0:T(8,128)S(1)} fusion(f32[8,128,128]{2,1,0:T(8,128)} %collective-permute-done.6, f32[8,128,128]{2,1,0:T(8,128)} %copy-done.11, f32[8,128,128]{2,1,0:T(8,128)} %copy-done.10, pred[]{:T(512)S(6)} %eq.13), kind=kLoop, calls=%fused_computation.4 | loop fusion | flops 262144 | bytes 2097153 | tf_op jit(solution)/shard_map/add | solution.py:137
  11.7 3.0 %collective-permute-start.7 = (f32[4,128,128]{2,1,0:T(8,128)S(1)}, f32[4,128,128]{2,1,0:T(8,128)S(1)}, u32[]{:S(2)}, u32[]{:S(2)}) collective-permute-start(f32[4,128,128]{2,1,0:T(8,128)S(1)} %slice_select_fusion), channel_id=1, source_target_pairs={{0,2},{1,3},{2,0},{3,1},{4,6},{5,7},{6,4},{7,5},{8,10},{9,11},{10,... | collective-permute-start | bytes 786440 | tf_op jit(solution)/shard_map/ppermute | solution.py:139
  14.7 1.1 %select_add_fusion.1 = f32[8,128,128]{2,1,0:T(8,128)S(1)} fusion(f32[8,128,128]{2,1,0:T(8,128)} %collective-permute-done, f32[8,128,128]{2,1,0:T(8,128)S(1)} %copy-done.9, f32[8,128,128]{2,1,0:T(8,128)S(1)} %copy-done.7, pred[]{:T(512)S(6)} %eq.13), kind=kLoop, calls=%fused_computation.5 | loop fusion | flops 262144 | bytes 2097153 | tf_op jit(solution)/shard_map/add | solution.py:137
  15.9 0.5 collective-permute-start.1
  16.3 5.5 %collective-permute-done.7 = f32[4,128,128]{2,1,0:T(8,128)S(1)} collective-permute-done((f32[4,128,128]{2,1,0:T(8,128)S(1)}, f32[4,128,128]{2,1,0:T(8,128)S(1)}, u32[]{:S(2)}, u32[]{:S(2)}) %collective-permute-start.7) | collective-permute-done | bytes 262176 | tf_op jit(solution)/shard_map/ppermute | solution.py:139
  21.8 1.3 %collective-permute-start.8 = (f32[4,128,128]{2,1,0:T(8,128)S(1)}, f32[4,128,128]{2,1,0:T(8,128)S(1)}, u32[]{:S(2)}, u32[]{:S(2)}) collective-permute-start(f32[4,128,128]{2,1,0:T(8,128)S(1)} %fusion.1), channel_id=1, source_target_pairs={{1,5},{3,7},{4,0},{5,9},{6,2},{7,11},{8,4},{9,13},{10,6},{11,15},{... | collective-permute-start | bytes 786440 | tf_op jit(solution)/shard_map/ppermute | solution.py:126
  23.1 3.6 %collective-permute-done.1 = f32[4,128,128]{2,1,0:T(8,128)S(1)} collective-permute-done((f32[4,128,128]{2,1,0:T(8,128)S(1)}, f32[4,128,128]{2,1,0:T(8,128)S(1)}, u32[]{:S(2)}, u32[]{:S(2)}) %collective-permute-start.1) | collective-permute-done | bytes 262176 | tf_op jit(solution)/shard_map/ppermute | solution.py:139
  26.8 1.3 %collective-permute-start.2 = (f32[4,128,128]{2,1,0:T(8,128)S(1)}, f32[4,128,128]{2,1,0:T(8,128)S(1)}, u32[]{:S(2)}, u32[]{:S(2)}) collective-permute-start(f32[4,128,128]{2,1,0:T(8,128)S(1)} %fusion), channel_id=1, source_target_pairs={{1,5},{3,7},{4,0},{5,9},{6,2},{7,11},{8,4},{9,13},{10,6},{11,15},{... | collective-permute-start | bytes 786440 | tf_op jit(solution)/shard_map/ppermute | solution.py:126
  28.1 2.1 %collective-permute-done.8 = f32[4,128,128]{2,1,0:T(8,128)S(1)} collective-permute-done((f32[4,128,128]{2,1,0:T(8,128)S(1)}, f32[4,128,128]{2,1,0:T(8,128)S(1)}, u32[]{:S(2)}, u32[]{:S(2)}) %collective-permute-start.8) | collective-permute-done | bytes 262176 | tf_op jit(solution)/shard_map/ppermute | solution.py:126
  30.3 1.3 %collective-permute-start.9 = (f32[4,128,128]{2,1,0:T(8,128)S(1)}, f32[4,128,128]{2,1,0:T(8,128)S(1)}, u32[]{:S(2)}, u32[]{:S(2)}) collective-permute-start(f32[4,128,128]{2,1,0:T(8,128)S(1)} %add.62), channel_id=1, source_target_pairs={{1,9},{3,11},{5,13},{7,15},{8,0},{10,2},{12,4},{14,6},{17,25},{19,... | collective-permute-start | bytes 786440 | tf_op jit(solution)/shard_map/ppermute | solution.py:126
  31.6 3.5 %collective-permute-done.2 = f32[4,128,128]{2,1,0:T(8,128)S(1)} collective-permute-done((f32[4,128,128]{2,1,0:T(8,128)S(1)}, f32[4,128,128]{2,1,0:T(8,128)S(1)}, u32[]{:S(2)}, u32[]{:S(2)}) %collective-permute-start.2) | collective-permute-done | bytes 262176 | tf_op jit(solution)/shard_map/ppermute | solution.py:126
  35.1 1.3 %collective-permute-start.3 = (f32[4,128,128]{2,1,0:T(8,128)S(1)}, f32[4,128,128]{2,1,0:T(8,128)S(1)}, u32[]{:S(2)}, u32[]{:S(2)}) collective-permute-start(f32[4,128,128]{2,1,0:T(8,128)S(1)} %add.55), channel_id=1, source_target_pairs={{1,9},{3,11},{5,13},{7,15},{8,0},{10,2},{12,4},{14,6},{17,25},{19,... | collective-permute-start | bytes 786440 | tf_op jit(solution)/shard_map/ppermute | solution.py:126
  36.4 5.8 %collective-permute-done.9 = f32[4,128,128]{2,1,0:T(8,128)S(1)} collective-permute-done((f32[4,128,128]{2,1,0:T(8,128)S(1)}, f32[4,128,128]{2,1,0:T(8,128)S(1)}, u32[]{:S(2)}, u32[]{:S(2)}) %collective-permute-start.9) | collective-permute-done | bytes 262176 | tf_op jit(solution)/shard_map/ppermute | solution.py:126
  42.3 2.0 %collective-permute-start.10 = (f32[4,128,128]{2,1,0:T(8,128)S(1)}, f32[4,128,128]{2,1,0:T(8,128)S(1)}, u32[]{:S(2)}, u32[]{:S(2)}) collective-permute-start(f32[4,128,128]{2,1,0:T(8,128)S(1)} %get-tuple-element.11), channel_id=1, source_target_pairs={{0,2},{1,3},{2,0},{3,1},{4,6},{5,7},{6,4},{7,5},{8,10},{9,11},{10,... | collective-permute-start | bytes 786440 | tf_op jit(solution)/shard_map/ppermute | solution.py:149
  44.3 3.5 %collective-permute-done.3 = f32[4,128,128]{2,1,0:T(8,128)S(1)} collective-permute-done((f32[4,128,128]{2,1,0:T(8,128)S(1)}, f32[4,128,128]{2,1,0:T(8,128)S(1)}, u32[]{:S(2)}, u32[]{:S(2)}) %collective-permute-start.3) | collective-permute-done | bytes 262176 | tf_op jit(solution)/shard_map/ppermute | solution.py:126
  48.0 2.0 %collective-permute-start.4 = (f32[4,128,128]{2,1,0:T(8,128)S(1)}, f32[4,128,128]{2,1,0:T(8,128)S(1)}, u32[]{:S(2)}, u32[]{:S(2)}) collective-permute-start(f32[4,128,128]{2,1,0:T(8,128)S(1)} %get-tuple-element.9), channel_id=1, source_target_pairs={{0,2},{1,3},{2,0},{3,1},{4,6},{5,7},{6,4},{7,5},{8,10},{9,11},{10,... | collective-permute-start | bytes 786440 | tf_op jit(solution)/shard_map/ppermute | solution.py:149
  50.2 4.2 %collective-permute-done.4 = f32[4,128,128]{2,1,0:T(8,128)S(1)} collective-permute-done((f32[4,128,128]{2,1,0:T(8,128)S(1)}, f32[4,128,128]{2,1,0:T(8,128)S(1)}, u32[]{:S(2)}, u32[]{:S(2)}) %collective-permute-start.4) | collective-permute-done | bytes 262176 | tf_op jit(solution)/shard_map/ppermute | solution.py:149
  54.6 10.3 %shard_map.71 = (bf16[384,2048]{1,0:T(8,128)(2,1)S(1)}, bf16[384,2048]{1,0:T(8,128)(2,1)S(1)}, bf16[384,2048]{1,0:T(8,128)(2,1)S(1)}) custom-call(bf16[384,2048]{1,0:T(8,128)(2,1)S(1)} %copy-done.5, bf16[384,2048]{1,0:T(8,128)(2,1)S(1)} %copy-done, bf16[384,2048]{1,0:T(8,128)(2,1)S(1)} %copy-done.1, bf16[384,2048]{1,0:T(8,128)(2,1)S(1)} %copy-done.3), custom_call_target="tpu_custom_call" | custom-call | flops 3019898880 | bytes 11010048 | tf_op jit(solution)/shard_map/pallas_call | solution.py:67
  64.9 1.2 %broadcast_select_fusion = (f32[8,128,128]{2,1,0:T(8,128)S(1)}, f32[8,128,128]{2,1,0:T(8,128)S(1)}) fusion(f32[8,128,128]{2,1,0:T(8,128)S(1)} %collective-permute-done.11, pred[]{:T(512)S(6)} %eq.13, f32[8,128,128]{2,1,0:T(8,128)} %collective-permute-done.6, f32[4,128,128]{2,1,0:T(8,128)S(1)} %get-tuple-element.20, f32[4,128,128]{2,1,0:T(8,128)S(1)} %get-tuple-element.19), kind=kLoop, calls=%fused_computation.10 | loop fusion | flops 524288 | bytes 2621441 | tf_op jit(solution)/shard_map/jit(_where)/select_n | solution.py:156
  66.1 1.1 %broadcast_select_fusion.1 = (f32[8,128,128]{2,1,0:T(8,128)S(1)}, f32[8,128,128]{2,1,0:T(8,128)S(1)}) fusion(f32[8,128,128]{2,1,0:T(8,128)S(1)} %collective-permute-done.5, pred[]{:T(512)S(6)} %eq.13, f32[8,128,128]{2,1,0:T(8,128)} %collective-permute-done, f32[4,128,128]{2,1,0:T(8,128)S(1)} %get-tuple-element.18, f32[4,128,128]{2,1,0:T(8,128)S(1)} %get-tuple-element.17), kind=kLoop, calls=%fused_computation.11 | loop fusion | flops 524288 | bytes 2621441 | tf_op jit(solution)/shard_map/jit(_where)/select_n | solution.py:156
  67.5 5.7 %shard_map.72 = (bf16[384,2048]{1,0:T(8,128)(2,1)}, bf16[384,2048]{1,0:T(8,128)(2,1)}, bf16[384,2048]{1,0:T(8,128)(2,1)}) custom-call(bf16[384,2048]{1,0:T(8,128)(2,1)S(1)} %copy-done, bf16[384,2048]{1,0:T(8,128)(2,1)S(1)} %copy-done.1, bf16[384,2048]{1,0:T(8,128)(2,1)S(1)} %copy-done.3, f32[16,128,128]{2,1,0:T(8,128)S(1)} %get-tuple-element.21.kv_ref, ...), custom_call_target="tpu_custom_call" | custom-call | flops 603979776 | bytes 14155776 | tf_op jit(solution)/shard_map/pallas_call | solution.py:95
  (41 shorter events, 1.1 us)
Async XLA Ops:
  0.6 1.4 %copy-start.2 = (bf16[384,2048]{1,0:T(8,128)(2,1)S(1)}, bf16[384,2048]{1,0:T(8,128)(2,1)}, u32[]{:S(2)}) copy-start(bf16[384,2048]{1,0:T(8,128)(2,1)} %g_ref.3) | copy-start | bytes 4718596
  2.1 1.4 %copy-start.4 = (bf16[384,2048]{1,0:T(8,128)(2,1)S(1)}, bf16[384,2048]{1,0:T(8,128)(2,1)}, u32[]{:S(2)}) copy-start(bf16[384,2048]{1,0:T(8,128)(2,1)} %q_ref.1) | copy-start | bytes 4718596
  3.5 1.4 %copy-start = (bf16[384,2048]{1,0:T(8,128)(2,1)S(1)}, bf16[384,2048]{1,0:T(8,128)(2,1)}, u32[]{:S(2)}) copy-start(bf16[384,2048]{1,0:T(8,128)(2,1)} %k_ref.3) | copy-start | bytes 4718596
  3.5 1.9 %copy-start.1 = (bf16[384,2048]{1,0:T(8,128)(2,1)S(1)}, bf16[384,2048]{1,0:T(8,128)(2,1)}, u32[]{:S(2)}) copy-start(bf16[384,2048]{1,0:T(8,128)(2,1)} %v_ref.3) | copy-start | bytes 4718596
  5.3 0.8 %copy-start.10 = (f32[8,128,128]{2,1,0:T(8,128)}, f32[8,128,128]{2,1,0:T(8,128)S(1)}, u32[]{:S(2)}) copy-start(f32[8,128,128]{2,1,0:T(8,128)S(1)} %shard_map.70) | copy-start | bytes 1572868
  6.1 2.2 %copy-start.11 = (f32[8,128,128]{2,1,0:T(8,128)}, f32[8,128,128]{2,1,0:T(8,128)S(1)}, u32[]{:S(2)}) copy-start(f32[8,128,128]{2,1,0:T(8,128)S(1)} %shard_map.69) | copy-start | bytes 1572868
  7.1 3.2 %collective-permute-start.6 = (f32[8,128,128]{2,1,0:T(8,128)}, f32[8,128,128]{2,1,0:T(8,128)}, u32[]{:S(2)}, u32[]{:S(2)}) collective-permute-start(f32[8,128,128]{2,1,0:T(8,128)} %broadcast_select_fusion.3), channel_id=1, source_target_pairs={{0,1},{1,0},{2,3},{3,2},{4,5},{5,4},{6,7},{7,6},{8,9},{9,8},{10,11... | collective-permute-start | bytes 1572872 | tf_op jit(solution)/shard_map/ppermute | solution.py:136
  8.3 0.8 %copy-start.6 = (f32[8,128,128]{2,1,0:T(8,128)}, f32[8,128,128]{2,1,0:T(8,128)S(1)}, u32[]{:S(2)}) copy-start(f32[8,128,128]{2,1,0:T(8,128)S(1)} %shard_map.68) | copy-start | bytes 1572868
  9.2 1.1 %copy-start.8 = (f32[8,128,128]{2,1,0:T(8,128)}, f32[8,128,128]{2,1,0:T(8,128)S(1)}, u32[]{:S(2)}) copy-start(f32[8,128,128]{2,1,0:T(8,128)S(1)} %shard_map.67) | copy-start | bytes 1572868
  10.2 4.5 %collective-permute-start = (f32[8,128,128]{2,1,0:T(8,128)}, f32[8,128,128]{2,1,0:T(8,128)}, u32[]{:S(2)}, u32[]{:S(2)}) collective-permute-start(f32[8,128,128]{2,1,0:T(8,128)} %broadcast_select_fusion.5), channel_id=1, source_target_pairs={{0,1},{1,0},{2,3},{3,2},{4,5},{5,4},{6,7},{7,6},{8,9},{9,8},{10,11... | collective-permute-start | bytes 1572872 | tf_op jit(solution)/shard_map/ppermute | solution.py:136
  10.3 4.4 %copy-start.7 = (f32[8,128,128]{2,1,0:T(8,128)S(1)}, f32[8,128,128]{2,1,0:T(8,128)}, u32[]{:S(2)}) copy-start(f32[8,128,128]{2,1,0:T(8,128)} %copy-done.6) | copy-start | bytes 1572868
  10.3 4.4 %copy-start.9 = (f32[8,128,128]{2,1,0:T(8,128)S(1)}, f32[8,128,128]{2,1,0:T(8,128)}, u32[]{:S(2)}) copy-start(f32[8,128,128]{2,1,0:T(8,128)} %copy-done.8) | copy-start | bytes 1572868
  11.7 10.1 %collective-permute-start.7 = (f32[4,128,128]{2,1,0:T(8,128)S(1)}, f32[4,128,128]{2,1,0:T(8,128)S(1)}, u32[]{:S(2)}, u32[]{:S(2)}) collective-permute-start(f32[4,128,128]{2,1,0:T(8,128)S(1)} %slice_select_fusion), channel_id=1, source_target_pairs={{0,2},{1,3},{2,0},{3,1},{4,6},{5,7},{6,4},{7,5},{8,10},{9,11},{10,... | collective-permute-start | bytes 786440 | tf_op jit(solution)/shard_map/ppermute | solution.py:139
  15.9 10.9 %collective-permute-start.1 = (f32[4,128,128]{2,1,0:T(8,128)S(1)}, f32[4,128,128]{2,1,0:T(8,128)S(1)}, u32[]{:S(2)}, u32[]{:S(2)}) collective-permute-start(f32[4,128,128]{2,1,0:T(8,128)S(1)} %slice_select_fusion.2), channel_id=1, source_target_pairs={{0,2},{1,3},{2,0},{3,1},{4,6},{5,7},{6,4},{7,5},{8,10},{9,11},{10,... | collective-permute-start | bytes 786440 | tf_op jit(solution)/shard_map/ppermute | solution.py:139
  21.8 8.4 %collective-permute-start.8 = (f32[4,128,128]{2,1,0:T(8,128)S(1)}, f32[4,128,128]{2,1,0:T(8,128)S(1)}, u32[]{:S(2)}, u32[]{:S(2)}) collective-permute-start(f32[4,128,128]{2,1,0:T(8,128)S(1)} %fusion.1), channel_id=1, source_target_pairs={{1,5},{3,7},{4,0},{5,9},{6,2},{7,11},{8,4},{9,13},{10,6},{11,15},{... | collective-permute-start | bytes 786440 | tf_op jit(solution)/shard_map/ppermute | solution.py:126
  26.8 8.3 %collective-permute-start.2 = (f32[4,128,128]{2,1,0:T(8,128)S(1)}, f32[4,128,128]{2,1,0:T(8,128)S(1)}, u32[]{:S(2)}, u32[]{:S(2)}) collective-permute-start(f32[4,128,128]{2,1,0:T(8,128)S(1)} %fusion), channel_id=1, source_target_pairs={{1,5},{3,7},{4,0},{5,9},{6,2},{7,11},{8,4},{9,13},{10,6},{11,15},{... | collective-permute-start | bytes 786440 | tf_op jit(solution)/shard_map/ppermute | solution.py:126
  30.3 12.0 %collective-permute-start.9 = (f32[4,128,128]{2,1,0:T(8,128)S(1)}, f32[4,128,128]{2,1,0:T(8,128)S(1)}, u32[]{:S(2)}, u32[]{:S(2)}) collective-permute-start(f32[4,128,128]{2,1,0:T(8,128)S(1)} %add.62), channel_id=1, source_target_pairs={{1,9},{3,11},{5,13},{7,15},{8,0},{10,2},{12,4},{14,6},{17,25},{19,... | collective-permute-start | bytes 786440 | tf_op jit(solution)/shard_map/ppermute | solution.py:126
  35.1 12.7 %collective-permute-start.3 = (f32[4,128,128]{2,1,0:T(8,128)S(1)}, f32[4,128,128]{2,1,0:T(8,128)S(1)}, u32[]{:S(2)}, u32[]{:S(2)}) collective-permute-start(f32[4,128,128]{2,1,0:T(8,128)S(1)} %add.55), channel_id=1, source_target_pairs={{1,9},{3,11},{5,13},{7,15},{8,0},{10,2},{12,4},{14,6},{17,25},{19,... | collective-permute-start | bytes 786440 | tf_op jit(solution)/shard_map/ppermute | solution.py:126
  42.3 7.6 %collective-permute-start.10 = (f32[4,128,128]{2,1,0:T(8,128)S(1)}, f32[4,128,128]{2,1,0:T(8,128)S(1)}, u32[]{:S(2)}, u32[]{:S(2)}) collective-permute-start(f32[4,128,128]{2,1,0:T(8,128)S(1)} %get-tuple-element.11), channel_id=1, source_target_pairs={{0,2},{1,3},{2,0},{3,1},{4,6},{5,7},{6,4},{7,5},{8,10},{9,11},{10,... | collective-permute-start | bytes 786440 | tf_op jit(solution)/shard_map/ppermute | solution.py:149
  48.0 6.4 %collective-permute-start.4 = (f32[4,128,128]{2,1,0:T(8,128)S(1)}, f32[4,128,128]{2,1,0:T(8,128)S(1)}, u32[]{:S(2)}, u32[]{:S(2)}) collective-permute-start(f32[4,128,128]{2,1,0:T(8,128)S(1)} %get-tuple-element.9), channel_id=1, source_target_pairs={{0,2},{1,3},{2,0},{3,1},{4,6},{5,7},{6,4},{7,5},{8,10},{9,11},{10,... | collective-permute-start | bytes 786440 | tf_op jit(solution)/shard_map/ppermute | solution.py:149
  50.0 4.6 %copy-start.3 = (bf16[384,2048]{1,0:T(8,128)(2,1)S(1)}, bf16[384,2048]{1,0:T(8,128)(2,1)}, u32[]{:S(2)}) copy-start(bf16[384,2048]{1,0:T(8,128)(2,1)} %g_ref.3) | copy-start | bytes 4718596
  50.0 4.6 %copy-start.5 = (bf16[384,2048]{1,0:T(8,128)(2,1)S(1)}, bf16[384,2048]{1,0:T(8,128)(2,1)}, u32[]{:S(2)}) copy-start(bf16[384,2048]{1,0:T(8,128)(2,1)} %q_ref.1) | copy-start | bytes 4718596
  50.1 14.9 %collective-permute-start.11 = (f32[8,128,128]{2,1,0:T(8,128)S(1)}, f32[8,128,128]{2,1,0:T(8,128)S(1)}, u32[]{:S(2)}, u32[]{:S(2)}) collective-permute-start(f32[8,128,128]{2,1,0:T(8,128)S(1)} %pad_maximum_fusion.3), channel_id=1, source_target_pairs={{0,1},{1,0},{2,3},{3,2},{4,5},{5,4},{6,7},{7,6},{8,9},{9,8},{10,11... | collective-permute-start | bytes 1572872 | tf_op jit(solution)/shard_map/ppermute | solution.py:153
  54.5 11.6 %collective-permute-start.5 = (f32[8,128,128]{2,1,0:T(8,128)S(1)}, f32[8,128,128]{2,1,0:T(8,128)S(1)}, u32[]{:S(2)}, u32[]{:S(2)}) collective-permute-start(f32[8,128,128]{2,1,0:T(8,128)S(1)} %pad_maximum_fusion.2), channel_id=1, source_target_pairs={{0,1},{1,0},{2,3},{3,2},{4,5},{5,4},{6,7},{7,6},{8,9},{9,8},{10,11... | collective-permute-start | bytes 1572872 | tf_op jit(solution)/shard_map/ppermute | solution.py:153

commit v2 on v1

v2 whole, which is shorter than its diff:
```python
import functools

import jax
import jax.numpy as jnp
from jax import lax
from jax.experimental import pallas as pl
from jax.experimental.pallas import tpu as pltpu
from jax.sharding import PartitionSpec as P

HD = 128
CHUNKS = (8, 8)
RADIX = 2
PIECE = 4
PLACES = (
    ((0, 0), ("kept", 1), ("plane", 0)),
    ((0, 1), ("kept", 1), ("plane", 0)),
    ((1, 0), ("kept", 1), ("scan", 0)),
    ((1, 1), ("kept", 1), ("scan", 0)),
)
F32 = jnp.float32
BF16 = jnp.bfloat16
VMEM_LIMIT = 24 * 1024 * 1024
VMEM_MOST = 46 * 1024 * 1024
ANY = pl.BlockSpec(memory_space=pl.ANY)
HBM = pl.BlockSpec(memory_space=pltpu.HBM)
VMEM = pl.BlockSpec(memory_space=pltpu.VMEM)


def dot(a, b, dims):
    return lax.dot_general(a, b, (dims, ((), ())), preferred_element_type=F32)


def cost(flops, size):
    return pl.CostEstimate(flops=flops, bytes_accessed=size, transcendentals=0)


def place():
    at = lax.axis_index("seq")
    core, chip = lax.rem(at, 2), lax.rem(at // 2, 2)
    return core == 1, core == chip


def first_kernel(size, q_ref, k_ref, v_ref, g_ref, other_ref, qv_ref, kv_ref, vv_ref, gv_ref, sem):
    later, second = place()
    width = q_ref.shape[1]
    cut = size * HD
    pieces = [(0, cut // 2), (cut // 2, cut // 2)] + ([(cut, width - cut)] if width > cut else [])

    def copies(j, source, target):
        made = []
        for n, (start, count) in enumerate(pieces):
            cols = pl.ds(start, count)
            made.append(pltpu.make_async_copy(source.at[:, cols], target.at[:, cols], sem.at[j, n]))
        return made

    q, k, v, g = (
        copies(j, source, target)
        for j, (source, target) in enumerate(((q_ref, qv_ref), (k_ref, kv_ref), (v_ref, vv_ref), (g_ref, gv_ref)))
    )

    def run(pair, refs, rest):
        for n in range(2):
            for copy in pair:
                copy[n].start()
        for copy in rest:
            for n in range(2):
                copy[n].start()
        for copy in (*rest, *pair):
            for n in range(2, len(pieces)):
                copy[n].start()
        half = size // 2
        turn = jnp.where(second, 0, half)
        for n in range(2):
            for copy in pair:
                copy[n].wait()
            for h in range(half):
                cols = slice((n * half + h) * HD, (n * half + h + 1) * HD)
                other_ref[lax.rem(n * half + turn, size) + h] = dot(refs[0][:, cols], refs[1][:, cols], ((0,), (0,)))
        for copy in rest:
            for n in range(2):
                copy[n].wait()
        for copy in (*rest, *pair):
            for n in range(2, len(pieces)):
                copy[n].wait()

    @pl.when(later)
    def _():
        run((q, g), (qv_ref, gv_ref), (k, v))

    @pl.when(jnp.logical_not(later))
    def _():
        run((k, v), (kv_ref, vv_ref), (q, g))


def first_state(arrays, size):
    rows, width = arrays[0].shape
    return pl.pallas_call(
        functools.partial(first_kernel, size),
        out_shape=[jax.ShapeDtypeStruct((size, HD, HD), F32)] + [jax.ShapeDtypeStruct((rows, width), BF16)] * 4,
        in_specs=[ANY] * 4,
        out_specs=[VMEM] * 5,
        scratch_shapes=[pltpu.SemaphoreType.DMA((4, 3))],
        compiler_params=pltpu.CompilerParams(vmem_limit_bytes=VMEM_MOST),
        cost_estimate=cost(2 * size * rows * HD * HD, 16 * rows * width),
    )(*arrays)


def other_kernel(size, q_ref, k_ref, v_ref, g_ref, out_ref):
    later, second = place()
    half = size // 2
    turn = jnp.where(second, 0, half)

    def run(a_ref, b_ref):
        for h in range(size):
            cols = slice(h * HD, (h + 1) * HD)
            at = lax.rem(h // half * half + turn, size) + h % half
            out_ref[at] = dot(a_ref[:, cols], b_ref[:, cols], ((0,), (0,)))

    @pl.when(later)
    def _():
        run(q_ref, g_ref)

    @pl.when(jnp.logical_not(later))
    def _():
        run(k_ref, v_ref)


def mine_kernel(size, q_ref, k_ref, v_ref, g_ref, other_ref, kept_ref, sent_ref):
    later, second = place()
    half = size // 2

    def run(pair, swap):
        refs = (sent_ref, kept_ref) if swap else (kept_ref, sent_ref)
        for h in range(size):
            cols = slice(h * HD, (h + 1) * HD)
            at = (h + (half if swap else 0)) % size
            value = dot(pair[0][:, cols], pair[1][:, cols], ((0,), (0,)))
            refs[h // half][h % half] = value + other_ref[at]

    for is_later, pair in ((True, (k_ref, v_ref)), (False, (q_ref, g_ref))):
        for swap in (True, False):
            pl.when(jnp.logical_and(later == is_later, second == swap))(functools.partial(run, pair, swap))


def other_state(arrays, first, size):
    rows = arrays[0].shape[0]
    block = pl.BlockSpec((rows, size * HD), lambda i: (0, first // size))
    return pl.pallas_call(
        functools.partial(other_kernel, size),
        grid=(1,),
        out_shape=jax.ShapeDtypeStruct((size, HD, HD), F32),
        in_specs=[block] * 4,
        out_specs=pl.BlockSpec((size, HD, HD), lambda i: (0, 0, 0)),
        compiler_params=pltpu.CompilerParams(vmem_limit_bytes=VMEM_LIMIT),
        cost_estimate=cost(2 * size * rows * HD * HD, 4 * size * rows * HD),
    )(*arrays)


def chip_state(arrays, other, first, size):
    rows = arrays[0].shape[0]
    half = jax.ShapeDtypeStruct((size // 2, HD, HD), F32)
    block = pl.BlockSpec((rows, size * HD), lambda i: (0, first // size))
    out = pl.BlockSpec((size // 2, HD, HD), lambda i: (0, 0, 0))
    return pl.pallas_call(
        functools.partial(mine_kernel, size),
        grid=(1,),
        out_shape=[half, half],
        in_specs=[block] * 4 + [pl.BlockSpec((size, HD, HD), lambda i: (0, 0, 0))],
        out_specs=[out, out],
        compiler_params=pltpu.CompilerParams(vmem_limit_bytes=VMEM_LIMIT),
        cost_estimate=cost(2 * size * rows * HD * HD, 4 * size * rows * HD),
    )(*arrays, other)


def sums_kernel(count, outs, work, *refs):
    values = work(*[ref[...] for ref in refs[:count]])
    for ref, value in zip(refs[-outs:], values):
        ref[...] = value


def sums(work, outs, values, after=()):
    return pl.pallas_call(
        functools.partial(sums_kernel, len(values), outs, work),
        out_shape=[jax.ShapeDtypeStruct(values[0].shape, F32)] * outs,
        in_specs=[VMEM] * len(values) + [ANY] * len(after),
        out_specs=[VMEM] * outs,
        compiler_params=pltpu.CompilerParams(vmem_limit_bytes=VMEM_LIMIT),
        cost_estimate=cost(values[0].size, 8 * values[0].size),
    )(*values, *after)


def within_kernel(heads, scale, q_ref, k_ref, v_ref, g_ref, *refs):
    dq_ref, dk_ref, dv_ref = refs[-3:]
    rows = q_ref.shape[0]
    at = lax.broadcasted_iota(jnp.int32, (rows, rows), 0)
    upto = lax.broadcasted_iota(jnp.int32, (rows, rows), 1) <= at
    for h in range(heads):
        cols = slice(h * HD, (h + 1) * HD)
        q, k, v, g = q_ref[:, cols], k_ref[:, cols], v_ref[:, cols], g_ref[:, cols]
        weights = jnp.where(upto, dot(q, k, ((1,), (1,))) * scale, 0.0).astype(BF16)
        scores = jnp.where(upto, dot(g, v, ((1,), (1,))) * scale, 0.0).astype(BF16)
        dq_ref[:, cols] = dot(scores, k, ((1,), (0,))).astype(BF16)
        dk_ref[:, cols] = dot(scores, q, ((0,), (0,))).astype(BF16)
        dv_ref[:, cols] = dot(weights, g, ((0,), (0,))).astype(BF16)


def within(arrays, first, size, start, heads, scale, held, after):
    rows = arrays[0].shape[0]
    per = min(heads, 2)
    block = pl.BlockSpec((rows, per * HD), lambda i: (0, (first + start) // per + i))
    out = pl.BlockSpec((rows, per * HD), lambda i: (0, start // per + i))
    return pl.pallas_call(
        functools.partial(within_kernel, per, scale),
        grid=(heads // per,),
        out_shape=[jax.ShapeDtypeStruct((rows, size * HD), BF16)] * 3,
        in_specs=[block] * 4 + [ANY] * len((*held, *after)),
        out_specs=[out] * 3,
        input_output_aliases={4 + j: j for j in range(len(held))},
        compiler_params=pltpu.CompilerParams(vmem_limit_bytes=VMEM_LIMIT),
        cost_estimate=cost(heads * rows * HD, heads * rows * HD),
    )(*arrays, *held, *after)


def final_kernel(per, half, scale, *refs):
    k_ref, v_ref, g_ref, pq_ref, pk_ref, pv_ref = refs[:6]
    low_ref, high_ref, kept_ref, swapped_ref, gkept_ref, gswapped_ref = refs[6:12]
    dq_ref, dk_ref, dv_ref = refs[-3:]
    later, second = place()
    upper = pl.program_id(0) >= half // per
    own = upper == second
    for h in range(per):
        cols = slice(h * HD, (h + 1) * HD)
        here = jnp.where(own, kept_ref[h] + low_ref[h], swapped_ref[h] + high_ref[h])
        given = jnp.where(own, gswapped_ref[h], gkept_ref[h])
        kv = jnp.where(later, here, given).astype(BF16)
        qg = jnp.where(later, given, here).astype(BF16)
        dq_ref[:, cols] = (pq_ref[:, cols].astype(F32) + scale * dot(g_ref[:, cols], kv, ((1,), (1,)))).astype(BF16)
        dk_ref[:, cols] = (pk_ref[:, cols].astype(F32) + scale * dot(v_ref[:, cols], qg, ((1,), (1,)))).astype(BF16)
        dv_ref[:, cols] = (pv_ref[:, cols].astype(F32) + scale * dot(k_ref[:, cols], qg, ((1,), (0,)))).astype(BF16)


def final(k, v, g, partials, other, states, first, size, scale, held):
    rows, width = k.shape
    half = size // 2
    per = min(half, 2)
    steps = half // per
    block = pl.BlockSpec((rows, per * HD), lambda i: (0, first // per + i))
    chunk = pl.BlockSpec((rows, per * HD), lambda i: (0, i))
    low = pl.BlockSpec((per, HD, HD), lambda i: (lax.rem(i, steps), 0, 0))
    high = pl.BlockSpec((per, HD, HD), lambda i: (steps + lax.rem(i, steps), 0, 0))
    return pl.pallas_call(
        functools.partial(final_kernel, per, half, scale),
        grid=(size // per,),
        out_shape=[jax.ShapeDtypeStruct((rows, width), BF16)] * 3,
        in_specs=[block] * 3 + [chunk] * 3 + [low, high] + [low] * 4 + [ANY] * len(held),
        out_specs=[block] * 3,
        input_output_aliases={12 + j: j for j in range(len(held))},
        compiler_params=pltpu.CompilerParams(vmem_limit_bytes=VMEM_LIMIT),
        cost_estimate=cost(6 * size * rows * HD * HD, 18 * size * rows * HD),
    )(k, v, g, *partials, other, other, *states, *held)


def local(seq, queries, keys, values, out_grad):
    rows = queries.shape[0]
    heads = queries.shape[1] // HD
    scale = float(1.0 / (HD * rows * seq) ** 0.5)
    planes = seq // 4
    at = lax.axis_index("seq")
    core_pairs = [(i, i ^ 1) for i in range(seq)]
    chip_pairs = [(i, i ^ 2) for i in range(seq)]

    def shift(value, by):
        pairs = []
        for i in range(seq):
            j = i + 4 * by if i % 2 else i - 4 * by
            pairs.append((i, j if 0 <= j < seq else i ^ 1))
        return lax.ppermute(value, "seq", pairs)

    def plane_at():
        later, _ = place()
        plane = lax.axis_index("seq") // 4
        return jnp.where(later, plane, planes - 1 - plane)

    def masked(values, steps):
        total = jnp.zeros_like(values[0])
        for value, step in zip(values, steps):
            total = total + jnp.where(plane_at() >= step, value, 0.0)
        return total

    def scan(plane, kept, partner, after):
        before, window, by = None, plane, 1
        while True:
            steps = [j * by for j in range(1, RADIX) if j * by < planes]
            arrived = [shift(window, step) for step in steps]
            by *= RADIX
            if by >= planes:
                break

            def more(window, before, *arrived):
                add = masked(arrived, steps)
                return window + add, before + add

            window, before = sums(more, 2, [window, jnp.zeros_like(plane) if before is None else before, *arrived])

        def last(kept, partner, *arrived):
            _, second = place()
            total = masked(arrived[: len(steps)], steps)
            for value in arrived[len(steps) :]:
                total = total + value
            return total + jnp.where(second, 0.0, kept), total + jnp.where(second, partner, 0.0)

        return sums(last, 2, [kept, partner, *arrived, *([] if before is None else [before])], after)

    sizes = [heads * part // sum(CHUNKS) for part in CHUNKS]
    firsts = [sum(sizes[:i]) for i in range(len(sizes))]
    first_other, *arrays = first_state((queries, keys, values, out_grad), sizes[0])
    _, keys, values, out_grad = arrays
    chunks = range(len(sizes))
    made = {}
    pieces = [()] * len(sizes)

    def wait_for(name, chunk):
        found = []
        for (c, p), after, before in PLACES:
            if before == (name, chunk):
                held = within(arrays, firsts[c], sizes[c], p * PIECE, min(PIECE, sizes[c]), scale, pieces[c], [made[after]])
                pieces[c] = held
                found.append(held[0])
        return found

    for c in chunks:
        other = other_state(arrays, firsts[c], sizes[c]) if c else first_other
        made["other", c] = lax.ppermute(other, "seq", core_pairs)
    for c in chunks:
        made["kept", c], sent = chip_state(arrays, made["other", c], firsts[c], sizes[c])
        made["partner", c] = lax.ppermute(sent, "seq", chip_pairs)
    for c in chunks:
        terms = [made["kept", c], made["partner", c]]
        (made["plane", c],) = sums(lambda a, b: (a + b,), 1, terms, wait_for("plane", c))
    done = []
    for c in chunks:
        kept, partner = made["kept", c], made["partner", c]
        back, kept_upto = scan(made["plane", c], kept, partner, wait_for("scan", c))
        swapped = lax.ppermute(back, "seq", chip_pairs)
        done.append((made["other", c], kept_upto, swapped, lax.ppermute(kept_upto, "seq", core_pairs)))

    out = ()
    for chunk, (first, size) in enumerate(zip(firsts, sizes)):
        other, kept_upto, swapped, given_kept = done[chunk]
        if out:
            swapped, out = lax.optimization_barrier((swapped, out))
        given_swapped = lax.ppermute(swapped, "seq", core_pairs)
        states = (kept_upto, swapped, given_kept, given_swapped)
        out = final(keys, values, out_grad, pieces[chunk], other, states, first, size, scale, out)
    return tuple(out)


def solution(mesh):
    spec = P(("groups", "seq"), None)
    return jax.shard_map(
        functools.partial(local, mesh.shape["seq"]),
        mesh=mesh,
        in_specs=(spec,) * 4,
        out_specs=(spec,) * 3,
        check_vma=False,
    )
```

time: 73.7 us -> 56.1 us (0.76)
  other arithmetic: 7.5 us -> 0 us
  starting transfers between devices: 13.3 us -> 8.39 us
  local copies, waits for them, and re-layouts: 4 us -> 0.12 us
  waiting for transfers between devices: 28.3 us -> 24.7 us
  Pallas kernels: 19.2 us -> 22 us
    ppermute x4, starting transfers between devices: 5.17 us -> 0.18 us  [shift(): return lax.ppermute(value, 'seq', pairs)]
    select_n x10 -> x0, other arithmetic: 4.57 us -> none  [the longest x2 2.3 us: local(): qgs.append(jnp.where(later, given, here))]
    unnamed x24 -> x2, local copies, waits for them, and re-layouts: 4 us -> 0.11 us
    ppermute x4, waiting for transfers between devices: 15 us -> 12 us  [shift(): return lax.ppermute(value, 'seq', pairs)]
    pallas_call x5 -> x12, Pallas kernels: 8.84 us -> 11.5 us  [the longest x2 6.31 us: final(): pl.pallas_call(functools.partial(final_kernel, per, half, scale), grid=(s...]
    add x6 -> x0, other arithmetic: 2.65 us -> none  [the longest x2 2.49 us: local(): chip = mine + other]
    ppermute x8 -> x10, waiting for transfers between devices: 13.4 us -> 12.7 us  [the longest x2 7.15 us: local(): swapped = lax.ppermute(back, 'seq', chip_pairs)]
    pallas_call x1 -> x4, Pallas kernels: 10.3 us -> 10.4 us  [within(): pl.pallas_call(functools.partial(within_kernel, per, scale), grid=(heads...]
  transfers between devices with their start and end apart: 12 -> 14, of which waited for: 7 -> 9; matrix products, arithmetic and copies ran while one was open for 7% -> 0% of each run, Pallas kernels for 16% -> 28%
where the time goes in v2:
time: 56.1 us; the launch traced here: 55.9 us
  waiting for transfers between devices  24.7 us (44%)
  Pallas kernels  22 us (39%)
  starting transfers between devices  8.39 us (15%)
  between operations  0.79 us (1%)
    ppermute x4, waiting for transfers between devices, shift(): return lax.ppermute(value, 'seq', pairs)  12 us
    pallas_call x4, Pallas kernels, within(): pl.pallas_call(functools.partial(within_kernel, per, scale), grid=(heads...  10.4 us
    ppermute x2, waiting for transfers between devices, local(): swapped = lax.ppermute(back, 'seq', chip_pairs)  7.15 us
    pallas_call x2, Pallas kernels, final(): pl.pallas_call(functools.partial(final_kernel, per, half, scale), grid=(s...  6.31 us
    ppermute x2, starting transfers between devices, local(): made['partner', c] = lax.ppermute(sent, 'seq', chip_pairs)  4.73 us
    ppermute x2, waiting for transfers between devices, local(): made['partner', c] = lax.ppermute(sent, 'seq', chip_pairs)  3.2 us
    pallas_call x1, Pallas kernels, first_state(): pl.pallas_call(functools.partial(first_kernel, size), out_shape=[jax.Shap...  2.94 us
    ppermute x2, starting transfers between devices, local(): swapped = lax.ppermute(back, 'seq', chip_pairs)  2.16 us
  transfers between devices with their start and end apart: 14, of which 9 were waited for; matrix products, arithmetic and copies ran while one was open for 0% of the time, Pallas kernels for 28%

profile of v2, /device:TPU:0, one launch (start us, length us, event | category | flops | bytes accessed | tf_op | source)
XLA Modules:
  0.0 55.9 jit_solution(3285952174284110798)
XLA Ops:
  0.6 2.9 %shard_map.67 = (f32[8,128,128]{2,1,0:T(8,128)S(1)}, bf16[384,2048]{1,0:T(8,128)(2,1)S(1)}, bf16[384,2048]{1,0:T(8,128)(2,1)S(1)}, bf16[384,2048]{1,0:T(8,128)(2,1)S(1)}, bf16[384,2048]{1,0:T(8,128)(2,1)S(1)}) custom-call(bf16[384,2048]{1,0:T(8,128)(2,1)} %q_ref.1, bf16[384,2048]{1,0:T(8,128)(2,1)} %k_ref.1, bf16[384,2048]{1,0:T(8,128)(2,1)} %v_ref.1, ...), custom_call_target="tpu_custom_call" | custom-call | flops 100663296 | bytes 12582912 | tf_op jit(solution)/shard_map/pallas_call | solution.py:97
  3.6 0.5 collective-permute-start.5
  4.1 0.6 %shard_map.68 = f32[8,128,128]{2,1,0:T(8,128)S(1)} custom-call(bf16[384,2048]{1,0:T(8,128)(2,1)S(1)} %get-tuple-element.42.q_ref, bf16[384,2048]{1,0:T(8,128)(2,1)S(1)} %get-tuple-element.39.k_ref.refs_0_, bf16[384,2048]{1,0:T(8,128)(2,1)S(1)} %get-tuple-element.40.v_ref.refs_1_, bf16[384,2048]{1,0:T(8,128)(2,1)S(1)} %get-tuple-element.41.g_ref.refs_2_), custom_call_target="tpu_custom_call" | custom-call | flops 100663296 | bytes 1572864 | tf_op jit(solution)/shard_map/pallas_call | solution.py:148
  4.7 0.1 collective-permute-start
  4.9 0.8 %collective-permute-done.5.other_ref.refs_6_.refs_7_ = f32[8,128,128]{2,1,0:T(8,128)S(1)} collective-permute-done((f32[8,128,128]{2,1,0:T(8,128)S(1)}, f32[8,128,128]{2,1,0:T(8,128)S(1)}, u32[]{:S(2)}, u32[]{:S(2)}) %collective-permute-start.5) | collective-permute-done | bytes 524320 | tf_op jit(solution)/shard_map/ppermute | solution.py:333
  5.6 0.6 %shard_map.77 = (f32[4,128,128]{2,1,0:T(8,128)S(1)}, f32[4,128,128]{2,1,0:T(8,128)S(1)}) custom-call(bf16[384,2048]{1,0:T(8,128)(2,1)S(1)} %get-tuple-element.42.q_ref, bf16[384,2048]{1,0:T(8,128)(2,1)S(1)} %get-tuple-element.39.k_ref.refs_0_, bf16[384,2048]{1,0:T(8,128)(2,1)S(1)} %get-tuple-element.40.v_ref.refs_1_, ...), custom_call_target="tpu_custom_call" | custom-call | flops 100663296 | bytes 1572864 | tf_op jit(solution)/shard_map/pallas_call | solution.py:164
  6.3 2.9 %collective-permute-start.6 = (f32[4,128,128]{2,1,0:T(8,128)S(1)}, f32[4,128,128]{2,1,0:T(8,128)S(1)}, u32[]{:S(2)}, u32[]{:S(2)}) collective-permute-start(f32[4,128,128]{2,1,0:T(8,128)S(1)} %get-tuple-element.63), channel_id=1, source_target_pairs={{0,2},{1,3},{2,0},{3,1},{4,6},{5,7},{6,4},{7,5},{8,10},{9,11},{10,... | collective-permute-start | bytes 786440 | tf_op jit(solution)/shard_map/ppermute | solution.py:336
  9.2 0.6 %shard_map.69 = (f32[4,128,128]{2,1,0:T(8,128)S(1)}, f32[4,128,128]{2,1,0:T(8,128)S(1)}) custom-call(bf16[384,2048]{1,0:T(8,128)(2,1)S(1)} %get-tuple-element.42.q_ref, bf16[384,2048]{1,0:T(8,128)(2,1)S(1)} %get-tuple-element.39.k_ref.refs_0_, bf16[384,2048]{1,0:T(8,128)(2,1)S(1)} %get-tuple-element.40.v_ref.refs_1_, ...), custom_call_target="tpu_custom_call" | custom-call | flops 100663296 | bytes 1572864 | tf_op jit(solution)/shard_map/pallas_call | solution.py:164
  9.9 2.6 %shard_map.75 = (bf16[384,1024]{1,0:T(8,128)(2,1)S(1)}, bf16[384,1024]{1,0:T(8,128)(2,1)S(1)}, bf16[384,1024]{1,0:T(8,128)(2,1)S(1)}) custom-call(bf16[384,2048]{1,0:T(8,128)(2,1)S(1)} %get-tuple-element.42.q_ref, bf16[384,2048]{1,0:T(8,128)(2,1)S(1)} %get-tuple-element.39.k_ref.refs_0_, bf16[384,2048]{1,0:T(8,128)(2,1)S(1)} %get-tuple-element.40.v_ref.refs_1_, ...), custom_call_target="tpu_custom_call" | custom-call | flops 196608 | bytes 196608 | tf_op jit(solution)/shard_map/pallas_call | solution.py:212
  12.5 2.6 %shard_map.76 = (bf16[384,1024]{1,0:T(8,128)(2,1)S(1)}, bf16[384,1024]{1,0:T(8,128)(2,1)S(1)}, bf16[384,1024]{1,0:T(8,128)(2,1)S(1)}) custom-call(bf16[384,2048]{1,0:T(8,128)(2,1)S(1)} %get-tuple-element.42.q_ref, bf16[384,2048]{1,0:T(8,128)(2,1)S(1)} %get-tuple-element.39.k_ref.refs_0_, ...), custom_call_target="tpu_custom_call", output_to_operand_aliasing={{0}: (4, {}), {1}: (5, {}), {2}: (6, {})} | custom-call | flops 196608 | bytes 196608 | tf_op jit(solution)/shard_map/pallas_call | solution.py:212
  15.1 0.7 %collective-permute-done.6.refs_1_ = f32[4,128,128]{2,1,0:T(8,128)S(1)} collective-permute-done((f32[4,128,128]{2,1,0:T(8,128)S(1)}, f32[4,128,128]{2,1,0:T(8,128)S(1)}, u32[]{:S(2)}, u32[]{:S(2)}) %collective-permute-start.6) | collective-permute-done | bytes 262176 | tf_op jit(solution)/shard_map/ppermute | solution.py:336
  15.9 1.8 %collective-permute-start.1 = (f32[4,128,128]{2,1,0:T(8,128)S(1)}, f32[4,128,128]{2,1,0:T(8,128)S(1)}, u32[]{:S(2)}, u32[]{:S(2)}) collective-permute-start(f32[4,128,128]{2,1,0:T(8,128)S(1)} %get-tuple-element.50), channel_id=1, source_target_pairs={{0,2},{1,3},{2,0},{3,1},{4,6},{5,7},{6,4},{7,5},{8,10},{9,11},{10,... | collective-permute-start | bytes 786440 | tf_op jit(solution)/shard_map/ppermute | solution.py:336
  17.7 4.6 %collective-permute-done.7.refs_2_ = f32[4,128,128]{2,1,0:T(8,128)S(1)} collective-permute-done((f32[4,128,128]{2,1,0:T(8,128)S(1)}, f32[4,128,128]{2,1,0:T(8,128)S(1)}, u32[]{:S(2)}, u32[]{:S(2)}) %collective-permute-start.7) | collective-permute-done | bytes 262176 | tf_op jit(solution)/shard_map/ppermute | solution.py:277
  22.3 0.1 shard_map.79
  22.3 0.1 collective-permute-start.8
  22.4 2.5 %collective-permute-done.1.refs_1_ = f32[4,128,128]{2,1,0:T(8,128)S(1)} collective-permute-done((f32[4,128,128]{2,1,0:T(8,128)S(1)}, f32[4,128,128]{2,1,0:T(8,128)S(1)}, u32[]{:S(2)}, u32[]{:S(2)}) %collective-permute-start.1) | collective-permute-done | bytes 262176 | tf_op jit(solution)/shard_map/ppermute | solution.py:336
  25.0 2.6 %shard_map.70 = (bf16[384,1024]{1,0:T(8,128)(2,1)S(1)}, bf16[384,1024]{1,0:T(8,128)(2,1)S(1)}, bf16[384,1024]{1,0:T(8,128)(2,1)S(1)}) custom-call(bf16[384,2048]{1,0:T(8,128)(2,1)S(1)} %get-tuple-element.42.q_ref, bf16[384,2048]{1,0:T(8,128)(2,1)S(1)} %get-tuple-element.39.k_ref.refs_0_, bf16[384,2048]{1,0:T(8,128)(2,1)S(1)} %get-tuple-element.40.v_ref.refs_1_, ...), custom_call_target="tpu_custom_call" | custom-call | flops 196608 | bytes 196608 | tf_op jit(solution)/shard_map/pallas_call | solution.py:212
  27.7 2.6 %shard_map.71 = (bf16[384,1024]{1,0:T(8,128)(2,1)S(1)}, bf16[384,1024]{1,0:T(8,128)(2,1)S(1)}, bf16[384,1024]{1,0:T(8,128)(2,1)S(1)}) custom-call(bf16[384,2048]{1,0:T(8,128)(2,1)S(1)} %get-tuple-element.42.q_ref, bf16[384,2048]{1,0:T(8,128)(2,1)S(1)} %get-tuple-element.39.k_ref.refs_0_, ...), custom_call_target="tpu_custom_call", output_to_operand_aliasing={{0}: (4, {}), {1}: (5, {}), {2}: (6, {})} | custom-call | flops 196608 | bytes 196608 | tf_op jit(solution)/shard_map/pallas_call | solution.py:212
  30.3 2.3 %collective-permute-done.8.refs_2_ = f32[4,128,128]{2,1,0:T(8,128)S(1)} collective-permute-done((f32[4,128,128]{2,1,0:T(8,128)S(1)}, f32[4,128,128]{2,1,0:T(8,128)S(1)}, u32[]{:S(2)}, u32[]{:S(2)}) %collective-permute-start.8) | collective-permute-done | bytes 262176 | tf_op jit(solution)/shard_map/ppermute | solution.py:277
  32.6 0.1 shard_map.80
  32.7 1.8 %collective-permute-start.9 = (f32[4,128,128]{2,1,0:T(8,128)S(1)}, f32[4,128,128]{2,1,0:T(8,128)S(1)}, u32[]{:S(2)}, u32[]{:S(2)}) collective-permute-start(f32[4,128,128]{2,1,0:T(8,128)S(1)} %get-tuple-element.67), channel_id=1, source_target_pairs={{0,2},{1,3},{2,0},{3,1},{4,6},{5,7},{6,4},{7,5},{8,10},{9,11},{10,... | collective-permute-start | bytes 786440 | tf_op jit(solution)/shard_map/ppermute | solution.py:344
  34.5 0.1 shard_map.73
  34.6 0.1 collective-permute-start.3
  34.6 0.7 %collective-permute-start.10 = (f32[4,128,128]{2,1,0:T(8,128)S(1)}, f32[4,128,128]{2,1,0:T(8,128)S(1)}, u32[]{:S(2)}, u32[]{:S(2)}) collective-permute-start(f32[4,128,128]{2,1,0:T(8,128)S(1)} %get-tuple-element.66.refs_8_), channel_id=1, source_target_pairs={{0,1},{1,0},{2,3},{3,2},{4,5},{5,4},{6,7},{7,6},{8,9},{9,8},{10,11... | collective-permute-start | bytes 786440 | tf_op jit(solution)/shard_map/ppermute | solution.py:345
  35.3 4.2 %collective-permute-done.9.refs_9_ = f32[4,128,128]{2,1,0:T(8,128)S(1)} collective-permute-done((f32[4,128,128]{2,1,0:T(8,128)S(1)}, f32[4,128,128]{2,1,0:T(8,128)S(1)}, u32[]{:S(2)}, u32[]{:S(2)}) %collective-permute-start.9) | collective-permute-done | bytes 262176 | tf_op jit(solution)/shard_map/ppermute | solution.py:344
  39.6 5.2 %collective-permute-done.3.refs_2_ = f32[4,128,128]{2,1,0:T(8,128)S(1)} collective-permute-done((f32[4,128,128]{2,1,0:T(8,128)S(1)}, f32[4,128,128]{2,1,0:T(8,128)S(1)}, u32[]{:S(2)}, u32[]{:S(2)}) %collective-permute-start.3) | collective-permute-done | bytes 262176 | tf_op jit(solution)/shard_map/ppermute | solution.py:277
  44.7 0.1 shard_map.74
  44.8 0.4 collective-permute-start.4
  45.2 3.2 %shard_map.81 = (bf16[384,2048]{1,0:T(8,128)(2,1)}, bf16[384,2048]{1,0:T(8,128)(2,1)}, bf16[384,2048]{1,0:T(8,128)(2,1)}) custom-call(bf16[384,2048]{1,0:T(8,128)(2,1)S(1)} %get-tuple-element.39.k_ref.refs_0_, bf16[384,2048]{1,0:T(8,128)(2,1)S(1)} %get-tuple-element.40.v_ref.refs_1_, bf16[384,2048]{1,0:T(8,128)(2,1)S(1)} %get-tuple-element.41.g_ref.refs_2_, ...), custom_call_target="tpu_custom_call" | custom-call | flops 301989888 | bytes 7077888 | tf_op jit(solution)/shard_map/pallas_call | solution.py:251
  48.3 2.9 %collective-permute-done.4.refs_9_ = f32[4,128,128]{2,1,0:T(8,128)S(1)} collective-permute-done((f32[4,128,128]{2,1,0:T(8,128)S(1)}, f32[4,128,128]{2,1,0:T(8,128)S(1)}, u32[]{:S(2)}, u32[]{:S(2)}) %collective-permute-start.4) | collective-permute-done | bytes 262176 | tf_op jit(solution)/shard_map/ppermute | solution.py:344
  51.2 1.5 %collective-permute-done.13.refs_11_ = f32[4,128,128]{2,1,0:T(8,128)S(1)} collective-permute-done((f32[4,128,128]{2,1,0:T(8,128)S(1)}, f32[4,128,128]{2,1,0:T(8,128)S(1)}, u32[]{:S(2)}, u32[]{:S(2)}) %collective-permute-start.13) | collective-permute-done | bytes 262176 | tf_op jit(solution)/shard_map/ppermute | solution.py:352
  52.8 3.1 %shard_map.82 = (bf16[384,2048]{1,0:T(8,128)(2,1)}, bf16[384,2048]{1,0:T(8,128)(2,1)}, bf16[384,2048]{1,0:T(8,128)(2,1)}) custom-call(bf16[384,2048]{1,0:T(8,128)(2,1)S(1)} %get-tuple-element.39.k_ref.refs_0_, bf16[384,2048]{1,0:T(8,128)(2,1)S(1)} %get-tuple-element.40.v_ref.refs_1_, ...), custom_call_target="tpu_custom_call", output_to_operand_aliasing={{0}: (12, {}), {1}: (13, {}), {2}: (14, {})} | custom-call | flops 301989888 | bytes 7077888 | tf_op jit(solution)/shard_map/pallas_call | solution.py:251
  (15 shorter events, 0.2 us)
Async XLA Ops:
  3.6 2.1 %collective-permute-start.5 = (f32[8,128,128]{2,1,0:T(8,128)S(1)}, f32[8,128,128]{2,1,0:T(8,128)S(1)}, u32[]{:S(2)}, u32[]{:S(2)}) collective-permute-start(f32[8,128,128]{2,1,0:T(8,128)S(1)} %get-tuple-element.61), channel_id=1, source_target_pairs={{0,1},{1,0},{2,3},{3,2},{4,5},{5,4},{6,7},{7,6},{8,9},{9,8},{10,11... | collective-permute-start | bytes 1572872 | tf_op jit(solution)/shard_map/ppermute | solution.py:333
  4.7 4.5 %collective-permute-start = (f32[8,128,128]{2,1,0:T(8,128)S(1)}, f32[8,128,128]{2,1,0:T(8,128)S(1)}, u32[]{:S(2)}, u32[]{:S(2)}) collective-permute-start(f32[8,128,128]{2,1,0:T(8,128)S(1)} %shard_map.68), channel_id=1, source_target_pairs={{0,1},{1,0},{2,3},{3,2},{4,5},{5,4},{6,7},{7,6},{8,9},{9,8},{10,11... | collective-permute-start | bytes 1572872 | tf_op jit(solution)/shard_map/ppermute | solution.py:333
  6.3 9.6 %collective-permute-start.6 = (f32[4,128,128]{2,1,0:T(8,128)S(1)}, f32[4,128,128]{2,1,0:T(8,128)S(1)}, u32[]{:S(2)}, u32[]{:S(2)}) collective-permute-start(f32[4,128,128]{2,1,0:T(8,128)S(1)} %get-tuple-element.63), channel_id=1, source_target_pairs={{0,2},{1,3},{2,0},{3,1},{4,6},{5,7},{6,4},{7,5},{8,10},{9,11},{10,... | collective-permute-start | bytes 786440 | tf_op jit(solution)/shard_map/ppermute | solution.py:336
  15.9 6.4 %collective-permute-start.7 = (f32[4,128,128]{2,1,0:T(8,128)S(1)}, f32[4,128,128]{2,1,0:T(8,128)S(1)}, u32[]{:S(2)}, u32[]{:S(2)}) collective-permute-start(f32[4,128,128]{2,1,0:T(8,128)S(1)} %shard_map.78.refs_0_), channel_id=1, source_target_pairs={{0,1},{1,5},{2,3},{3,7},{4,0},{5,9},{6,2},{7,11},{8,4},{9,13},{10,... | collective-permute-start | bytes 786440 | tf_op jit(solution)/shard_map/ppermute | solution.py:277
  15.9 9.0 %collective-permute-start.1 = (f32[4,128,128]{2,1,0:T(8,128)S(1)}, f32[4,128,128]{2,1,0:T(8,128)S(1)}, u32[]{:S(2)}, u32[]{:S(2)}) collective-permute-start(f32[4,128,128]{2,1,0:T(8,128)S(1)} %get-tuple-element.50), channel_id=1, source_target_pairs={{0,2},{1,3},{2,0},{3,1},{4,6},{5,7},{6,4},{7,5},{8,10},{9,11},{10,... | collective-permute-start | bytes 786440 | tf_op jit(solution)/shard_map/ppermute | solution.py:336
  22.3 10.2 %collective-permute-start.8 = (f32[4,128,128]{2,1,0:T(8,128)S(1)}, f32[4,128,128]{2,1,0:T(8,128)S(1)}, u32[]{:S(2)}, u32[]{:S(2)}) collective-permute-start(f32[4,128,128]{2,1,0:T(8,128)S(1)} %get-tuple-element.64), channel_id=1, source_target_pairs={{0,1},{1,9},{2,3},{3,11},{4,5},{5,13},{6,7},{7,15},{8,0},{9,8},{10... | collective-permute-start | bytes 786440 | tf_op jit(solution)/shard_map/ppermute | solution.py:277
  25.0 9.5 %collective-permute-start.2 = (f32[4,128,128]{2,1,0:T(8,128)S(1)}, f32[4,128,128]{2,1,0:T(8,128)S(1)}, u32[]{:S(2)}, u32[]{:S(2)}) collective-permute-start(f32[4,128,128]{2,1,0:T(8,128)S(1)} %shard_map.72.refs_0_), channel_id=1, source_target_pairs={{0,1},{1,5},{2,3},{3,7},{4,0},{5,9},{6,2},{7,11},{8,4},{9,13},{10,... | collective-permute-start | bytes 786440 | tf_op jit(solution)/shard_map/ppermute | solution.py:277
  32.7 6.9 %collective-permute-start.9 = (f32[4,128,128]{2,1,0:T(8,128)S(1)}, f32[4,128,128]{2,1,0:T(8,128)S(1)}, u32[]{:S(2)}, u32[]{:S(2)}) collective-permute-start(f32[4,128,128]{2,1,0:T(8,128)S(1)} %get-tuple-element.67), channel_id=1, source_target_pairs={{0,2},{1,3},{2,0},{3,1},{4,6},{5,7},{6,4},{7,5},{8,10},{9,11},{10,... | collective-permute-start | bytes 786440 | tf_op jit(solution)/shard_map/ppermute | solution.py:344
  34.6 10.1 %collective-permute-start.3 = (f32[4,128,128]{2,1,0:T(8,128)S(1)}, f32[4,128,128]{2,1,0:T(8,128)S(1)}, u32[]{:S(2)}, u32[]{:S(2)}) collective-permute-start(f32[4,128,128]{2,1,0:T(8,128)S(1)} %get-tuple-element.51), channel_id=1, source_target_pairs={{0,1},{1,9},{2,3},{3,11},{4,5},{5,13},{6,7},{7,15},{8,0},{9,8},{10... | collective-permute-start | bytes 786440 | tf_op jit(solution)/shard_map/ppermute | solution.py:277
  34.6 10.5 %collective-permute-start.10 = (f32[4,128,128]{2,1,0:T(8,128)S(1)}, f32[4,128,128]{2,1,0:T(8,128)S(1)}, u32[]{:S(2)}, u32[]{:S(2)}) collective-permute-start(f32[4,128,128]{2,1,0:T(8,128)S(1)} %get-tuple-element.66.refs_8_), channel_id=1, source_target_pairs={{0,1},{1,0},{2,3},{3,2},{4,5},{5,4},{6,7},{7,6},{8,9},{9,8},{10,11... | collective-permute-start | bytes 786440 | tf_op jit(solution)/shard_map/ppermute | solution.py:345
  39.5 5.6 %collective-permute-start.11 = (f32[4,128,128]{2,1,0:T(8,128)S(1)}, f32[4,128,128]{2,1,0:T(8,128)S(1)}, u32[]{:S(2)}, u32[]{:S(2)}) collective-permute-start(f32[4,128,128]{2,1,0:T(8,128)S(1)} %collective-permute-done.9.refs_9_), channel_id=1, source_target_pairs={{0,1},{1,0},{2,3},{3,2},{4,5},{5,4},{6,7},{7,6},{8,9},{9,8},{10,11... | collective-permute-start | bytes 786440 | tf_op jit(solution)/shard_map/ppermute | solution.py:352
  44.8 6.4 %collective-permute-start.4 = (f32[4,128,128]{2,1,0:T(8,128)S(1)}, f32[4,128,128]{2,1,0:T(8,128)S(1)}, u32[]{:S(2)}, u32[]{:S(2)}) collective-permute-start(f32[4,128,128]{2,1,0:T(8,128)S(1)} %get-tuple-element.54), channel_id=1, source_target_pairs={{0,2},{1,3},{2,0},{3,1},{4,6},{5,7},{6,4},{7,5},{8,10},{9,11},{10,... | collective-permute-start | bytes 786440 | tf_op jit(solution)/shard_map/ppermute | solution.py:344
  45.1 6.1 %collective-permute-start.12 = (f32[4,128,128]{2,1,0:T(8,128)S(1)}, f32[4,128,128]{2,1,0:T(8,128)S(1)}, u32[]{:S(2)}, u32[]{:S(2)}) collective-permute-start(f32[4,128,128]{2,1,0:T(8,128)S(1)} %get-tuple-element.53.refs_8_), channel_id=1, source_target_pairs={{0,1},{1,0},{2,3},{3,2},{4,5},{5,4},{6,7},{7,6},{8,9},{9,8},{10,11... | collective-permute-start | bytes 786440 | tf_op jit(solution)/shard_map/ppermute | solution.py:345
  51.2 1.5 %collective-permute-start.13 = (f32[4,128,128]{2,1,0:T(8,128)S(1)}, f32[4,128,128]{2,1,0:T(8,128)S(1)}, u32[]{:S(2)}, u32[]{:S(2)}) collective-permute-start(f32[4,128,128]{2,1,0:T(8,128)S(1)} %collective-permute-done.4.refs_9_), channel_id=1, source_target_pairs={{0,1},{1,0},{2,3},{3,2},{4,5},{5,4},{6,7},{7,6},{8,9},{9,8},{10,11... | collective-permute-start | bytes 786440 | tf_op jit(solution)/shard_map/ppermute | solution.py:352

commit v3 on v2

--- a/solution.py
+++ b/solution.py
@@ -10,13 +10,17 @@
 HD = 128
 CHUNKS = (8, 8)
 RADIX = 2
+TREE = True
 PIECE = 4
 PLACES = (
     ((0, 0), ("kept", 1), ("plane", 0)),
     ((0, 1), ("kept", 1), ("plane", 0)),
-    ((1, 0), ("kept", 1), ("scan", 0)),
-    ((1, 1), ("kept", 1), ("scan", 0)),
+    ((1, 0), ("back", 0), ("scan", 1)),
+    ((1, 1), ("back", 0), ("scan", 1)),
 )
+RADIX = 2
+TREE = True
+PIECE = 4
 F32 = jnp.float32
 BF16 = jnp.bfloat16
 VMEM_LIMIT = 24 * 1024 * 1024
@@ -31,7 +35,7 @@
 
 
 def cost(flops, size):
-    return pl.CostEstimate(flops=flops, bytes_accessed=size, transcendentals=0)
+    return pl.CostEstimate(flops=0, bytes_accessed=0, transcendentals=0)
 
 
 def place():
@@ -105,14 +109,14 @@
     )(*arrays)
 
 
-def other_kernel(size, q_ref, k_ref, v_ref, g_ref, out_ref):
+def other_kernel(first, size, q_ref, k_ref, v_ref, g_ref, out_ref):
     later, second = place()
     half = size // 2
     turn = jnp.where(second, 0, half)
 
     def run(a_ref, b_ref):
         for h in range(size):
-            cols = slice(h * HD, (h + 1) * HD)
+            cols = slice((first + h) * HD, (first + h + 1) * HD)
             at = lax.rem(h // half * half + turn, size) + h % half
             out_ref[at] = dot(a_ref[:, cols], b_ref[:, cols], ((0,), (0,)))
 
@@ -125,14 +129,14 @@
         run(k_ref, v_ref)
 
 
-def mine_kernel(size, q_ref, k_ref, v_ref, g_ref, other_ref, kept_ref, sent_ref):
+def mine_kernel(first, size, q_ref, k_ref, v_ref, g_ref, other_ref, kept_ref, sent_ref):
     later, second = place()
     half = size // 2
 
     def run(pair, swap):
         refs = (sent_ref, kept_ref) if swap else (kept_ref, sent_ref)
         for h in range(size):
-            cols = slice(h * HD, (h + 1) * HD)
+            cols = slice((first + h) * HD, (first + h + 1) * HD)
             at = (h + (half if swap else 0)) % size
             value = dot(pair[0][:, cols], pair[1][:, cols], ((0,), (0,)))
             refs[h // half][h % half] = value + other_ref[at]
@@ -144,13 +148,11 @@
 
 def other_state(arrays, first, size):
     rows = arrays[0].shape[0]
-    block = pl.BlockSpec((rows, size * HD), lambda i: (0, first // size))
-    return pl.pallas_call(
-        functools.partial(other_kernel, size),
-        grid=(1,),
+    return pl.pallas_call(
+        functools.partial(other_kernel, first, size),
         out_shape=jax.ShapeDtypeStruct((size, HD, HD), F32),
-        in_specs=[block] * 4,
-        out_specs=pl.BlockSpec((size, HD, HD), lambda i: (0, 0, 0)),
+        in_specs=[VMEM] * 4,
+        out_specs=VMEM,
         compiler_params=pltpu.CompilerParams(vmem_limit_bytes=VMEM_LIMIT),
         cost_estimate=cost(2 * size * rows * HD * HD, 4 * size * rows * HD),
     )(*arrays)
@@ -159,14 +161,11 @@
 def chip_state(arrays, other, first, size):
     rows = arrays[0].shape[0]
     half = jax.ShapeDtypeStruct((size // 2, HD, HD), F32)
-    block = pl.BlockSpec((rows, size * HD), lambda i: (0, first // size))
-    out = pl.BlockSpec((size // 2, HD, HD), lambda i: (0, 0, 0))
-    return pl.pallas_call(
-        functools.partial(mine_kernel, size),
-        grid=(1,),
+    return pl.pallas_call(
+        functools.partial(mine_kernel, first, size),
         out_shape=[half, half],
-        in_specs=[block] * 4 + [pl.BlockSpec((size, HD, HD), lambda i: (0, 0, 0))],
-        out_specs=[out, out],
+        in_specs=[VMEM] * 5,
+        out_specs=[VMEM, VMEM],
         compiler_params=pltpu.CompilerParams(vmem_limit_bytes=VMEM_LIMIT),
         cost_estimate=cost(2 * size * rows * HD * HD, 4 * size * rows * HD),
     )(*arrays, other)
@@ -265,51 +264,42 @@
     heads = queries.shape[1] // HD
     scale = float(1.0 / (HD * rows * seq) ** 0.5)
     planes = seq // 4
-    at = lax.axis_index("seq")
     core_pairs = [(i, i ^ 1) for i in range(seq)]
     chip_pairs = [(i, i ^ 2) for i in range(seq)]
 
-    def shift(value, by):
-        pairs = []
+    def moved(value, plan):
+        pairs = {}
+        for to, source in plan.items():
+            for chip in range(2):
+                pairs[4 * source + 2 * chip + 1] = 4 * to + 2 * chip + 1
+                pairs[4 * (planes - 1 - source) + 2 * chip] = 4 * (planes - 1 - to) + 2 * chip
+        free = set(range(seq)) - set(pairs.values())
         for i in range(seq):
-            j = i + 4 * by if i % 2 else i - 4 * by
-            pairs.append((i, j if 0 <= j < seq else i ^ 1))
-        return lax.ppermute(value, "seq", pairs)
-
-    def plane_at():
+            if i not in pairs and i ^ 1 in free:
+                pairs[i] = i ^ 1
+                free.discard(i ^ 1)
+        for chip in range(2):
+            senders = [i for i in range(seq) if i not in pairs and i // 2 % 2 == chip]
+            targets = [i for i in sorted(free) if i // 2 % 2 == chip]
+            pairs.update(zip(senders, targets))
+        return lax.ppermute(value, "seq", sorted(pairs.items()))
+
+    def masked(total, values, plans):
         later, _ = place()
         plane = lax.axis_index("seq") // 4
-        return jnp.where(later, plane, planes - 1 - plane)
-
-    def masked(values, steps):
-        total = jnp.zeros_like(values[0])
-        for value, step in zip(values, steps):
-            total = total + jnp.where(plane_at() >= step, value, 0.0)
+        plane = jnp.where(later, plane, planes - 1 - plane)
+        for value, plan in zip(values, plans):
+            wanted = functools.reduce(jnp.logical_or, [plane == to for to in plan])
+            total = total + jnp.where(wanted, value, 0.0)
         return total
 
-    def scan(plane, kept, partner, after):
-        before, window, by = None, plane, 1
-        while True:
-            steps = [j * by for j in range(1, RADIX) if j * by < planes]
-            arrived = [shift(window, step) for step in steps]
+    if planes == 4 and TREE:
+        levels = [[{1: 0, 3: 2}], [{2: 1}, {3: 1}]]
+    else:
+        levels, by = [], 1
+        while by < planes:
+            levels.append([{to: to - j * by for to in range(j * by, planes)} for j in range(1, RADIX) if j * by < planes])
             by *= RADIX
-            if by >= planes:
-                break
-
-            def more(window, before, *arrived):
-                add = masked(arrived, steps)
-                return window + add, before + add
-
-            window, before = sums(more, 2, [window, jnp.zeros_like(plane) if before is None else before, *arrived])
-
-        def last(kept, partner, *arrived):
-            _, second = place()
-            total = masked(arrived[: len(steps)], steps)
-            for value in arrived[len(steps) :]:
-                total = total + value
-            return total + jnp.where(second, 0.0, kept), total + jnp.where(second, partner, 0.0)
-
-        return sums(last, 2, [kept, partner, *arrived, *([] if before is None else [before])], after)
 
     sizes = [heads * part // sum(CHUNKS) for part in CHUNKS]
     firsts = [sum(sizes[:i]) for i in range(len(sizes))]
@@ -334,21 +324,50 @@
     for c in chunks:
         made["kept", c], sent = chip_state(arrays, made["other", c], firsts[c], sizes[c])
         made["partner", c] = lax.ppermute(sent, "seq", chip_pairs)
+    def stage(name, c, before):
+        return wait_for(name, c) + ([made[before, c + 1]] if c + 1 < len(sizes) else [])
+
     for c in chunks:
         terms = [made["kept", c], made["partner", c]]
-        (made["plane", c],) = sums(lambda a, b: (a + b,), 1, terms, wait_for("plane", c))
+        (made["plane", c],) = sums(lambda a, b: (a + b,), 1, terms, stage("plane", c, "kept"))
+        made["before", c] = None
+    last = "plane"
+    for number, plans in enumerate(levels[:-1]):
+        name = f"window{number}"
+        for c in chunks:
+
+            def more(window, *arrived):
+                add = masked(jnp.zeros_like(window), arrived[: len(plans)], plans)
+                return window + add, sum(arrived[len(plans) :], add)
+
+            window = made[last, c]
+            arrived = [moved(window, plan) for plan in plans]
+            held = [] if made["before", c] is None else [made["before", c]]
+            made[name, c], made["before", c] = sums(more, 2, [window, *arrived, *held], stage(name, c, last))
+        last = name
+
     done = []
     for c in chunks:
-        kept, partner = made["kept", c], made["partner", c]
-        back, kept_upto = scan(made["plane", c], kept, partner, wait_for("scan", c))
-        swapped = lax.ppermute(back, "seq", chip_pairs)
+        plans = levels[-1]
+
+        def ready(kept, partner, *arrived):
+            _, second = place()
+            total = masked(jnp.zeros_like(kept), arrived[: len(plans)], plans)
+            total = sum(arrived[len(plans) :], total)
+            return total + jnp.where(second, 0.0, kept), total + jnp.where(second, partner, 0.0)
+
+        arrived = [moved(made[last, c], plan) for plan in plans]
+        held = [] if made["before", c] is None else [made["before", c]]
+        terms = [made["kept", c], made["partner", c], *arrived, *held]
+        made["back", c], kept_upto = sums(ready, 2, terms, stage("scan", c, last))
+        swapped = lax.ppermute(made["back", c], "seq", chip_pairs)
         done.append((made["other", c], kept_upto, swapped, lax.ppermute(kept_upto, "seq", core_pairs)))
 
     out = ()
     for chunk, (first, size) in enumerate(zip(firsts, sizes)):
         other, kept_upto, swapped, given_kept = done[chunk]
-        if out:
-            swapped, out = lax.optimization_barrier((swapped, out))
+        ahead = [made["back", chunk + 1]] if chunk + 1 < len(sizes) else []
+        swapped, out, ahead = lax.optimization_barrier((swapped, out, ahead))
         given_swapped = lax.ppermute(swapped, "seq", core_pairs)
         states = (kept_upto, swapped, given_kept, given_swapped)
         out = final(keys, values, out_grad, pieces[chunk], other, states, first, size, scale, out)

time: 56.1 us -> 53.3 us (0.950)
  waiting for transfers between devices: 24.7 us -> 21.7 us
  starting transfers between devices: 8.39 us -> 9.2 us
  Pallas kernels: 22 us -> 21.4 us
    ppermute x6 -> x8, waiting for transfers between devices: 19.1 us -> 13.1 us  [the longest x6 8.27 us: moved(): return lax.ppermute(value, 'seq', sorted(pairs.items()))]
    ppermute x2, waiting for transfers between devices: 3.2 us -> 6.09 us  [local(): made['partner', c] = lax.ppermute(sent, 'seq', chip_pairs)]
    ppermute x6 -> x8, starting transfers between devices: 2.34 us -> 4.83 us  [the longest x2 3.55 us: local(): swapped = lax.ppermute(made['back', c], 'seq', chip_pairs)]
    ppermute x2, starting transfers between devices: 4.73 us -> 3.23 us  [local(): made['partner', c] = lax.ppermute(sent, 'seq', chip_pairs)]
    pallas_call x3, Pallas kernels: 1.91 us -> 1.3 us  [the longest x2 0.87 us: chip_state(): pl.pallas_call(functools.partial(mine_kernel, first, size), out_shape=[ha...]
  transfers between devices with their start and end apart: 14 -> 16, of which waited for: 9 -> 8; matrix products, arithmetic and copies ran while one was open for 0% -> 0% of each run, Pallas kernels for 28% -> 29%
where the time goes in v3:
time: 53.3 us; the launch traced here: 53.2 us
  waiting for transfers between devices  21.7 us (41%)
  Pallas kernels  21.4 us (40%)
  starting transfers between devices  9.2 us (17%)
  between operations  0.82 us (2%)
    pallas_call x4, Pallas kernels, within(): pl.pallas_call(functools.partial(within_kernel, per, scale), grid=(heads...  10.4 us
    ppermute x6, waiting for transfers between devices, moved(): return lax.ppermute(value, 'seq', sorted(pairs.items()))  8.27 us
    pallas_call x2, Pallas kernels, final(): pl.pallas_call(functools.partial(final_kernel, per, half, scale), grid=(s...  6.3 us
    ppermute x2, waiting for transfers between devices, local(): made['partner', c] = lax.ppermute(sent, 'seq', chip_pairs)  6.09 us
    ppermute x2, waiting for transfers between devices, local(): swapped = lax.ppermute(made['back', c], 'seq', chip_pairs)  4.81 us
    ppermute x2, starting transfers between devices, local(): swapped = lax.ppermute(made['back', c], 'seq', chip_pairs)  3.55 us
    ppermute x2, starting transfers between devices, local(): made['partner', c] = lax.ppermute(sent, 'seq', chip_pairs)  3.23 us
    pallas_call x1, Pallas kernels, first_state(): pl.pallas_call(functools.partial(first_kernel, size), out_shape=[jax.Shap...  2.94 us
  transfers between devices with their start and end apart: 16, of which 8 were waited for; matrix products, arithmetic and copies ran while one was open for 0% of the time, Pallas kernels for 29%

profile of v3, /device:TPU:0, one launch (start us, length us, event | category | flops | bytes accessed | tf_op | source)
XLA Modules:
  0.0 53.2 jit_solution(8260442915977530177)
XLA Ops:
  0.6 2.9 %shard_map.67 = (f32[8,128,128]{2,1,0:T(8,128)S(1)}, bf16[384,2048]{1,0:T(8,128)(2,1)S(1)}, bf16[384,2048]{1,0:T(8,128)(2,1)S(1)}, bf16[384,2048]{1,0:T(8,128)(2,1)S(1)}, bf16[384,2048]{1,0:T(8,128)(2,1)S(1)}) custom-call(bf16[384,2048]{1,0:T(8,128)(2,1)} %q_ref.1, bf16[384,2048]{1,0:T(8,128)(2,1)} %k_ref.1, bf16[384,2048]{1,0:T(8,128)(2,1)} %v_ref.1, ...), custom_call_target="tpu_custom_call" | custom-call | tf_op jit(solution)/shard_map/pallas_call | solution.py:101
  3.6 0.5 collective-permute-start
  4.1 0.4 shard_map.69
  4.5 0.1 collective-permute-start.2
  4.7 1.0 %collective-permute-done.other_ref.refs_6_.refs_7_ = f32[8,128,128]{2,1,0:T(8,128)S(1)} collective-permute-done((f32[8,128,128]{2,1,0:T(8,128)S(1)}, f32[8,128,128]{2,1,0:T(8,128)S(1)}, u32[]{:S(2)}, u32[]{:S(2)}) %collective-permute-start) | collective-permute-done | bytes 524320 | tf_op jit(solution)/shard_map/ppermute | solution.py:323
  5.6 0.4 shard_map.68
  6.1 2.9 %collective-permute-start.1 = (f32[4,128,128]{2,1,0:T(8,128)S(1)}, f32[4,128,128]{2,1,0:T(8,128)S(1)}, u32[]{:S(2)}, u32[]{:S(2)}) collective-permute-start(f32[4,128,128]{2,1,0:T(8,128)S(1)} %get-tuple-element.46), channel_id=1, source_target_pairs={{0,2},{1,3},{2,0},{3,1},{4,6},{5,7},{6,4},{7,5},{8,10},{9,11},{10,... | collective-permute-start | bytes 786440 | tf_op jit(solution)/shard_map/ppermute | solution.py:326
  9.0 0.4 shard_map.70
  9.4 0.3 collective-permute-start.4
  9.8 2.6 %shard_map.71 = (bf16[384,1024]{1,0:T(8,128)(2,1)S(1)}, bf16[384,1024]{1,0:T(8,128)(2,1)S(1)}, bf16[384,1024]{1,0:T(8,128)(2,1)S(1)}) custom-call(bf16[384,2048]{1,0:T(8,128)(2,1)S(1)} %get-tuple-element.43.q_ref, bf16[384,2048]{1,0:T(8,128)(2,1)S(1)} %get-tuple-element.40.k_ref.refs_0_, bf16[384,2048]{1,0:T(8,128)(2,1)S(1)} %get-tuple-element.41.v_ref.refs_1_, ...), custom_call_target="tpu_custom_call" | custom-call | tf_op jit(solution)/shard_map/pallas_call | solution.py:211
  12.4 2.6 %shard_map.72 = (bf16[384,1024]{1,0:T(8,128)(2,1)S(1)}, bf16[384,1024]{1,0:T(8,128)(2,1)S(1)}, bf16[384,1024]{1,0:T(8,128)(2,1)S(1)}) custom-call(bf16[384,2048]{1,0:T(8,128)(2,1)S(1)} %get-tuple-element.43.q_ref, bf16[384,2048]{1,0:T(8,128)(2,1)S(1)} %get-tuple-element.40.k_ref.refs_0_, ...), custom_call_target="tpu_custom_call", output_to_operand_aliasing={{0}: (4, {}), {1}: (5, {}), {2}: (6, {})} | custom-call | tf_op jit(solution)/shard_map/pallas_call | solution.py:211
  15.0 1.1 %collective-permute-done.1.refs_1_ = f32[4,128,128]{2,1,0:T(8,128)S(1)} collective-permute-done((f32[4,128,128]{2,1,0:T(8,128)S(1)}, f32[4,128,128]{2,1,0:T(8,128)S(1)}, u32[]{:S(2)}, u32[]{:S(2)}) %collective-permute-start.1) | collective-permute-done | bytes 262176 | tf_op jit(solution)/shard_map/ppermute | solution.py:326
  16.1 0.1 collective-permute-start.3
  16.2 5.0 %collective-permute-done.4.refs_1_ = f32[4,128,128]{2,1,0:T(8,128)S(1)} collective-permute-done((f32[4,128,128]{2,1,0:T(8,128)S(1)}, f32[4,128,128]{2,1,0:T(8,128)S(1)}, u32[]{:S(2)}, u32[]{:S(2)}) %collective-permute-start.4) | collective-permute-done | bytes 262176 | tf_op jit(solution)/shard_map/ppermute | solution.py:326
  21.3 0.1 collective-permute-start.7
  21.3 1.3 %collective-permute-done.3.refs_1_ = f32[4,128,128]{2,1,0:T(8,128)S(1)} collective-permute-done((f32[4,128,128]{2,1,0:T(8,128)S(1)}, f32[4,128,128]{2,1,0:T(8,128)S(1)}, u32[]{:S(2)}, u32[]{:S(2)}) %collective-permute-start.3) | collective-permute-done | bytes 262176 | tf_op jit(solution)/shard_map/ppermute | solution.py:285
  22.8 0.8 %collective-permute-start.5 = (f32[4,128,128]{2,1,0:T(8,128)S(1)}, f32[4,128,128]{2,1,0:T(8,128)S(1)}, u32[]{:S(2)}, u32[]{:S(2)}) collective-permute-start(f32[4,128,128]{2,1,0:T(8,128)S(1)} %get-tuple-element.53), channel_id=1, source_target_pairs={{0,1},{1,0},{2,3},{3,2},{4,5},{5,9},{6,7},{7,11},{8,4},{9,8},{10,6... | collective-permute-start | bytes 786440 | tf_op jit(solution)/shard_map/ppermute | solution.py:285
  23.6 6.9 %collective-permute-done.7.refs_1_ = f32[4,128,128]{2,1,0:T(8,128)S(1)} collective-permute-done((f32[4,128,128]{2,1,0:T(8,128)S(1)}, f32[4,128,128]{2,1,0:T(8,128)S(1)}, u32[]{:S(2)}, u32[]{:S(2)}) %collective-permute-start.7) | collective-permute-done | bytes 262176 | tf_op jit(solution)/shard_map/ppermute | solution.py:285
  30.6 0.2 collective-permute-start.8
  30.9 0.1 shard_map.77
  31.0 1.8 %collective-permute-start.11 = (f32[4,128,128]{2,1,0:T(8,128)S(1)}, f32[4,128,128]{2,1,0:T(8,128)S(1)}, u32[]{:S(2)}, u32[]{:S(2)}) collective-permute-start(f32[4,128,128]{2,1,0:T(8,128)S(1)} %get-tuple-element.56.refs_0_.refs_3_), channel_id=1, source_target_pairs={{0,2},{1,3},{2,0},{3,1},{4,6},{5,7},{6,4},{7,5},{8,10},{9,11},{10,... | collective-permute-start | bytes 786440 | tf_op jit(solution)/shard_map/ppermute | solution.py:363
  32.8 2.6 %shard_map.78 = (bf16[384,1024]{1,0:T(8,128)(2,1)S(1)}, bf16[384,1024]{1,0:T(8,128)(2,1)S(1)}, bf16[384,1024]{1,0:T(8,128)(2,1)S(1)}) custom-call(bf16[384,2048]{1,0:T(8,128)(2,1)S(1)} %get-tuple-element.43.q_ref, bf16[384,2048]{1,0:T(8,128)(2,1)S(1)} %get-tuple-element.40.k_ref.refs_0_, bf16[384,2048]{1,0:T(8,128)(2,1)S(1)} %get-tuple-element.41.v_ref.refs_1_, ...), custom_call_target="tpu_custom_call" | custom-call | tf_op jit(solution)/shard_map/pallas_call | solution.py:211
  35.4 0.3 collective-permute-start.12
  35.8 2.6 %shard_map.79 = (bf16[384,1024]{1,0:T(8,128)(2,1)S(1)}, bf16[384,1024]{1,0:T(8,128)(2,1)S(1)}, bf16[384,1024]{1,0:T(8,128)(2,1)S(1)}) custom-call(bf16[384,2048]{1,0:T(8,128)(2,1)S(1)} %get-tuple-element.43.q_ref, bf16[384,2048]{1,0:T(8,128)(2,1)S(1)} %get-tuple-element.40.k_ref.refs_0_, ...), custom_call_target="tpu_custom_call", output_to_operand_aliasing={{0}: (4, {}), {1}: (5, {}), {2}: (6, {})} | custom-call | tf_op jit(solution)/shard_map/pallas_call | solution.py:211
  38.4 0.1 shard_map.80
  38.6 1.2 %collective-permute-done.11.refs_9_ = f32[4,128,128]{2,1,0:T(8,128)S(1)} collective-permute-done((f32[4,128,128]{2,1,0:T(8,128)S(1)}, f32[4,128,128]{2,1,0:T(8,128)S(1)}, u32[]{:S(2)}, u32[]{:S(2)}) %collective-permute-start.11) | collective-permute-done | bytes 262176 | tf_op jit(solution)/shard_map/ppermute | solution.py:363
  39.8 1.7 %collective-permute-start.10 = (f32[4,128,128]{2,1,0:T(8,128)S(1)}, f32[4,128,128]{2,1,0:T(8,128)S(1)}, u32[]{:S(2)}, u32[]{:S(2)}) collective-permute-start(f32[4,128,128]{2,1,0:T(8,128)S(1)} %get-tuple-element.65), channel_id=1, source_target_pairs={{0,2},{1,3},{2,0},{3,1},{4,6},{5,7},{6,4},{7,5},{8,10},{9,11},{10,... | collective-permute-start | bytes 786440 | tf_op jit(solution)/shard_map/ppermute | solution.py:363
  41.5 0.2 collective-permute-start.14
  41.8 3.2 %shard_map.81 = (bf16[384,2048]{1,0:T(8,128)(2,1)}, bf16[384,2048]{1,0:T(8,128)(2,1)}, bf16[384,2048]{1,0:T(8,128)(2,1)}) custom-call(bf16[384,2048]{1,0:T(8,128)(2,1)S(1)} %get-tuple-element.40.k_ref.refs_0_, bf16[384,2048]{1,0:T(8,128)(2,1)S(1)} %get-tuple-element.41.v_ref.refs_1_, bf16[384,2048]{1,0:T(8,128)(2,1)S(1)} %get-tuple-element.42.g_ref.refs_2_, ...), custom_call_target="tpu_custom_call" | custom-call | tf_op jit(solution)/shard_map/pallas_call | solution.py:250
  44.9 3.6 %collective-permute-done.10.refs_9_ = f32[4,128,128]{2,1,0:T(8,128)S(1)} collective-permute-done((f32[4,128,128]{2,1,0:T(8,128)S(1)}, f32[4,128,128]{2,1,0:T(8,128)S(1)}, u32[]{:S(2)}, u32[]{:S(2)}) %collective-permute-start.10) | collective-permute-done | bytes 262176 | tf_op jit(solution)/shard_map/ppermute | solution.py:363
  48.5 1.5 %collective-permute-done.15.refs_11_ = f32[4,128,128]{2,1,0:T(8,128)S(1)} collective-permute-done((f32[4,128,128]{2,1,0:T(8,128)S(1)}, f32[4,128,128]{2,1,0:T(8,128)S(1)}, u32[]{:S(2)}, u32[]{:S(2)}) %collective-permute-start.15) | collective-permute-done | bytes 262176 | tf_op jit(solution)/shard_map/ppermute | solution.py:371
  50.0 3.1 %shard_map.82 = (bf16[384,2048]{1,0:T(8,128)(2,1)}, bf16[384,2048]{1,0:T(8,128)(2,1)}, bf16[384,2048]{1,0:T(8,128)(2,1)}) custom-call(bf16[384,2048]{1,0:T(8,128)(2,1)S(1)} %get-tuple-element.40.k_ref.refs_0_, bf16[384,2048]{1,0:T(8,128)(2,1)S(1)} %get-tuple-element.41.v_ref.refs_1_, ...), custom_call_target="tpu_custom_call", output_to_operand_aliasing={{0}: (12, {}), {1}: (13, {}), {2}: (14, {})} | custom-call | tf_op jit(solution)/shard_map/pallas_call | solution.py:250
  (18 shorter events, 0.4 us)
Async XLA Ops:
  3.6 2.1 %collective-permute-start = (f32[8,128,128]{2,1,0:T(8,128)S(1)}, f32[8,128,128]{2,1,0:T(8,128)S(1)}, u32[]{:S(2)}, u32[]{:S(2)}) collective-permute-start(f32[8,128,128]{2,1,0:T(8,128)S(1)} %get-tuple-element.44), channel_id=1, source_target_pairs={{0,1},{1,0},{2,3},{3,2},{4,5},{5,4},{6,7},{7,6},{8,9},{9,8},{10,11... | collective-permute-start | bytes 1572872 | tf_op jit(solution)/shard_map/ppermute | solution.py:323
  4.5 4.5 %collective-permute-start.2 = (f32[8,128,128]{2,1,0:T(8,128)S(1)}, f32[8,128,128]{2,1,0:T(8,128)S(1)}, u32[]{:S(2)}, u32[]{:S(2)}) collective-permute-start(f32[8,128,128]{2,1,0:T(8,128)S(1)} %shard_map.69), channel_id=1, source_target_pairs={{0,1},{1,0},{2,3},{3,2},{4,5},{5,4},{6,7},{7,6},{8,9},{9,8},{10,11... | collective-permute-start | bytes 1572872 | tf_op jit(solution)/shard_map/ppermute | solution.py:323
  6.1 10.0 %collective-permute-start.1 = (f32[4,128,128]{2,1,0:T(8,128)S(1)}, f32[4,128,128]{2,1,0:T(8,128)S(1)}, u32[]{:S(2)}, u32[]{:S(2)}) collective-permute-start(f32[4,128,128]{2,1,0:T(8,128)S(1)} %get-tuple-element.46), channel_id=1, source_target_pairs={{0,2},{1,3},{2,0},{3,1},{4,6},{5,7},{6,4},{7,5},{8,10},{9,11},{10,... | collective-permute-start | bytes 786440 | tf_op jit(solution)/shard_map/ppermute | solution.py:326
  9.4 11.8 %collective-permute-start.4 = (f32[4,128,128]{2,1,0:T(8,128)S(1)}, f32[4,128,128]{2,1,0:T(8,128)S(1)}, u32[]{:S(2)}, u32[]{:S(2)}) collective-permute-start(f32[4,128,128]{2,1,0:T(8,128)S(1)} %get-tuple-element.52), channel_id=1, source_target_pairs={{0,2},{1,3},{2,0},{3,1},{4,6},{5,7},{6,4},{7,5},{8,10},{9,11},{10,... | collective-permute-start | bytes 786440 | tf_op jit(solution)/shard_map/ppermute | solution.py:326
  16.1 6.6 %collective-permute-start.3 = (f32[4,128,128]{2,1,0:T(8,128)S(1)}, f32[4,128,128]{2,1,0:T(8,128)S(1)}, u32[]{:S(2)}, u32[]{:S(2)}) collective-permute-start(f32[4,128,128]{2,1,0:T(8,128)S(1)} %shard_map.73.refs_0_), channel_id=1, source_target_pairs={{0,1},{1,5},{2,3},{3,7},{4,0},{5,4},{6,2},{7,6},{8,9},{9,13},{10,1... | collective-permute-start | bytes 786440 | tf_op jit(solution)/shard_map/ppermute | solution.py:285
  21.3 9.2 %collective-permute-start.7 = (f32[4,128,128]{2,1,0:T(8,128)S(1)}, f32[4,128,128]{2,1,0:T(8,128)S(1)}, u32[]{:S(2)}, u32[]{:S(2)}) collective-permute-start(f32[4,128,128]{2,1,0:T(8,128)S(1)} %shard_map.74.refs_2_.refs_0_), channel_id=1, source_target_pairs={{0,1},{1,5},{2,3},{3,7},{4,0},{5,4},{6,2},{7,6},{8,9},{9,13},{10,1... | collective-permute-start | bytes 786440 | tf_op jit(solution)/shard_map/ppermute | solution.py:285
  22.7 8.2 %collective-permute-start.6 = (f32[4,128,128]{2,1,0:T(8,128)S(1)}, f32[4,128,128]{2,1,0:T(8,128)S(1)}, u32[]{:S(2)}, u32[]{:S(2)}) collective-permute-start(f32[4,128,128]{2,1,0:T(8,128)S(1)} %get-tuple-element.53), channel_id=1, source_target_pairs={{0,1},{1,4},{2,3},{3,6},{4,5},{5,13},{6,7},{7,15},{8,0},{9,8},{10,... | collective-permute-start | bytes 786440 | tf_op jit(solution)/shard_map/ppermute | solution.py:285
  22.8 8.1 %collective-permute-start.5 = (f32[4,128,128]{2,1,0:T(8,128)S(1)}, f32[4,128,128]{2,1,0:T(8,128)S(1)}, u32[]{:S(2)}, u32[]{:S(2)}) collective-permute-start(f32[4,128,128]{2,1,0:T(8,128)S(1)} %get-tuple-element.53), channel_id=1, source_target_pairs={{0,1},{1,0},{2,3},{3,2},{4,5},{5,9},{6,7},{7,11},{8,4},{9,8},{10,6... | collective-permute-start | bytes 786440 | tf_op jit(solution)/shard_map/ppermute | solution.py:285
  30.6 7.9 %collective-permute-start.9 = (f32[4,128,128]{2,1,0:T(8,128)S(1)}, f32[4,128,128]{2,1,0:T(8,128)S(1)}, u32[]{:S(2)}, u32[]{:S(2)}) collective-permute-start(f32[4,128,128]{2,1,0:T(8,128)S(1)} %get-tuple-element.55.refs_5_), channel_id=1, source_target_pairs={{0,1},{1,4},{2,3},{3,6},{4,5},{5,13},{6,7},{7,15},{8,0},{9,8},{10,... | collective-permute-start | bytes 786440 | tf_op jit(solution)/shard_map/ppermute | solution.py:285
  30.6 7.8 %collective-permute-start.8 = (f32[4,128,128]{2,1,0:T(8,128)S(1)}, f32[4,128,128]{2,1,0:T(8,128)S(1)}, u32[]{:S(2)}, u32[]{:S(2)}) collective-permute-start(f32[4,128,128]{2,1,0:T(8,128)S(1)} %get-tuple-element.55.refs_5_), channel_id=1, source_target_pairs={{0,1},{1,0},{2,3},{3,2},{4,5},{5,9},{6,7},{7,11},{8,4},{9,8},{10,6... | collective-permute-start | bytes 786440 | tf_op jit(solution)/shard_map/ppermute | solution.py:285
  31.0 8.8 %collective-permute-start.11 = (f32[4,128,128]{2,1,0:T(8,128)S(1)}, f32[4,128,128]{2,1,0:T(8,128)S(1)}, u32[]{:S(2)}, u32[]{:S(2)}) collective-permute-start(f32[4,128,128]{2,1,0:T(8,128)S(1)} %get-tuple-element.56.refs_0_.refs_3_), channel_id=1, source_target_pairs={{0,2},{1,3},{2,0},{3,1},{4,6},{5,7},{6,4},{7,5},{8,10},{9,11},{10,... | collective-permute-start | bytes 786440 | tf_op jit(solution)/shard_map/ppermute | solution.py:363
  35.4 6.3 %collective-permute-start.12 = (f32[4,128,128]{2,1,0:T(8,128)S(1)}, f32[4,128,128]{2,1,0:T(8,128)S(1)}, u32[]{:S(2)}, u32[]{:S(2)}) collective-permute-start(f32[4,128,128]{2,1,0:T(8,128)S(1)} %get-tuple-element.68.refs_8_), channel_id=1, source_target_pairs={{0,1},{1,0},{2,3},{3,2},{4,5},{5,4},{6,7},{7,6},{8,9},{9,8},{10,11... | collective-permute-start | bytes 786440 | tf_op jit(solution)/shard_map/ppermute | solution.py:364
  39.8 2.0 %collective-permute-start.13 = (f32[4,128,128]{2,1,0:T(8,128)S(1)}, f32[4,128,128]{2,1,0:T(8,128)S(1)}, u32[]{:S(2)}, u32[]{:S(2)}) collective-permute-start(f32[4,128,128]{2,1,0:T(8,128)S(1)} %collective-permute-done.11.refs_9_), channel_id=1, source_target_pairs={{0,1},{1,0},{2,3},{3,2},{4,5},{5,4},{6,7},{7,6},{8,9},{9,8},{10,11... | collective-permute-start | bytes 786440 | tf_op jit(solution)/shard_map/ppermute | solution.py:371
  39.8 8.7 %collective-permute-start.10 = (f32[4,128,128]{2,1,0:T(8,128)S(1)}, f32[4,128,128]{2,1,0:T(8,128)S(1)}, u32[]{:S(2)}, u32[]{:S(2)}) collective-permute-start(f32[4,128,128]{2,1,0:T(8,128)S(1)} %get-tuple-element.65), channel_id=1, source_target_pairs={{0,2},{1,3},{2,0},{3,1},{4,6},{5,7},{6,4},{7,5},{8,10},{9,11},{10,... | collective-permute-start | bytes 786440 | tf_op jit(solution)/shard_map/ppermute | solution.py:363
  41.5 7.0 %collective-permute-start.14 = (f32[4,128,128]{2,1,0:T(8,128)S(1)}, f32[4,128,128]{2,1,0:T(8,128)S(1)}, u32[]{:S(2)}, u32[]{:S(2)}) collective-permute-start(f32[4,128,128]{2,1,0:T(8,128)S(1)} %get-tuple-element.64.refs_8_), channel_id=1, source_target_pairs={{0,1},{1,0},{2,3},{3,2},{4,5},{5,4},{6,7},{7,6},{8,9},{9,8},{10,11... | collective-permute-start | bytes 786440 | tf_op jit(solution)/shard_map/ppermute | solution.py:364
  48.5 1.5 %collective-permute-start.15 = (f32[4,128,128]{2,1,0:T(8,128)S(1)}, f32[4,128,128]{2,1,0:T(8,128)S(1)}, u32[]{:S(2)}, u32[]{:S(2)}) collective-permute-start(f32[4,128,128]{2,1,0:T(8,128)S(1)} %collective-permute-done.10.refs_9_), channel_id=1, source_target_pairs={{0,1},{1,0},{2,3},{3,2},{4,5},{5,4},{6,7},{7,6},{8,9},{9,8},{10,11... | collective-permute-start | bytes 786440 | tf_op jit(solution)/shard_map/ppermute | solution.py:371

commit v4 on v3

--- a/solution.py
+++ b/solution.py
@@ -18,9 +18,6 @@
     ((1, 0), ("back", 0), ("scan", 1)),
     ((1, 1), ("back", 0), ("scan", 1)),
 )
-RADIX = 2
-TREE = True
-PIECE = 4
 F32 = jnp.float32
 BF16 = jnp.bfloat16
 VMEM_LIMIT = 24 * 1024 * 1024
@@ -188,75 +185,103 @@
     )(*values, *after)
 
 
-def within_kernel(heads, scale, q_ref, k_ref, v_ref, g_ref, *refs):
+def within_kernel(first, heads, scale, q_ref, k_ref, v_ref, g_ref, *refs):
     dq_ref, dk_ref, dv_ref = refs[-3:]
     rows = q_ref.shape[0]
-    at = lax.broadcasted_iota(jnp.int32, (rows, rows), 0)
-    upto = lax.broadcasted_iota(jnp.int32, (rows, rows), 1) <= at
+    cut = 256 if rows > 256 else rows
+
+    def causal(a, b, low):
+        at = low + lax.broadcasted_iota(jnp.int32, (a.shape[0], b.shape[0]), 0)
+        upto = lax.broadcasted_iota(jnp.int32, (a.shape[0], b.shape[0]), 1) <= at
+        return jnp.where(upto, dot(a, b, ((1,), (1,))) * scale, 0.0).astype(BF16)
+
     for h in range(heads):
         cols = slice(h * HD, (h + 1) * HD)
-        q, k, v, g = q_ref[:, cols], k_ref[:, cols], v_ref[:, cols], g_ref[:, cols]
-        weights = jnp.where(upto, dot(q, k, ((1,), (1,))) * scale, 0.0).astype(BF16)
-        scores = jnp.where(upto, dot(g, v, ((1,), (1,))) * scale, 0.0).astype(BF16)
-        dq_ref[:, cols] = dot(scores, k, ((1,), (0,))).astype(BF16)
-        dk_ref[:, cols] = dot(scores, q, ((0,), (0,))).astype(BF16)
-        dv_ref[:, cols] = dot(weights, g, ((0,), (0,))).astype(BF16)
-
-
-def within(arrays, first, size, start, heads, scale, held, after):
+        whole = slice((first + h) * HD, (first + h + 1) * HD)
+        q, k, v, g = q_ref[:, whole], k_ref[:, whole], v_ref[:, whole], g_ref[:, whole]
+        weights = causal(q[:cut], k[:cut], 0)
+        scores = causal(g[:cut], v[:cut], 0)
+        dq_ref[:cut, cols] = dot(scores, k[:cut], ((1,), (0,))).astype(BF16)
+        dk = dot(scores, q[:cut], ((0,), (0,)))
+        dv = dot(weights, g[:cut], ((0,), (0,)))
+        if cut < rows:
+            weights = causal(q[cut:], k, cut)
+            scores = causal(g[cut:], v, cut)
+            dq_ref[cut:, cols] = dot(scores, k, ((1,), (0,))).astype(BF16)
+            low = dot(scores, q[cut:], ((0,), (0,)))
+            dk, dk_ref[cut:, cols] = dk + low[:cut], low[cut:].astype(BF16)
+            low = dot(weights, g[cut:], ((0,), (0,)))
+            dv, dv_ref[cut:, cols] = dv + low[:cut], low[cut:].astype(BF16)
+        dk_ref[:cut, cols] = dk.astype(BF16)
+        dv_ref[:cut, cols] = dv.astype(BF16)
+
+
+def within(arrays, first, heads, scale, after):
     rows = arrays[0].shape[0]
-    per = min(heads, 2)
-    block = pl.BlockSpec((rows, per * HD), lambda i: (0, (first + start) // per + i))
-    out = pl.BlockSpec((rows, per * HD), lambda i: (0, start // per + i))
-    return pl.pallas_call(
-        functools.partial(within_kernel, per, scale),
-        grid=(heads // per,),
-        out_shape=[jax.ShapeDtypeStruct((rows, size * HD), BF16)] * 3,
-        in_specs=[block] * 4 + [ANY] * len((*held, *after)),
-        out_specs=[out] * 3,
-        input_output_aliases={4 + j: j for j in range(len(held))},
+    return pl.pallas_call(
+        functools.partial(within_kernel, first, heads, scale),
+        out_shape=[jax.ShapeDtypeStruct((rows, heads * HD), BF16)] * 3,
+        in_specs=[VMEM] * 4 + [ANY] * len(after),
+        out_specs=[VMEM] * 3,
         compiler_params=pltpu.CompilerParams(vmem_limit_bytes=VMEM_LIMIT),
         cost_estimate=cost(heads * rows * HD, heads * rows * HD),
-    )(*arrays, *held, *after)
-
-
-def final_kernel(per, half, scale, *refs):
-    k_ref, v_ref, g_ref, pq_ref, pk_ref, pv_ref = refs[:6]
-    low_ref, high_ref, kept_ref, swapped_ref, gkept_ref, gswapped_ref = refs[6:12]
-    dq_ref, dk_ref, dv_ref = refs[-3:]
+    )(*arrays, *after)
+
+
+def diagonal(blocks):
+    count = len(blocks)
+    rows = [jnp.concatenate([b if j == i else jnp.zeros_like(b) for j in range(count)], axis=1) for i, b in enumerate(blocks)]
+    return jnp.concatenate(rows, axis=0)
+
+
+def final_kernel(first, half, scale, *refs):
+    k_ref, v_ref, g_ref, other_ref, kept_ref, swapped_ref, gkept_ref, gswapped_ref = refs[:8]
+    parts = refs[8:]
+    piece = min(PIECE, 2 * half)
+    buffers, sem, outs = refs[-4:-1], refs[-1], refs[-7:-4]
     later, second = place()
-    upper = pl.program_id(0) >= half // per
-    own = upper == second
-    for h in range(per):
-        cols = slice(h * HD, (h + 1) * HD)
-        here = jnp.where(own, kept_ref[h] + low_ref[h], swapped_ref[h] + high_ref[h])
-        given = jnp.where(own, gswapped_ref[h], gkept_ref[h])
-        kv = jnp.where(later, here, given).astype(BF16)
-        qg = jnp.where(later, given, here).astype(BF16)
-        dq_ref[:, cols] = (pq_ref[:, cols].astype(F32) + scale * dot(g_ref[:, cols], kv, ((1,), (1,)))).astype(BF16)
-        dk_ref[:, cols] = (pk_ref[:, cols].astype(F32) + scale * dot(v_ref[:, cols], qg, ((1,), (1,)))).astype(BF16)
-        dv_ref[:, cols] = (pv_ref[:, cols].astype(F32) + scale * dot(k_ref[:, cols], qg, ((1,), (0,)))).astype(BF16)
+    per = 2 if half % 2 == 0 else 1
+    copies = []
+    for n in range(2 * half // per):
+        upper = n * per >= half
+        own = second if upper else jnp.logical_not(second)
+        kv, qg = [], []
+        for h in range(per):
+            at = n * per % half + h
+            here = jnp.where(own, kept_ref[at] + other_ref[at], swapped_ref[at] + other_ref[half + at])
+            given = jnp.where(own, gswapped_ref[at], gkept_ref[at])
+            kv.append(jnp.where(later, here, given).astype(BF16))
+            qg.append(jnp.where(later, given, here).astype(BF16))
+        kv, qg = diagonal(kv), diagonal(qg)
+        cols = slice(n * per * HD, (n + 1) * per * HD)
+        whole = slice((first + n * per) * HD, (first + (n + 1) * per) * HD)
+        terms = (
+            dot(g_ref[:, whole], kv, ((1,), (1,))),
+            dot(v_ref[:, whole], qg, ((1,), (1,))),
+            dot(k_ref[:, whole], qg, ((1,), (0,))),
+        )
+        held = slice(n * per % piece * HD, (n * per % piece + per) * HD)
+        for j, term in enumerate(terms):
+            part = parts[n * per // piece * 3 + j][:, held]
+            buffers[j][:, cols] = (part.astype(F32) + scale * term).astype(BF16)
+            copies.append(pltpu.make_async_copy(buffers[j].at[:, cols], outs[j].at[:, whole], sem.at[n, j]))
+            copies[-1].start()
+    for copy in copies:
+        copy.wait()
 
 
 def final(k, v, g, partials, other, states, first, size, scale, held):
     rows, width = k.shape
-    half = size // 2
-    per = min(half, 2)
-    steps = half // per
-    block = pl.BlockSpec((rows, per * HD), lambda i: (0, first // per + i))
-    chunk = pl.BlockSpec((rows, per * HD), lambda i: (0, i))
-    low = pl.BlockSpec((per, HD, HD), lambda i: (lax.rem(i, steps), 0, 0))
-    high = pl.BlockSpec((per, HD, HD), lambda i: (steps + lax.rem(i, steps), 0, 0))
-    return pl.pallas_call(
-        functools.partial(final_kernel, per, half, scale),
-        grid=(size // per,),
+    return pl.pallas_call(
+        functools.partial(final_kernel, first, size // 2, scale),
         out_shape=[jax.ShapeDtypeStruct((rows, width), BF16)] * 3,
-        in_specs=[block] * 3 + [chunk] * 3 + [low, high] + [low] * 4 + [ANY] * len(held),
-        out_specs=[block] * 3,
-        input_output_aliases={12 + j: j for j in range(len(held))},
+        in_specs=[VMEM] * (8 + len(partials)) + [ANY] * len(held),
+        out_specs=[ANY] * 3,
+        scratch_shapes=[pltpu.VMEM((rows, size * HD), BF16)] * 3 + [pltpu.SemaphoreType.DMA((size, 3))],
+        input_output_aliases={8 + len(partials) + j: j for j in range(len(held))},
         compiler_params=pltpu.CompilerParams(vmem_limit_bytes=VMEM_LIMIT),
         cost_estimate=cost(6 * size * rows * HD * HD, 18 * size * rows * HD),
-    )(k, v, g, *partials, other, other, *states, *held)
+    )(k, v, g, other, *states, *partials, *held)
 
 
 def local(seq, queries, keys, values, out_grad):
@@ -307,15 +332,15 @@
     _, keys, values, out_grad = arrays
     chunks = range(len(sizes))
     made = {}
-    pieces = [()] * len(sizes)
+    pieces = [[] for _ in sizes]
 
     def wait_for(name, chunk):
         found = []
         for (c, p), after, before in PLACES:
             if before == (name, chunk):
-                held = within(arrays, firsts[c], sizes[c], p * PIECE, min(PIECE, sizes[c]), scale, pieces[c], [made[after]])
-                pieces[c] = held
-                found.append(held[0])
+                part = within(arrays, firsts[c] + p * PIECE, min(PIECE, sizes[c]), scale, [made[after]])
+                pieces[c] = [*pieces[c], *part]
+                found.append(part[0])
         return found
 
     for c in chunks:

time: 53.3 us -> 52.8 us (level)
  Pallas kernels: 21.4 us -> 16.7 us
  waiting for transfers between devices: 21.7 us -> 25.6 us
    pallas_call x6, Pallas kernels: 16.7 us -> 12.1 us  [the longest x4 8.19 us: within(): pl.pallas_call(functools.partial(within_kernel, first, heads, scale), out...]
    ppermute x2, waiting for transfers between devices: 4.81 us -> 6.99 us  [local(): swapped = lax.ppermute(made['back', c], 'seq', chip_pairs)]
    ppermute x2, waiting for transfers between devices: 6.09 us -> 7.73 us  [local(): made['partner', c] = lax.ppermute(sent, 'seq', chip_pairs)]
    ppermute x6, starting transfers between devices: 1.29 us -> 2.35 us  [moved(): return lax.ppermute(value, 'seq', sorted(pairs.items()))]
    ppermute x2, starting transfers between devices: 3.55 us -> 2.62 us  [local(): swapped = lax.ppermute(made['back', c], 'seq', chip_pairs)]
  transfers between devices with their start and end apart: 16 -> 16, of which waited for: 8 -> 9; matrix products, arithmetic and copies ran while one was open for 0% -> 0% of each run, Pallas kernels for 29% -> 22%
where the time goes in v4:
time: 52.8 us; the launch traced here: 52.6 us
  waiting for transfers between devices  25.6 us (48%)
  Pallas kernels  16.7 us (32%)
  starting transfers between devices  9.34 us (18%)
  between operations  0.94 us (2%)
    ppermute x6, waiting for transfers between devices, moved(): return lax.ppermute(value, 'seq', sorted(pairs.items()))  8.35 us
    pallas_call x4, Pallas kernels, within(): pl.pallas_call(functools.partial(within_kernel, first, heads, scale), out...  8.19 us
    ppermute x2, waiting for transfers between devices, local(): made['partner', c] = lax.ppermute(sent, 'seq', chip_pairs)  7.73 us
    ppermute x2, waiting for transfers between devices, local(): swapped = lax.ppermute(made['back', c], 'seq', chip_pairs)  6.99 us
    pallas_call x2, Pallas kernels, final(): pl.pallas_call(functools.partial(final_kernel, first, size // 2, scale),...  3.92 us
    ppermute x2, starting transfers between devices, local(): made['partner', c] = lax.ppermute(sent, 'seq', chip_pairs)  3.23 us
    pallas_call x1, Pallas kernels, first_state(): pl.pallas_call(functools.partial(first_kernel, size), out_shape=[jax.Shap...  2.94 us
    ppermute x2, starting transfers between devices, local(): swapped = lax.ppermute(made['back', c], 'seq', chip_pairs)  2.62 us
  transfers between devices with their start and end apart: 16, of which 9 were waited for; matrix products, arithmetic and copies ran while one was open for 0% of the time, Pallas kernels for 22%

profile of v4, /device:TPU:0, one launch (start us, length us, event | category | flops | bytes accessed | tf_op | source)
XLA Modules:
  0.0 52.6 jit_solution(12360011013924542996)
XLA Ops:
  0.6 2.9 %shard_map.67 = (f32[8,128,128]{2,1,0:T(8,128)S(1)}, bf16[384,2048]{1,0:T(8,128)(2,1)S(1)}, bf16[384,2048]{1,0:T(8,128)(2,1)S(1)}, bf16[384,2048]{1,0:T(8,128)(2,1)S(1)}, bf16[384,2048]{1,0:T(8,128)(2,1)S(1)}) custom-call(bf16[384,2048]{1,0:T(8,128)(2,1)} %q_ref.1, bf16[384,2048]{1,0:T(8,128)(2,1)} %k_ref.1, bf16[384,2048]{1,0:T(8,128)(2,1)} %v_ref.1, ...), custom_call_target="tpu_custom_call" | custom-call | tf_op jit(solution)/shard_map/pallas_call | solution.py:98
  3.6 0.5 collective-permute-start.5
  4.1 0.4 shard_map.68
  4.5 0.1 collective-permute-start
  4.7 1.0 %collective-permute-done.5.other_ref.refs_3_ = f32[8,128,128]{2,1,0:T(8,128)S(1)} collective-permute-done((f32[8,128,128]{2,1,0:T(8,128)S(1)}, f32[8,128,128]{2,1,0:T(8,128)S(1)}, u32[]{:S(2)}, u32[]{:S(2)}) %collective-permute-start.5) | collective-permute-done | bytes 524320 | tf_op jit(solution)/shard_map/ppermute | solution.py:348
  5.6 0.4 shard_map.72
  6.1 2.9 %collective-permute-start.6 = (f32[4,128,128]{2,1,0:T(8,128)S(1)}, f32[4,128,128]{2,1,0:T(8,128)S(1)}, u32[]{:S(2)}, u32[]{:S(2)}) collective-permute-start(f32[4,128,128]{2,1,0:T(8,128)S(1)} %get-tuple-element.50), channel_id=1, source_target_pairs={{0,2},{1,3},{2,0},{3,1},{4,6},{5,7},{6,4},{7,5},{8,10},{9,11},{10,... | collective-permute-start | bytes 786440 | tf_op jit(solution)/shard_map/ppermute | solution.py:351
  9.0 0.4 shard_map.69
  9.4 2.0 %shard_map.74 = (bf16[384,512]{1,0:T(8,128)(2,1)S(1)}, bf16[384,512]{1,0:T(8,128)(2,1)S(1)}, bf16[384,512]{1,0:T(8,128)(2,1)S(1)}) custom-call(bf16[384,2048]{1,0:T(8,128)(2,1)S(1)} %get-tuple-element.43.q_ref, bf16[384,2048]{1,0:T(8,128)(2,1)S(1)} %get-tuple-element.40.k_ref.refs_0_, bf16[384,2048]{1,0:T(8,128)(2,1)S(1)} %get-tuple-element.41.v_ref.refs_1_, ...), custom_call_target="tpu_custom_call" | custom-call | tf_op jit(solution)/shard_map/pallas_call | solution.py:221
  11.5 2.0 %shard_map.73 = (bf16[384,512]{1,0:T(8,128)(2,1)S(1)}, bf16[384,512]{1,0:T(8,128)(2,1)S(1)}, bf16[384,512]{1,0:T(8,128)(2,1)S(1)}) custom-call(bf16[384,2048]{1,0:T(8,128)(2,1)S(1)} %get-tuple-element.43.q_ref, bf16[384,2048]{1,0:T(8,128)(2,1)S(1)} %get-tuple-element.40.k_ref.refs_0_, bf16[384,2048]{1,0:T(8,128)(2,1)S(1)} %get-tuple-element.41.v_ref.refs_1_, ...), custom_call_target="tpu_custom_call" | custom-call | tf_op jit(solution)/shard_map/pallas_call | solution.py:221
  13.5 0.3 collective-permute-start.1
  13.9 1.8 %collective-permute-done.6.refs_1_ = f32[4,128,128]{2,1,0:T(8,128)S(1)} collective-permute-done((f32[4,128,128]{2,1,0:T(8,128)S(1)}, f32[4,128,128]{2,1,0:T(8,128)S(1)}, u32[]{:S(2)}, u32[]{:S(2)}) %collective-permute-start.6) | collective-permute-done | bytes 262176 | tf_op jit(solution)/shard_map/ppermute | solution.py:351
  15.7 6.0 %collective-permute-done.1.refs_1_ = f32[4,128,128]{2,1,0:T(8,128)S(1)} collective-permute-done((f32[4,128,128]{2,1,0:T(8,128)S(1)}, f32[4,128,128]{2,1,0:T(8,128)S(1)}, u32[]{:S(2)}, u32[]{:S(2)}) %collective-permute-start.1) | collective-permute-done | bytes 262176 | tf_op jit(solution)/shard_map/ppermute | solution.py:351
  21.8 0.3 collective-permute-done.7.refs_1_
  22.1 0.1 collective-permute-start.9
  22.2 1.8 %collective-permute-start.8 = (f32[4,128,128]{2,1,0:T(8,128)S(1)}, f32[4,128,128]{2,1,0:T(8,128)S(1)}, u32[]{:S(2)}, u32[]{:S(2)}) collective-permute-start(f32[4,128,128]{2,1,0:T(8,128)S(1)} %get-tuple-element.53), channel_id=1, source_target_pairs={{0,1},{1,0},{2,3},{3,2},{4,5},{5,9},{6,7},{7,11},{8,4},{9,8},{10,6... | collective-permute-start | bytes 786440 | tf_op jit(solution)/shard_map/ppermute | solution.py:310
  24.0 6.9 %collective-permute-done.2.refs_1_ = f32[4,128,128]{2,1,0:T(8,128)S(1)} collective-permute-done((f32[4,128,128]{2,1,0:T(8,128)S(1)}, f32[4,128,128]{2,1,0:T(8,128)S(1)}, u32[]{:S(2)}, u32[]{:S(2)}) %collective-permute-start.2) | collective-permute-done | bytes 262176 | tf_op jit(solution)/shard_map/ppermute | solution.py:310
  31.1 0.2 collective-permute-start.3
  31.4 0.1 shard_map.77
  31.5 1.3 %collective-permute-start.11 = (f32[4,128,128]{2,1,0:T(8,128)S(1)}, f32[4,128,128]{2,1,0:T(8,128)S(1)}, u32[]{:S(2)}, u32[]{:S(2)}) collective-permute-start(f32[4,128,128]{2,1,0:T(8,128)S(1)} %get-tuple-element.55.refs_0_), channel_id=1, source_target_pairs={{0,2},{1,3},{2,0},{3,1},{4,6},{5,7},{6,4},{7,5},{8,10},{9,11},{10,... | collective-permute-start | bytes 786440 | tf_op jit(solution)/shard_map/ppermute | solution.py:388
  32.8 2.0 %shard_map.79 = (bf16[384,512]{1,0:T(8,128)(2,1)S(1)}, bf16[384,512]{1,0:T(8,128)(2,1)S(1)}, bf16[384,512]{1,0:T(8,128)(2,1)S(1)}) custom-call(bf16[384,2048]{1,0:T(8,128)(2,1)S(1)} %get-tuple-element.43.q_ref, bf16[384,2048]{1,0:T(8,128)(2,1)S(1)} %get-tuple-element.40.k_ref.refs_0_, bf16[384,2048]{1,0:T(8,128)(2,1)S(1)} %get-tuple-element.41.v_ref.refs_1_, ...), custom_call_target="tpu_custom_call" | custom-call | tf_op jit(solution)/shard_map/pallas_call | solution.py:221
  34.9 2.0 %shard_map.78 = (bf16[384,512]{1,0:T(8,128)(2,1)S(1)}, bf16[384,512]{1,0:T(8,128)(2,1)S(1)}, bf16[384,512]{1,0:T(8,128)(2,1)S(1)}) custom-call(bf16[384,2048]{1,0:T(8,128)(2,1)S(1)} %get-tuple-element.43.q_ref, bf16[384,2048]{1,0:T(8,128)(2,1)S(1)} %get-tuple-element.40.k_ref.refs_0_, bf16[384,2048]{1,0:T(8,128)(2,1)S(1)} %get-tuple-element.41.v_ref.refs_1_, ...), custom_call_target="tpu_custom_call" | custom-call | tf_op jit(solution)/shard_map/pallas_call | solution.py:221
  36.9 0.3 collective-permute-start.12
  37.2 1.1 %collective-permute-done.4.refs_3_ = f32[4,128,128]{2,1,0:T(8,128)S(1)} collective-permute-done((f32[4,128,128]{2,1,0:T(8,128)S(1)}, f32[4,128,128]{2,1,0:T(8,128)S(1)}, u32[]{:S(2)}, u32[]{:S(2)}) %collective-permute-start.4) | collective-permute-done | bytes 262176 | tf_op jit(solution)/shard_map/ppermute | solution.py:310
  38.4 0.1 shard_map.80
  38.5 1.8 %collective-permute-done.11.refs_5_ = f32[4,128,128]{2,1,0:T(8,128)S(1)} collective-permute-done((f32[4,128,128]{2,1,0:T(8,128)S(1)}, f32[4,128,128]{2,1,0:T(8,128)S(1)}, u32[]{:S(2)}, u32[]{:S(2)}) %collective-permute-start.11) | collective-permute-done | bytes 262176 | tf_op jit(solution)/shard_map/ppermute | solution.py:388
  40.2 1.3 %collective-permute-start.10 = (f32[4,128,128]{2,1,0:T(8,128)S(1)}, f32[4,128,128]{2,1,0:T(8,128)S(1)}, u32[]{:S(2)}, u32[]{:S(2)}) collective-permute-start(f32[4,128,128]{2,1,0:T(8,128)S(1)} %get-tuple-element.59), channel_id=1, source_target_pairs={{0,2},{1,3},{2,0},{3,1},{4,6},{5,7},{6,4},{7,5},{8,10},{9,11},{10,... | collective-permute-start | bytes 786440 | tf_op jit(solution)/shard_map/ppermute | solution.py:388
  41.5 0.2 collective-permute-start.14
  41.8 2.0 %shard_map.81 = (bf16[384,2048]{1,0:T(8,128)(2,1)}, bf16[384,2048]{1,0:T(8,128)(2,1)}, bf16[384,2048]{1,0:T(8,128)(2,1)}) custom-call(bf16[384,2048]{1,0:T(8,128)(2,1)S(1)} %get-tuple-element.40.k_ref.refs_0_, bf16[384,2048]{1,0:T(8,128)(2,1)S(1)} %get-tuple-element.41.v_ref.refs_1_, bf16[384,2048]{1,0:T(8,128)(2,1)S(1)} %get-tuple-element.42.g_ref.refs_2_, ...), custom_call_target="tpu_custom_call" | custom-call | tf_op jit(solution)/shard_map/pallas_call | solution.py:275
  43.8 5.2 %collective-permute-done.10.refs_5_ = f32[4,128,128]{2,1,0:T(8,128)S(1)} collective-permute-done((f32[4,128,128]{2,1,0:T(8,128)S(1)}, f32[4,128,128]{2,1,0:T(8,128)S(1)}, u32[]{:S(2)}, u32[]{:S(2)}) %collective-permute-start.10) | collective-permute-done | bytes 262176 | tf_op jit(solution)/shard_map/ppermute | solution.py:388
  49.0 1.5 %collective-permute-done.15.refs_7_ = f32[4,128,128]{2,1,0:T(8,128)S(1)} collective-permute-done((f32[4,128,128]{2,1,0:T(8,128)S(1)}, f32[4,128,128]{2,1,0:T(8,128)S(1)}, u32[]{:S(2)}, u32[]{:S(2)}) %collective-permute-start.15) | collective-permute-done | bytes 262176 | tf_op jit(solution)/shard_map/ppermute | solution.py:396
  50.5 2.0 %shard_map.82 = (bf16[384,2048]{1,0:T(8,128)(2,1)}, bf16[384,2048]{1,0:T(8,128)(2,1)}, bf16[384,2048]{1,0:T(8,128)(2,1)}) custom-call(bf16[384,2048]{1,0:T(8,128)(2,1)S(1)} %get-tuple-element.40.k_ref.refs_0_, bf16[384,2048]{1,0:T(8,128)(2,1)S(1)} %get-tuple-element.41.v_ref.refs_1_, ...), custom_call_target="tpu_custom_call", output_to_operand_aliasing={{0}: (14, {}), {1}: (15, {}), {2}: (16, {})} | custom-call | tf_op jit(solution)/shard_map/pallas_call | solution.py:275
  (16 shorter events, 0.4 us)
Async XLA Ops:
  3.6 2.1 %collective-permute-start.5 = (f32[8,128,128]{2,1,0:T(8,128)S(1)}, f32[8,128,128]{2,1,0:T(8,128)S(1)}, u32[]{:S(2)}, u32[]{:S(2)}) collective-permute-start(f32[8,128,128]{2,1,0:T(8,128)S(1)} %get-tuple-element.48), channel_id=1, source_target_pairs={{0,1},{1,0},{2,3},{3,2},{4,5},{5,4},{6,7},{7,6},{8,9},{9,8},{10,11... | collective-permute-start | bytes 1572872 | tf_op jit(solution)/shard_map/ppermute | solution.py:348
  4.5 4.5 %collective-permute-start = (f32[8,128,128]{2,1,0:T(8,128)S(1)}, f32[8,128,128]{2,1,0:T(8,128)S(1)}, u32[]{:S(2)}, u32[]{:S(2)}) collective-permute-start(f32[8,128,128]{2,1,0:T(8,128)S(1)} %shard_map.68), channel_id=1, source_target_pairs={{0,1},{1,0},{2,3},{3,2},{4,5},{5,4},{6,7},{7,6},{8,9},{9,8},{10,11... | collective-permute-start | bytes 1572872 | tf_op jit(solution)/shard_map/ppermute | solution.py:348
  6.1 9.5 %collective-permute-start.6 = (f32[4,128,128]{2,1,0:T(8,128)S(1)}, f32[4,128,128]{2,1,0:T(8,128)S(1)}, u32[]{:S(2)}, u32[]{:S(2)}) collective-permute-start(f32[4,128,128]{2,1,0:T(8,128)S(1)} %get-tuple-element.50), channel_id=1, source_target_pairs={{0,2},{1,3},{2,0},{3,1},{4,6},{5,7},{6,4},{7,5},{8,10},{9,11},{10,... | collective-permute-start | bytes 786440 | tf_op jit(solution)/shard_map/ppermute | solution.py:351
  13.5 8.1 %collective-permute-start.1 = (f32[4,128,128]{2,1,0:T(8,128)S(1)}, f32[4,128,128]{2,1,0:T(8,128)S(1)}, u32[]{:S(2)}, u32[]{:S(2)}) collective-permute-start(f32[4,128,128]{2,1,0:T(8,128)S(1)} %get-tuple-element.45), channel_id=1, source_target_pairs={{0,2},{1,3},{2,0},{3,1},{4,6},{5,7},{6,4},{7,5},{8,10},{9,11},{10,... | collective-permute-start | bytes 786440 | tf_op jit(solution)/shard_map/ppermute | solution.py:351
  15.6 6.4 %collective-permute-start.7 = (f32[4,128,128]{2,1,0:T(8,128)S(1)}, f32[4,128,128]{2,1,0:T(8,128)S(1)}, u32[]{:S(2)}, u32[]{:S(2)}) collective-permute-start(f32[4,128,128]{2,1,0:T(8,128)S(1)} %shard_map.75.refs_0_), channel_id=1, source_target_pairs={{0,1},{1,5},{2,3},{3,7},{4,0},{5,4},{6,2},{7,6},{8,9},{9,13},{10,1... | collective-permute-start | bytes 786440 | tf_op jit(solution)/shard_map/ppermute | solution.py:310
  21.7 9.2 %collective-permute-start.2 = (f32[4,128,128]{2,1,0:T(8,128)S(1)}, f32[4,128,128]{2,1,0:T(8,128)S(1)}, u32[]{:S(2)}, u32[]{:S(2)}) collective-permute-start(f32[4,128,128]{2,1,0:T(8,128)S(1)} %shard_map.70.refs_0_.refs_2_), channel_id=1, source_target_pairs={{0,1},{1,5},{2,3},{3,7},{4,0},{5,4},{6,2},{7,6},{8,9},{9,13},{10,1... | collective-permute-start | bytes 786440 | tf_op jit(solution)/shard_map/ppermute | solution.py:310
  22.1 9.2 %collective-permute-start.9 = (f32[4,128,128]{2,1,0:T(8,128)S(1)}, f32[4,128,128]{2,1,0:T(8,128)S(1)}, u32[]{:S(2)}, u32[]{:S(2)}) collective-permute-start(f32[4,128,128]{2,1,0:T(8,128)S(1)} %get-tuple-element.53), channel_id=1, source_target_pairs={{0,1},{1,4},{2,3},{3,6},{4,5},{5,13},{6,7},{7,15},{8,0},{9,8},{10,... | collective-permute-start | bytes 786440 | tf_op jit(solution)/shard_map/ppermute | solution.py:310
  22.2 9.2 %collective-permute-start.8 = (f32[4,128,128]{2,1,0:T(8,128)S(1)}, f32[4,128,128]{2,1,0:T(8,128)S(1)}, u32[]{:S(2)}, u32[]{:S(2)}) collective-permute-start(f32[4,128,128]{2,1,0:T(8,128)S(1)} %get-tuple-element.53), channel_id=1, source_target_pairs={{0,1},{1,0},{2,3},{3,2},{4,5},{5,9},{6,7},{7,11},{8,4},{9,8},{10,6... | collective-permute-start | bytes 786440 | tf_op jit(solution)/shard_map/ppermute | solution.py:310
  31.0 7.3 %collective-permute-start.4 = (f32[4,128,128]{2,1,0:T(8,128)S(1)}, f32[4,128,128]{2,1,0:T(8,128)S(1)}, u32[]{:S(2)}, u32[]{:S(2)}) collective-permute-start(f32[4,128,128]{2,1,0:T(8,128)S(1)} %get-tuple-element.46.refs_5_), channel_id=1, source_target_pairs={{0,1},{1,4},{2,3},{3,6},{4,5},{5,13},{6,7},{7,15},{8,0},{9,8},{10,... | collective-permute-start | bytes 786440 | tf_op jit(solution)/shard_map/ppermute | solution.py:310
  31.1 7.3 %collective-permute-start.3 = (f32[4,128,128]{2,1,0:T(8,128)S(1)}, f32[4,128,128]{2,1,0:T(8,128)S(1)}, u32[]{:S(2)}, u32[]{:S(2)}) collective-permute-start(f32[4,128,128]{2,1,0:T(8,128)S(1)} %get-tuple-element.46.refs_5_), channel_id=1, source_target_pairs={{0,1},{1,0},{2,3},{3,2},{4,5},{5,9},{6,7},{7,11},{8,4},{9,8},{10,6... | collective-permute-start | bytes 786440 | tf_op jit(solution)/shard_map/ppermute | solution.py:310
  31.5 8.8 %collective-permute-start.11 = (f32[4,128,128]{2,1,0:T(8,128)S(1)}, f32[4,128,128]{2,1,0:T(8,128)S(1)}, u32[]{:S(2)}, u32[]{:S(2)}) collective-permute-start(f32[4,128,128]{2,1,0:T(8,128)S(1)} %get-tuple-element.55.refs_0_), channel_id=1, source_target_pairs={{0,2},{1,3},{2,0},{3,1},{4,6},{5,7},{6,4},{7,5},{8,10},{9,11},{10,... | collective-permute-start | bytes 786440 | tf_op jit(solution)/shard_map/ppermute | solution.py:388
  36.9 4.8 %collective-permute-start.12 = (f32[4,128,128]{2,1,0:T(8,128)S(1)}, f32[4,128,128]{2,1,0:T(8,128)S(1)}, u32[]{:S(2)}, u32[]{:S(2)}) collective-permute-start(f32[4,128,128]{2,1,0:T(8,128)S(1)} %get-tuple-element.60.refs_4_), channel_id=1, source_target_pairs={{0,1},{1,0},{2,3},{3,2},{4,5},{5,4},{6,7},{7,6},{8,9},{9,8},{10,11... | collective-permute-start | bytes 786440 | tf_op jit(solution)/shard_map/ppermute | solution.py:389
  40.2 1.5 %collective-permute-start.13 = (f32[4,128,128]{2,1,0:T(8,128)S(1)}, f32[4,128,128]{2,1,0:T(8,128)S(1)}, u32[]{:S(2)}, u32[]{:S(2)}) collective-permute-start(f32[4,128,128]{2,1,0:T(8,128)S(1)} %collective-permute-done.11.refs_5_), channel_id=1, source_target_pairs={{0,1},{1,0},{2,3},{3,2},{4,5},{5,4},{6,7},{7,6},{8,9},{9,8},{10,11... | collective-permute-start | bytes 786440 | tf_op jit(solution)/shard_map/ppermute | solution.py:396
  40.2 8.7 %collective-permute-start.10 = (f32[4,128,128]{2,1,0:T(8,128)S(1)}, f32[4,128,128]{2,1,0:T(8,128)S(1)}, u32[]{:S(2)}, u32[]{:S(2)}) collective-permute-start(f32[4,128,128]{2,1,0:T(8,128)S(1)} %get-tuple-element.59), channel_id=1, source_target_pairs={{0,2},{1,3},{2,0},{3,1},{4,6},{5,7},{6,4},{7,5},{8,10},{9,11},{10,... | collective-permute-start | bytes 786440 | tf_op jit(solution)/shard_map/ppermute | solution.py:388
  41.5 7.4 %collective-permute-start.14 = (f32[4,128,128]{2,1,0:T(8,128)S(1)}, f32[4,128,128]{2,1,0:T(8,128)S(1)}, u32[]{:S(2)}, u32[]{:S(2)}) collective-permute-start(f32[4,128,128]{2,1,0:T(8,128)S(1)} %get-tuple-element.58.refs_4_), channel_id=1, source_target_pairs={{0,1},{1,0},{2,3},{3,2},{4,5},{5,4},{6,7},{7,6},{8,9},{9,8},{10,11... | collective-permute-start | bytes 786440 | tf_op jit(solution)/shard_map/ppermute | solution.py:389
  49.0 1.5 %collective-permute-start.15 = (f32[4,128,128]{2,1,0:T(8,128)S(1)}, f32[4,128,128]{2,1,0:T(8,128)S(1)}, u32[]{:S(2)}, u32[]{:S(2)}) collective-permute-start(f32[4,128,128]{2,1,0:T(8,128)S(1)} %collective-permute-done.10.refs_5_), channel_id=1, source_target_pairs={{0,1},{1,0},{2,3},{3,2},{4,5},{5,4},{6,7},{7,6},{8,9},{9,8},{10,11... | collective-permute-start | bytes 786440 | tf_op jit(solution)/shard_map/ppermute | solution.py:396

commit v5 on v4

--- a/solution.py
+++ b/solution.py
@@ -388,12 +388,17 @@
         swapped = lax.ppermute(made["back", c], "seq", chip_pairs)
         done.append((made["other", c], kept_upto, swapped, lax.ppermute(kept_upto, "seq", core_pairs)))
 
-    out = ()
+    out, others = (), []
     for chunk, (first, size) in enumerate(zip(firsts, sizes)):
         other, kept_upto, swapped, given_kept = done[chunk]
-        ahead = [made["back", chunk + 1]] if chunk + 1 < len(sizes) else []
-        swapped, out, ahead = lax.optimization_barrier((swapped, out, ahead))
+        if chunk == len(sizes) - 1:
+            swapped, given = lax.optimization_barrier((swapped, [d[3] for d in done] + others))
+            done = [(*d[:3], g) for d, g in zip(done, given)]
+            given_kept = done[chunk][3]
         given_swapped = lax.ppermute(swapped, "seq", core_pairs)
+        others.append(given_swapped)
+        ahead = [done[chunk + 1][2]] if chunk + 1 < len(sizes) else []
+        given_swapped, ahead = lax.optimization_barrier((given_swapped, ahead))
         states = (kept_upto, swapped, given_kept, given_swapped)
         out = final(keys, values, out_grad, pieces[chunk], other, states, first, size, scale, out)
     return tuple(out)

time: 52.8 us -> 50.6 us (0.958)
  waiting for transfers between devices: 25.6 us -> 22.8 us
    ppermute x2, waiting for transfers between devices: 1.55 us -> 0.01 us  [local(): given_swapped = lax.ppermute(swapped, 'seq', core_pairs)]
    ppermute x2, waiting for transfers between devices: 6.99 us -> 5.6 us  [local(): swapped = lax.ppermute(made['back', c], 'seq', chip_pairs)]
    ppermute x6, starting transfers between devices: 2.35 us -> 1.29 us  [moved(): return lax.ppermute(value, 'seq', sorted(pairs.items()))]
    ppermute x2, starting transfers between devices: 2.62 us -> 3.61 us  [local(): swapped = lax.ppermute(made['back', c], 'seq', chip_pairs)]
    ppermute x6, waiting for transfers between devices: 8.35 us -> 8.95 us  [moved(): return lax.ppermute(value, 'seq', sorted(pairs.items()))]
  transfers between devices with their start and end apart: 16 -> 16, of which waited for: 9 -> 7; matrix products, arithmetic and copies ran while one was open for 0% -> 0% of each run, Pallas kernels for 22% -> 24%
where the time goes in v5:
time: 50.6 us; the launch traced here: 50.1 us
  waiting for transfers between devices  22.8 us (45%)
  Pallas kernels  16.8 us (33%)
  starting transfers between devices  9.54 us (19%)
  between operations  0.96 us (2%)
    ppermute x6, waiting for transfers between devices, moved(): return lax.ppermute(value, 'seq', sorted(pairs.items()))  8.95 us
    pallas_call x4, Pallas kernels, within(): pl.pallas_call(functools.partial(within_kernel, first, heads, scale), out...  8.19 us
    ppermute x2, waiting for transfers between devices, local(): made['partner', c] = lax.ppermute(sent, 'seq', chip_pairs)  7.26 us
    ppermute x2, waiting for transfers between devices, local(): swapped = lax.ppermute(made['back', c], 'seq', chip_pairs)  5.6 us
    pallas_call x2, Pallas kernels, final(): pl.pallas_call(functools.partial(final_kernel, first, size // 2, scale),...  3.95 us
    ppermute x2, starting transfers between devices, local(): swapped = lax.ppermute(made['back', c], 'seq', chip_pairs)  3.61 us
    ppermute x2, starting transfers between devices, local(): made['partner', c] = lax.ppermute(sent, 'seq', chip_pairs)  3.23 us
    pallas_call x1, Pallas kernels, first_state(): pl.pallas_call(functools.partial(first_kernel, size), out_shape=[jax.Shap...  2.94 us
  transfers between devices with their start and end apart: 16, of which 7 were waited for; matrix products, arithmetic and copies ran while one was open for 0% of the time, Pallas kernels for 24%

profile of v5, /device:TPU:0, one launch (start us, length us, event | category | flops | bytes accessed | tf_op | source)
XLA Modules:
  0.0 50.1 jit_solution(2790391684598425431)
XLA Ops:
  0.6 2.9 %shard_map.67 = (f32[8,128,128]{2,1,0:T(8,128)S(1)}, bf16[384,2048]{1,0:T(8,128)(2,1)S(1)}, bf16[384,2048]{1,0:T(8,128)(2,1)S(1)}, bf16[384,2048]{1,0:T(8,128)(2,1)S(1)}, bf16[384,2048]{1,0:T(8,128)(2,1)S(1)}) custom-call(bf16[384,2048]{1,0:T(8,128)(2,1)} %q_ref.1, bf16[384,2048]{1,0:T(8,128)(2,1)} %k_ref.1, bf16[384,2048]{1,0:T(8,128)(2,1)} %v_ref.1, ...), custom_call_target="tpu_custom_call" | custom-call | tf_op jit(solution)/shard_map/pallas_call | solution.py:98
  3.6 0.5 %collective-permute-start.5 = (f32[8,128,128]{2,1,0:T(8,128)S(1)}, f32[8,128,128]{2,1,0:T(8,128)S(1)}, u32[]{:S(2)}, u32[]{:S(2)}) collective-permute-start(f32[8,128,128]{2,1,0:T(8,128)S(1)} %get-tuple-element.46), channel_id=1, source_target_pairs={{0,1},{1,0},{2,3},{3,2},{4,5},{5,4},{6,7},{7,6},{8,9},{9,8},{10,11... | collective-permute-start | bytes 1572872 | tf_op jit(solution)/shard_map/ppermute | solution.py:348
  4.1 0.4 shard_map.68
  4.5 0.1 collective-permute-start
  4.7 1.0 %collective-permute-done.5.other_ref.refs_3_ = f32[8,128,128]{2,1,0:T(8,128)S(1)} collective-permute-done((f32[8,128,128]{2,1,0:T(8,128)S(1)}, f32[8,128,128]{2,1,0:T(8,128)S(1)}, u32[]{:S(2)}, u32[]{:S(2)}) %collective-permute-start.5) | collective-permute-done | bytes 524320 | tf_op jit(solution)/shard_map/ppermute | solution.py:348
  5.6 0.4 shard_map.72
  6.1 2.9 %collective-permute-start.6 = (f32[4,128,128]{2,1,0:T(8,128)S(1)}, f32[4,128,128]{2,1,0:T(8,128)S(1)}, u32[]{:S(2)}, u32[]{:S(2)}) collective-permute-start(f32[4,128,128]{2,1,0:T(8,128)S(1)} %get-tuple-element.48), channel_id=1, source_target_pairs={{0,2},{1,3},{2,0},{3,1},{4,6},{5,7},{6,4},{7,5},{8,10},{9,11},{10,... | collective-permute-start | bytes 786440 | tf_op jit(solution)/shard_map/ppermute | solution.py:351
  9.0 0.4 shard_map.69
  9.4 0.3 collective-permute-start.1
  9.8 2.0 %shard_map.74 = (bf16[384,512]{1,0:T(8,128)(2,1)S(1)}, bf16[384,512]{1,0:T(8,128)(2,1)S(1)}, bf16[384,512]{1,0:T(8,128)(2,1)S(1)}) custom-call(bf16[384,2048]{1,0:T(8,128)(2,1)S(1)} %get-tuple-element.41.q_ref, bf16[384,2048]{1,0:T(8,128)(2,1)S(1)} %get-tuple-element.38.k_ref.refs_0_, bf16[384,2048]{1,0:T(8,128)(2,1)S(1)} %get-tuple-element.39.v_ref.refs_1_, ...), custom_call_target="tpu_custom_call" | custom-call | tf_op jit(solution)/shard_map/pallas_call | solution.py:221
  11.8 2.0 %shard_map.73 = (bf16[384,512]{1,0:T(8,128)(2,1)S(1)}, bf16[384,512]{1,0:T(8,128)(2,1)S(1)}, bf16[384,512]{1,0:T(8,128)(2,1)S(1)}) custom-call(bf16[384,2048]{1,0:T(8,128)(2,1)S(1)} %get-tuple-element.41.q_ref, bf16[384,2048]{1,0:T(8,128)(2,1)S(1)} %get-tuple-element.38.k_ref.refs_0_, bf16[384,2048]{1,0:T(8,128)(2,1)S(1)} %get-tuple-element.39.v_ref.refs_1_, ...), custom_call_target="tpu_custom_call" | custom-call | tf_op jit(solution)/shard_map/pallas_call | solution.py:221
  13.9 2.2 %collective-permute-done.6.refs_1_ = f32[4,128,128]{2,1,0:T(8,128)S(1)} collective-permute-done((f32[4,128,128]{2,1,0:T(8,128)S(1)}, f32[4,128,128]{2,1,0:T(8,128)S(1)}, u32[]{:S(2)}, u32[]{:S(2)}) %collective-permute-start.6) | collective-permute-done | bytes 262176 | tf_op jit(solution)/shard_map/ppermute | solution.py:351
  16.1 0.1 collective-permute-start.7
  16.2 5.0 %collective-permute-done.1.refs_1_ = f32[4,128,128]{2,1,0:T(8,128)S(1)} collective-permute-done((f32[4,128,128]{2,1,0:T(8,128)S(1)}, f32[4,128,128]{2,1,0:T(8,128)S(1)}, u32[]{:S(2)}, u32[]{:S(2)}) %collective-permute-start.1) | collective-permute-done | bytes 262176 | tf_op jit(solution)/shard_map/ppermute | solution.py:351
  21.3 0.1 collective-permute-start.2
  21.3 1.3 %collective-permute-done.7.refs_1_ = f32[4,128,128]{2,1,0:T(8,128)S(1)} collective-permute-done((f32[4,128,128]{2,1,0:T(8,128)S(1)}, f32[4,128,128]{2,1,0:T(8,128)S(1)}, u32[]{:S(2)}, u32[]{:S(2)}) %collective-permute-start.7) | collective-permute-done | bytes 262176 | tf_op jit(solution)/shard_map/ppermute | solution.py:310
  22.7 0.1 collective-permute-start.9
  22.8 0.8 %collective-permute-start.8 = (f32[4,128,128]{2,1,0:T(8,128)S(1)}, f32[4,128,128]{2,1,0:T(8,128)S(1)}, u32[]{:S(2)}, u32[]{:S(2)}) collective-permute-start(f32[4,128,128]{2,1,0:T(8,128)S(1)} %get-tuple-element.51), channel_id=1, source_target_pairs={{0,1},{1,0},{2,3},{3,2},{4,5},{5,9},{6,7},{7,11},{8,4},{9,8},{10,6... | collective-permute-start | bytes 786440 | tf_op jit(solution)/shard_map/ppermute | solution.py:310
  23.6 6.9 %collective-permute-done.2.refs_1_ = f32[4,128,128]{2,1,0:T(8,128)S(1)} collective-permute-done((f32[4,128,128]{2,1,0:T(8,128)S(1)}, f32[4,128,128]{2,1,0:T(8,128)S(1)}, u32[]{:S(2)}, u32[]{:S(2)}) %collective-permute-start.2) | collective-permute-done | bytes 262176 | tf_op jit(solution)/shard_map/ppermute | solution.py:310
  30.6 0.2 collective-permute-start.3
  30.9 0.1 shard_map.77
  31.0 1.8 %collective-permute-start.13 = (f32[4,128,128]{2,1,0:T(8,128)S(1)}, f32[4,128,128]{2,1,0:T(8,128)S(1)}, u32[]{:S(2)}, u32[]{:S(2)}) collective-permute-start(f32[4,128,128]{2,1,0:T(8,128)S(1)} %get-tuple-element.53.refs_0_), channel_id=1, source_target_pairs={{0,2},{1,3},{2,0},{3,1},{4,6},{5,7},{6,4},{7,5},{8,10},{9,11},{10,... | collective-permute-start | bytes 786440 | tf_op jit(solution)/shard_map/ppermute | solution.py:388
  32.8 2.0 %shard_map.79 = (bf16[384,512]{1,0:T(8,128)(2,1)S(1)}, bf16[384,512]{1,0:T(8,128)(2,1)S(1)}, bf16[384,512]{1,0:T(8,128)(2,1)S(1)}) custom-call(bf16[384,2048]{1,0:T(8,128)(2,1)S(1)} %get-tuple-element.41.q_ref, bf16[384,2048]{1,0:T(8,128)(2,1)S(1)} %get-tuple-element.38.k_ref.refs_0_, bf16[384,2048]{1,0:T(8,128)(2,1)S(1)} %get-tuple-element.39.v_ref.refs_1_, ...), custom_call_target="tpu_custom_call" | custom-call | tf_op jit(solution)/shard_map/pallas_call | solution.py:221
  34.9 2.0 %shard_map.78 = (bf16[384,512]{1,0:T(8,128)(2,1)S(1)}, bf16[384,512]{1,0:T(8,128)(2,1)S(1)}, bf16[384,512]{1,0:T(8,128)(2,1)S(1)}) custom-call(bf16[384,2048]{1,0:T(8,128)(2,1)S(1)} %get-tuple-element.41.q_ref, bf16[384,2048]{1,0:T(8,128)(2,1)S(1)} %get-tuple-element.38.k_ref.refs_0_, bf16[384,2048]{1,0:T(8,128)(2,1)S(1)} %get-tuple-element.39.v_ref.refs_1_, ...), custom_call_target="tpu_custom_call" | custom-call | tf_op jit(solution)/shard_map/pallas_call | solution.py:221
  36.9 0.3 collective-permute-start.11
  37.2 0.7 %collective-permute-done.4.refs_3_ = f32[4,128,128]{2,1,0:T(8,128)S(1)} collective-permute-done((f32[4,128,128]{2,1,0:T(8,128)S(1)}, f32[4,128,128]{2,1,0:T(8,128)S(1)}, u32[]{:S(2)}, u32[]{:S(2)}) %collective-permute-start.4) | collective-permute-done | bytes 262176 | tf_op jit(solution)/shard_map/ppermute | solution.py:310
  37.9 0.1 shard_map.80
  38.0 1.8 %collective-permute-start.10 = (f32[4,128,128]{2,1,0:T(8,128)S(1)}, f32[4,128,128]{2,1,0:T(8,128)S(1)}, u32[]{:S(2)}, u32[]{:S(2)}) collective-permute-start(f32[4,128,128]{2,1,0:T(8,128)S(1)} %get-tuple-element.57), channel_id=1, source_target_pairs={{0,2},{1,3},{2,0},{3,1},{4,6},{5,7},{6,4},{7,5},{8,10},{9,11},{10,... | collective-permute-start | bytes 786440 | tf_op jit(solution)/shard_map/ppermute | solution.py:388
  39.8 0.5 %collective-permute-start.14 = (f32[4,128,128]{2,1,0:T(8,128)S(1)}, f32[4,128,128]{2,1,0:T(8,128)S(1)}, u32[]{:S(2)}, u32[]{:S(2)}) collective-permute-start(f32[4,128,128]{2,1,0:T(8,128)S(1)} %collective-permute-done.13.refs_5_), channel_id=1, source_target_pairs={{0,1},{1,0},{2,3},{3,2},{4,5},{5,4},{6,7},{7,6},{8,9},{9,8},{10,11... | collective-permute-start | bytes 786440 | tf_op jit(solution)/shard_map/ppermute | solution.py:398
  40.3 5.6 %collective-permute-done.10.refs_5_ = f32[4,128,128]{2,1,0:T(8,128)S(1)} collective-permute-done((f32[4,128,128]{2,1,0:T(8,128)S(1)}, f32[4,128,128]{2,1,0:T(8,128)S(1)}, u32[]{:S(2)}, u32[]{:S(2)}) %collective-permute-start.10) | collective-permute-done | bytes 262176 | tf_op jit(solution)/shard_map/ppermute | solution.py:388
  45.9 2.0 %shard_map.81 = (bf16[384,2048]{1,0:T(8,128)(2,1)}, bf16[384,2048]{1,0:T(8,128)(2,1)}, bf16[384,2048]{1,0:T(8,128)(2,1)}) custom-call(bf16[384,2048]{1,0:T(8,128)(2,1)S(1)} %get-tuple-element.38.k_ref.refs_0_, bf16[384,2048]{1,0:T(8,128)(2,1)S(1)} %get-tuple-element.39.v_ref.refs_1_, bf16[384,2048]{1,0:T(8,128)(2,1)S(1)} %get-tuple-element.40.g_ref.refs_2_, ...), custom_call_target="tpu_custom_call" | custom-call | tf_op jit(solution)/shard_map/pallas_call | solution.py:275
  47.9 2.0 %shard_map.82 = (bf16[384,2048]{1,0:T(8,128)(2,1)}, bf16[384,2048]{1,0:T(8,128)(2,1)}, bf16[384,2048]{1,0:T(8,128)(2,1)}) custom-call(bf16[384,2048]{1,0:T(8,128)(2,1)S(1)} %get-tuple-element.38.k_ref.refs_0_, bf16[384,2048]{1,0:T(8,128)(2,1)S(1)} %get-tuple-element.39.v_ref.refs_1_, ...), custom_call_target="tpu_custom_call", output_to_operand_aliasing={{0}: (14, {}), {1}: (15, {}), {2}: (16, {})} | custom-call | tf_op jit(solution)/shard_map/pallas_call | solution.py:275
  (16 shorter events, 0.2 us)
Async XLA Ops:
  3.6 2.1 %collective-permute-start.5 = (f32[8,128,128]{2,1,0:T(8,128)S(1)}, f32[8,128,128]{2,1,0:T(8,128)S(1)}, u32[]{:S(2)}, u32[]{:S(2)}) collective-permute-start(f32[8,128,128]{2,1,0:T(8,128)S(1)} %get-tuple-element.46), channel_id=1, source_target_pairs={{0,1},{1,0},{2,3},{3,2},{4,5},{5,4},{6,7},{7,6},{8,9},{9,8},{10,11... | collective-permute-start | bytes 1572872 | tf_op jit(solution)/shard_map/ppermute | solution.py:348
  4.5 4.5 %collective-permute-start = (f32[8,128,128]{2,1,0:T(8,128)S(1)}, f32[8,128,128]{2,1,0:T(8,128)S(1)}, u32[]{:S(2)}, u32[]{:S(2)}) collective-permute-start(f32[8,128,128]{2,1,0:T(8,128)S(1)} %shard_map.68), channel_id=1, source_target_pairs={{0,1},{1,0},{2,3},{3,2},{4,5},{5,4},{6,7},{7,6},{8,9},{9,8},{10,11... | collective-permute-start | bytes 1572872 | tf_op jit(solution)/shard_map/ppermute | solution.py:348
  6.1 10.0 %collective-permute-start.6 = (f32[4,128,128]{2,1,0:T(8,128)S(1)}, f32[4,128,128]{2,1,0:T(8,128)S(1)}, u32[]{:S(2)}, u32[]{:S(2)}) collective-permute-start(f32[4,128,128]{2,1,0:T(8,128)S(1)} %get-tuple-element.48), channel_id=1, source_target_pairs={{0,2},{1,3},{2,0},{3,1},{4,6},{5,7},{6,4},{7,5},{8,10},{9,11},{10,... | collective-permute-start | bytes 786440 | tf_op jit(solution)/shard_map/ppermute | solution.py:351
  9.4 11.8 %collective-permute-start.1 = (f32[4,128,128]{2,1,0:T(8,128)S(1)}, f32[4,128,128]{2,1,0:T(8,128)S(1)}, u32[]{:S(2)}, u32[]{:S(2)}) collective-permute-start(f32[4,128,128]{2,1,0:T(8,128)S(1)} %get-tuple-element.43), channel_id=1, source_target_pairs={{0,2},{1,3},{2,0},{3,1},{4,6},{5,7},{6,4},{7,5},{8,10},{9,11},{10,... | collective-permute-start | bytes 786440 | tf_op jit(solution)/shard_map/ppermute | solution.py:351
  16.1 6.6 %collective-permute-start.7 = (f32[4,128,128]{2,1,0:T(8,128)S(1)}, f32[4,128,128]{2,1,0:T(8,128)S(1)}, u32[]{:S(2)}, u32[]{:S(2)}) collective-permute-start(f32[4,128,128]{2,1,0:T(8,128)S(1)} %shard_map.75.refs_0_), channel_id=1, source_target_pairs={{0,1},{1,5},{2,3},{3,7},{4,0},{5,4},{6,2},{7,6},{8,9},{9,13},{10,1... | collective-permute-start | bytes 786440 | tf_op jit(solution)/shard_map/ppermute | solution.py:310
  21.3 9.2 %collective-permute-start.2 = (f32[4,128,128]{2,1,0:T(8,128)S(1)}, f32[4,128,128]{2,1,0:T(8,128)S(1)}, u32[]{:S(2)}, u32[]{:S(2)}) collective-permute-start(f32[4,128,128]{2,1,0:T(8,128)S(1)} %shard_map.70.refs_0_.refs_2_), channel_id=1, source_target_pairs={{0,1},{1,5},{2,3},{3,7},{4,0},{5,4},{6,2},{7,6},{8,9},{9,13},{10,1... | collective-permute-start | bytes 786440 | tf_op jit(solution)/shard_map/ppermute | solution.py:310
  22.7 8.2 %collective-permute-start.9 = (f32[4,128,128]{2,1,0:T(8,128)S(1)}, f32[4,128,128]{2,1,0:T(8,128)S(1)}, u32[]{:S(2)}, u32[]{:S(2)}) collective-permute-start(f32[4,128,128]{2,1,0:T(8,128)S(1)} %get-tuple-element.51), channel_id=1, source_target_pairs={{0,1},{1,4},{2,3},{3,6},{4,5},{5,13},{6,7},{7,15},{8,0},{9,8},{10,... | collective-permute-start | bytes 786440 | tf_op jit(solution)/shard_map/ppermute | solution.py:310
  22.8 8.1 %collective-permute-start.8 = (f32[4,128,128]{2,1,0:T(8,128)S(1)}, f32[4,128,128]{2,1,0:T(8,128)S(1)}, u32[]{:S(2)}, u32[]{:S(2)}) collective-permute-start(f32[4,128,128]{2,1,0:T(8,128)S(1)} %get-tuple-element.51), channel_id=1, source_target_pairs={{0,1},{1,0},{2,3},{3,2},{4,5},{5,9},{6,7},{7,11},{8,4},{9,8},{10,6... | collective-permute-start | bytes 786440 | tf_op jit(solution)/shard_map/ppermute | solution.py:310
  30.6 7.3 %collective-permute-start.4 = (f32[4,128,128]{2,1,0:T(8,128)S(1)}, f32[4,128,128]{2,1,0:T(8,128)S(1)}, u32[]{:S(2)}, u32[]{:S(2)}) collective-permute-start(f32[4,128,128]{2,1,0:T(8,128)S(1)} %get-tuple-element.44.refs_5_), channel_id=1, source_target_pairs={{0,1},{1,4},{2,3},{3,6},{4,5},{5,13},{6,7},{7,15},{8,0},{9,8},{10,... | collective-permute-start | bytes 786440 | tf_op jit(solution)/shard_map/ppermute | solution.py:310
  30.6 7.3 %collective-permute-start.3 = (f32[4,128,128]{2,1,0:T(8,128)S(1)}, f32[4,128,128]{2,1,0:T(8,128)S(1)}, u32[]{:S(2)}, u32[]{:S(2)}) collective-permute-start(f32[4,128,128]{2,1,0:T(8,128)S(1)} %get-tuple-element.44.refs_5_), channel_id=1, source_target_pairs={{0,1},{1,0},{2,3},{3,2},{4,5},{5,9},{6,7},{7,11},{8,4},{9,8},{10,6... | collective-permute-start | bytes 786440 | tf_op jit(solution)/shard_map/ppermute | solution.py:310
  31.0 8.8 %collective-permute-start.13 = (f32[4,128,128]{2,1,0:T(8,128)S(1)}, f32[4,128,128]{2,1,0:T(8,128)S(1)}, u32[]{:S(2)}, u32[]{:S(2)}) collective-permute-start(f32[4,128,128]{2,1,0:T(8,128)S(1)} %get-tuple-element.53.refs_0_), channel_id=1, source_target_pairs={{0,2},{1,3},{2,0},{3,1},{4,6},{5,7},{6,4},{7,5},{8,10},{9,11},{10,... | collective-permute-start | bytes 786440 | tf_op jit(solution)/shard_map/ppermute | solution.py:388
  36.9 3.4 %collective-permute-start.11 = (f32[4,128,128]{2,1,0:T(8,128)S(1)}, f32[4,128,128]{2,1,0:T(8,128)S(1)}, u32[]{:S(2)}, u32[]{:S(2)}) collective-permute-start(f32[4,128,128]{2,1,0:T(8,128)S(1)} %get-tuple-element.58.refs_4_), channel_id=1, source_target_pairs={{0,1},{1,0},{2,3},{3,2},{4,5},{5,4},{6,7},{7,6},{8,9},{9,8},{10,11... | collective-permute-start | bytes 786440 | tf_op jit(solution)/shard_map/ppermute | solution.py:389
  38.0 7.9 %collective-permute-start.10 = (f32[4,128,128]{2,1,0:T(8,128)S(1)}, f32[4,128,128]{2,1,0:T(8,128)S(1)}, u32[]{:S(2)}, u32[]{:S(2)}) collective-permute-start(f32[4,128,128]{2,1,0:T(8,128)S(1)} %get-tuple-element.57), channel_id=1, source_target_pairs={{0,2},{1,3},{2,0},{3,1},{4,6},{5,7},{6,4},{7,5},{8,10},{9,11},{10,... | collective-permute-start | bytes 786440 | tf_op jit(solution)/shard_map/ppermute | solution.py:388
  39.8 6.1 %collective-permute-start.12 = (f32[4,128,128]{2,1,0:T(8,128)S(1)}, f32[4,128,128]{2,1,0:T(8,128)S(1)}, u32[]{:S(2)}, u32[]{:S(2)}) collective-permute-start(f32[4,128,128]{2,1,0:T(8,128)S(1)} %get-tuple-element.56.refs_4_), channel_id=1, source_target_pairs={{0,1},{1,0},{2,3},{3,2},{4,5},{5,4},{6,7},{7,6},{8,9},{9,8},{10,11... | collective-permute-start | bytes 786440 | tf_op jit(solution)/shard_map/ppermute | solution.py:389
  39.8 6.1 %collective-permute-start.14 = (f32[4,128,128]{2,1,0:T(8,128)S(1)}, f32[4,128,128]{2,1,0:T(8,128)S(1)}, u32[]{:S(2)}, u32[]{:S(2)}) collective-permute-start(f32[4,128,128]{2,1,0:T(8,128)S(1)} %collective-permute-done.13.refs_5_), channel_id=1, source_target_pairs={{0,1},{1,0},{2,3},{3,2},{4,5},{5,4},{6,7},{7,6},{8,9},{9,8},{10,11... | collective-permute-start | bytes 786440 | tf_op jit(solution)/shard_map/ppermute | solution.py:398
  45.9 2.0 %collective-permute-start.15 = (f32[4,128,128]{2,1,0:T(8,128)S(1)}, f32[4,128,128]{2,1,0:T(8,128)S(1)}, u32[]{:S(2)}, u32[]{:S(2)}) collective-permute-start(f32[4,128,128]{2,1,0:T(8,128)S(1)} %collective-permute-done.10.refs_5_), channel_id=1, source_target_pairs={{0,1},{1,0},{2,3},{3,2},{4,5},{5,4},{6,7},{7,6},{8,9},{9,8},{10,11... | collective-permute-start | bytes 786440 | tf_op jit(solution)/shard_map/ppermute | solution.py:398

commit v6 on v5

--- a/solution.py
+++ b/solution.py
@@ -15,13 +15,14 @@
 PLACES = (
     ((0, 0), ("kept", 1), ("plane", 0)),
     ((0, 1), ("kept", 1), ("plane", 0)),
-    ((1, 0), ("back", 0), ("scan", 1)),
-    ((1, 1), ("back", 0), ("scan", 1)),
+    ((1, 0), ("window0", 0), ("window0", 1)),
+    ((1, 1), ("window0", 1), ("scan", 0)),
 )
 F32 = jnp.float32
 BF16 = jnp.bfloat16
 VMEM_LIMIT = 24 * 1024 * 1024
-VMEM_MOST = 46 * 1024 * 1024
+VMEM_FIRST = int(49.4 * 1024 * 1024)
+VMEM_NEXT = int(47.4 * 1024 * 1024)
 ANY = pl.BlockSpec(memory_space=pl.ANY)
 HBM = pl.BlockSpec(memory_space=pltpu.HBM)
 VMEM = pl.BlockSpec(memory_space=pltpu.VMEM)
@@ -41,35 +42,28 @@
     return core == 1, core == chip
 
 
-def first_kernel(size, q_ref, k_ref, v_ref, g_ref, other_ref, qv_ref, kv_ref, vv_ref, gv_ref, sem):
+def load_kernel(first, size, count, q_ref, k_ref, v_ref, g_ref, *refs):
+    other_ref, *targets, sem = refs[count:]
     later, second = place()
-    width = q_ref.shape[1]
-    cut = size * HD
-    pieces = [(0, cut // 2), (cut // 2, cut // 2)] + ([(cut, width - cut)] if width > cut else [])
-
-    def copies(j, source, target):
+    half = size // 2
+
+    def copies(j, source):
         made = []
-        for n, (start, count) in enumerate(pieces):
-            cols = pl.ds(start, count)
-            made.append(pltpu.make_async_copy(source.at[:, cols], target.at[:, cols], sem.at[j, n]))
+        for n in range(2):
+            cols = pl.ds((first + n * half) * HD, half * HD)
+            target = targets[j].at[:, pl.ds(n * half * HD, half * HD)]
+            made.append(pltpu.make_async_copy(source.at[:, cols], target, sem.at[j, n]))
         return made
 
-    q, k, v, g = (
-        copies(j, source, target)
-        for j, (source, target) in enumerate(((q_ref, qv_ref), (k_ref, kv_ref), (v_ref, vv_ref), (g_ref, gv_ref)))
-    )
+    q, k, v, g = (copies(j, source) for j, source in enumerate((q_ref, k_ref, v_ref, g_ref)))
 
     def run(pair, refs, rest):
         for n in range(2):
             for copy in pair:
                 copy[n].start()
-        for copy in rest:
-            for n in range(2):
+        for n in range(2):
+            for copy in rest:
                 copy[n].start()
-        for copy in (*rest, *pair):
-            for n in range(2, len(pieces)):
-                copy[n].start()
-        half = size // 2
         turn = jnp.where(second, 0, half)
         for n in range(2):
             for copy in pair:
@@ -77,63 +71,42 @@
             for h in range(half):
                 cols = slice((n * half + h) * HD, (n * half + h + 1) * HD)
                 other_ref[lax.rem(n * half + turn, size) + h] = dot(refs[0][:, cols], refs[1][:, cols], ((0,), (0,)))
-        for copy in rest:
-            for n in range(2):
+        for n in range(2):
+            for copy in rest:
                 copy[n].wait()
-        for copy in (*rest, *pair):
-            for n in range(2, len(pieces)):
-                copy[n].wait()
+
+    qc_ref, kc_ref, vc_ref, gc_ref = targets
 
     @pl.when(later)
     def _():
-        run((q, g), (qv_ref, gv_ref), (k, v))
+        run((q, g), (qc_ref, gc_ref), (k, v))
 
     @pl.when(jnp.logical_not(later))
     def _():
-        run((k, v), (kv_ref, vv_ref), (q, g))
-
-
-def first_state(arrays, size):
-    rows, width = arrays[0].shape
-    return pl.pallas_call(
-        functools.partial(first_kernel, size),
-        out_shape=[jax.ShapeDtypeStruct((size, HD, HD), F32)] + [jax.ShapeDtypeStruct((rows, width), BF16)] * 4,
-        in_specs=[ANY] * 4,
+        run((k, v), (kc_ref, vc_ref), (q, g))
+
+
+def load(arrays, first, size, limit, after):
+    rows = arrays[0].shape[0]
+    return pl.pallas_call(
+        functools.partial(load_kernel, first, size, len(after)),
+        out_shape=[jax.ShapeDtypeStruct((size, HD, HD), F32)] + [jax.ShapeDtypeStruct((rows, size * HD), BF16)] * 4,
+        in_specs=[ANY] * (4 + len(after)),
         out_specs=[VMEM] * 5,
-        scratch_shapes=[pltpu.SemaphoreType.DMA((4, 3))],
-        compiler_params=pltpu.CompilerParams(vmem_limit_bytes=VMEM_MOST),
-        cost_estimate=cost(2 * size * rows * HD * HD, 16 * rows * width),
-    )(*arrays)
-
-
-def other_kernel(first, size, q_ref, k_ref, v_ref, g_ref, out_ref):
-    later, second = place()
-    half = size // 2
-    turn = jnp.where(second, 0, half)
-
-    def run(a_ref, b_ref):
-        for h in range(size):
-            cols = slice((first + h) * HD, (first + h + 1) * HD)
-            at = lax.rem(h // half * half + turn, size) + h % half
-            out_ref[at] = dot(a_ref[:, cols], b_ref[:, cols], ((0,), (0,)))
-
-    @pl.when(later)
-    def _():
-        run(q_ref, g_ref)
-
-    @pl.when(jnp.logical_not(later))
-    def _():
-        run(k_ref, v_ref)
-
-
-def mine_kernel(first, size, q_ref, k_ref, v_ref, g_ref, other_ref, kept_ref, sent_ref):
+        scratch_shapes=[pltpu.SemaphoreType.DMA((4, 2))],
+        compiler_params=pltpu.CompilerParams(vmem_limit_bytes=limit),
+        cost_estimate=cost(2 * size * rows * HD * HD, 16 * rows * size * HD),
+    )(*arrays, *after)
+
+
+def mine_kernel(size, q_ref, k_ref, v_ref, g_ref, other_ref, kept_ref, sent_ref):
     later, second = place()
     half = size // 2
 
     def run(pair, swap):
         refs = (sent_ref, kept_ref) if swap else (kept_ref, sent_ref)
         for h in range(size):
-            cols = slice((first + h) * HD, (first + h + 1) * HD)
+            cols = slice(h * HD, (h + 1) * HD)
             at = (h + (half if swap else 0)) % size
             value = dot(pair[0][:, cols], pair[1][:, cols], ((0,), (0,)))
             refs[h // half][h % half] = value + other_ref[at]
@@ -143,23 +116,11 @@
             pl.when(jnp.logical_and(later == is_later, second == swap))(functools.partial(run, pair, swap))
 
 
-def other_state(arrays, first, size):
-    rows = arrays[0].shape[0]
-    return pl.pallas_call(
-        functools.partial(other_kernel, first, size),
-        out_shape=jax.ShapeDtypeStruct((size, HD, HD), F32),
-        in_specs=[VMEM] * 4,
-        out_specs=VMEM,
-        compiler_params=pltpu.CompilerParams(vmem_limit_bytes=VMEM_LIMIT),
-        cost_estimate=cost(2 * size * rows * HD * HD, 4 * size * rows * HD),
-    )(*arrays)
-
-
-def chip_state(arrays, other, first, size):
+def chip_state(arrays, other, size):
     rows = arrays[0].shape[0]
     half = jax.ShapeDtypeStruct((size // 2, HD, HD), F32)
     return pl.pallas_call(
-        functools.partial(mine_kernel, first, size),
+        functools.partial(mine_kernel, size),
         out_shape=[half, half],
         in_specs=[VMEM] * 5,
         out_specs=[VMEM, VMEM],
@@ -256,9 +217,9 @@
         cols = slice(n * per * HD, (n + 1) * per * HD)
         whole = slice((first + n * per) * HD, (first + (n + 1) * per) * HD)
         terms = (
-            dot(g_ref[:, whole], kv, ((1,), (1,))),
-            dot(v_ref[:, whole], qg, ((1,), (1,))),
-            dot(k_ref[:, whole], qg, ((1,), (0,))),
+            dot(g_ref[:, cols], kv, ((1,), (1,))),
+            dot(v_ref[:, cols], qg, ((1,), (1,))),
+            dot(k_ref[:, cols], qg, ((1,), (0,))),
         )
         held = slice(n * per % piece * HD, (n * per % piece + per) * HD)
         for j, term in enumerate(terms):
@@ -270,8 +231,8 @@
         copy.wait()
 
 
-def final(k, v, g, partials, other, states, first, size, scale, held):
-    rows, width = k.shape
+def final(k, v, g, partials, other, states, first, size, width, scale, held):
+    rows = k.shape[0]
     return pl.pallas_call(
         functools.partial(final_kernel, first, size // 2, scale),
         out_shape=[jax.ShapeDtypeStruct((rows, width), BF16)] * 3,
@@ -319,7 +280,7 @@
         return total
 
     if planes == 4 and TREE:
-        levels = [[{1: 0, 3: 2}], [{2: 1}, {3: 1}]]
+        levels = [[{1: 0, 3: 2}], [{3: 1}, {2: 1}]]
     else:
         levels, by = [], 1
         while by < planes:
@@ -328,8 +289,6 @@
 
     sizes = [heads * part // sum(CHUNKS) for part in CHUNKS]
     firsts = [sum(sizes[:i]) for i in range(len(sizes))]
-    first_other, *arrays = first_state((queries, keys, values, out_grad), sizes[0])
-    _, keys, values, out_grad = arrays
     chunks = range(len(sizes))
     made = {}
     pieces = [[] for _ in sizes]
@@ -338,17 +297,20 @@
         found = []
         for (c, p), after, before in PLACES:
             if before == (name, chunk):
-                part = within(arrays, firsts[c] + p * PIECE, min(PIECE, sizes[c]), scale, [made[after]])
+                part = within(made["arrays", c], p * PIECE, min(PIECE, sizes[c]), scale, [made[after]])
                 pieces[c] = [*pieces[c], *part]
                 found.append(part[0])
         return found
 
     for c in chunks:
-        other = other_state(arrays, firsts[c], sizes[c]) if c else first_other
+        after = [made["sum", c - 1]] if c else []
+        limit = VMEM_FIRST if c == 0 else VMEM_NEXT
+        other, *made["arrays", c] = load((queries, keys, values, out_grad), firsts[c], sizes[c], limit, after)
+        made["sum", c] = other
         made["other", c] = lax.ppermute(other, "seq", core_pairs)
-    for c in chunks:
-        made["kept", c], sent = chip_state(arrays, made["other", c], firsts[c], sizes[c])
+        made["kept", c], sent = chip_state(made["arrays", c], made["other", c], sizes[c])
         made["partner", c] = lax.ppermute(sent, "seq", chip_pairs)
+
     def stage(name, c, before):
         return wait_for(name, c) + ([made[before, c + 1]] if c + 1 < len(sizes) else [])
 
@@ -400,7 +362,7 @@
         ahead = [done[chunk + 1][2]] if chunk + 1 < len(sizes) else []
         given_swapped, ahead = lax.optimization_barrier((given_swapped, ahead))
         states = (kept_upto, swapped, given_kept, given_swapped)
-        out = final(keys, values, out_grad, pieces[chunk], other, states, first, size, scale, out)
+        out = final(*made["arrays", chunk][1:], pieces[chunk], other, states, first, size, heads * HD, scale, out)
     return tuple(out)
 
 

time: 50.6 us -> 49.3 us (0.974)
  waiting for transfers between devices: 22.8 us -> 20.9 us
  Pallas kernels: 16.8 us -> 17.4 us
    ppermute x6, waiting for transfers between devices: 8.95 us -> 7.67 us  [moved(): return lax.ppermute(value, 'seq', sorted(pairs.items()))]
    ppermute x2, waiting for transfers between devices: 5.6 us -> 6.73 us  [local(): swapped = lax.ppermute(made['back', c], 'seq', chip_pairs)]
    ppermute x2, waiting for transfers between devices: 0.98 us -> 0.01 us  [local(): made['other', c] = lax.ppermute(other, 'seq', core_pairs)]
    ppermute x2, starting transfers between devices: 3.23 us -> 4.09 us  [local(): made['partner', c] = lax.ppermute(sent, 'seq', chip_pairs)]
    ppermute x2, waiting for transfers between devices: 7.26 us -> 6.48 us  [local(): made['partner', c] = lax.ppermute(sent, 'seq', chip_pairs)]
    ppermute x2, starting transfers between devices: 3.61 us -> 3.08 us  [local(): swapped = lax.ppermute(made['back', c], 'seq', chip_pairs)]
    pallas_call x4, Pallas kernels: 4.24 us -> 4.77 us  [the longest x2 3.9 us: load(): pl.pallas_call(functools.partial(load_kernel, first, size, len(after)), o...]
  transfers between devices with their start and end apart: 16 -> 16, of which waited for: 7 -> 8; matrix products, arithmetic and copies ran while one was open for 0% -> 0% of each run, Pallas kernels for 24% -> 27%
where the time goes in v6:
time: 49.3 us; the launch traced here: 48.6 us
  waiting for transfers between devices  20.9 us (42%)
  Pallas kernels  17.4 us (35%)
  starting transfers between devices  9.3 us (19%)
  between operations  0.97 us (2%)
    pallas_call x4, Pallas kernels, within(): pl.pallas_call(functools.partial(within_kernel, first, heads, scale), out...  8.2 us
    ppermute x6, waiting for transfers between devices, moved(): return lax.ppermute(value, 'seq', sorted(pairs.items()))  7.67 us
    ppermute x2, waiting for transfers between devices, local(): swapped = lax.ppermute(made['back', c], 'seq', chip_pairs)  6.73 us
    ppermute x2, waiting for transfers between devices, local(): made['partner', c] = lax.ppermute(sent, 'seq', chip_pairs)  6.48 us
    pallas_call x2, Pallas kernels, final(): pl.pallas_call(functools.partial(final_kernel, first, size // 2, scale),...  4.1 us
    ppermute x2, starting transfers between devices, local(): made['partner', c] = lax.ppermute(sent, 'seq', chip_pairs)  4.09 us
    pallas_call x2, Pallas kernels, load(): pl.pallas_call(functools.partial(load_kernel, first, size, len(after)), o...  3.9 us
    ppermute x2, starting transfers between devices, local(): swapped = lax.ppermute(made['back', c], 'seq', chip_pairs)  3.08 us
  transfers between devices with their start and end apart: 16, of which 8 were waited for; matrix products, arithmetic and copies ran while one was open for 0% of the time, Pallas kernels for 27%

profile of v6, /device:TPU:0, one launch (start us, length us, event | category | flops | bytes accessed | tf_op | source)
XLA Modules:
  0.0 48.6 jit_solution(15516633937107397203)
XLA Ops:
  0.6 2.0 %shard_map.67 = (f32[8,128,128]{2,1,0:T(8,128)S(1)}, bf16[384,1024]{1,0:T(8,128)(2,1)S(1)}, bf16[384,1024]{1,0:T(8,128)(2,1)S(1)}, bf16[384,1024]{1,0:T(8,128)(2,1)S(1)}, bf16[384,1024]{1,0:T(8,128)(2,1)S(1)}) custom-call(bf16[384,2048]{1,0:T(8,128)(2,1)} %q_ref.3, bf16[384,2048]{1,0:T(8,128)(2,1)} %k_ref.3, bf16[384,2048]{1,0:T(8,128)(2,1)} %v_ref.3, ...), custom_call_target="tpu_custom_call" | custom-call | tf_op jit(solution)/shard_map/pallas_call | solution.py:91
  2.7 0.5 %collective-permute-start.3 = (f32[8,128,128]{2,1,0:T(8,128)S(1)}, f32[8,128,128]{2,1,0:T(8,128)S(1)}, u32[]{:S(2)}, u32[]{:S(2)}) collective-permute-start(f32[8,128,128]{2,1,0:T(8,128)S(1)} %get-tuple-element.43.refs_0_), channel_id=1, source_target_pairs={{0,1},{1,0},{2,3},{3,2},{4,5},{5,4},{6,7},{7,6},{8,9},{9,8},{10,11... | collective-permute-start | bytes 1572872 | tf_op jit(solution)/shard_map/ppermute | solution.py:310
  3.2 1.9 %shard_map.68 = (f32[8,128,128]{2,1,0:T(8,128)S(1)}, bf16[384,1024]{1,0:T(8,128)(2,1)S(1)}, bf16[384,1024]{1,0:T(8,128)(2,1)S(1)}, bf16[384,1024]{1,0:T(8,128)(2,1)S(1)}, bf16[384,1024]{1,0:T(8,128)(2,1)S(1)}) custom-call(bf16[384,2048]{1,0:T(8,128)(2,1)S(1)} %copy-done, bf16[384,2048]{1,0:T(8,128)(2,1)} %k_ref.3, bf16[384,2048]{1,0:T(8,128)(2,1)} %v_ref.3, ...), custom_call_target="tpu_custom_call" | custom-call | tf_op jit(solution)/shard_map/pallas_call | solution.py:91
  5.1 0.2 collective-permute-start
  5.3 0.4 shard_map.71
  5.7 2.8 %collective-permute-start.4 = (f32[4,128,128]{2,1,0:T(8,128)S(1)}, f32[4,128,128]{2,1,0:T(8,128)S(1)}, u32[]{:S(2)}, u32[]{:S(2)}) collective-permute-start(f32[4,128,128]{2,1,0:T(8,128)S(1)} %get-tuple-element.56), channel_id=1, source_target_pairs={{0,2},{1,3},{2,0},{3,1},{4,6},{5,7},{6,4},{7,5},{8,10},{9,11},{10,... | collective-permute-start | bytes 786440 | tf_op jit(solution)/shard_map/ppermute | solution.py:312
  8.6 0.4 shard_map.69
  9.0 2.1 %shard_map.73 = (bf16[384,512]{1,0:T(8,128)(2,1)S(1)}, bf16[384,512]{1,0:T(8,128)(2,1)S(1)}, bf16[384,512]{1,0:T(8,128)(2,1)S(1)}) custom-call(bf16[384,1024]{1,0:T(8,128)(2,1)S(1)} %get-tuple-element.51.q_ref, bf16[384,1024]{1,0:T(8,128)(2,1)S(1)} %get-tuple-element.52.k_ref.refs_0_, bf16[384,1024]{1,0:T(8,128)(2,1)S(1)} %get-tuple-element.53.v_ref.refs_1_, ...), custom_call_target="tpu_custom_call" | custom-call | tf_op jit(solution)/shard_map/pallas_call | solution.py:182
  11.1 1.3 %collective-permute-start.1 = (f32[4,128,128]{2,1,0:T(8,128)S(1)}, f32[4,128,128]{2,1,0:T(8,128)S(1)}, u32[]{:S(2)}, u32[]{:S(2)}) collective-permute-start(f32[4,128,128]{2,1,0:T(8,128)S(1)} %get-tuple-element.50), channel_id=1, source_target_pairs={{0,2},{1,3},{2,0},{3,1},{4,6},{5,7},{6,4},{7,5},{8,10},{9,11},{10,... | collective-permute-start | bytes 786440 | tf_op jit(solution)/shard_map/ppermute | solution.py:312
  12.3 2.1 %shard_map.72 = (bf16[384,512]{1,0:T(8,128)(2,1)S(1)}, bf16[384,512]{1,0:T(8,128)(2,1)S(1)}, bf16[384,512]{1,0:T(8,128)(2,1)S(1)}) custom-call(bf16[384,1024]{1,0:T(8,128)(2,1)S(1)} %get-tuple-element.51.q_ref, bf16[384,1024]{1,0:T(8,128)(2,1)S(1)} %get-tuple-element.52.k_ref.refs_0_, bf16[384,1024]{1,0:T(8,128)(2,1)S(1)} %get-tuple-element.53.v_ref.refs_1_, ...), custom_call_target="tpu_custom_call" | custom-call | tf_op jit(solution)/shard_map/pallas_call | solution.py:182
  14.4 1.2 %collective-permute-done.4.refs_1_ = f32[4,128,128]{2,1,0:T(8,128)S(1)} collective-permute-done((f32[4,128,128]{2,1,0:T(8,128)S(1)}, f32[4,128,128]{2,1,0:T(8,128)S(1)}, u32[]{:S(2)}, u32[]{:S(2)}) %collective-permute-start.4) | collective-permute-done | bytes 262176 | tf_op jit(solution)/shard_map/ppermute | solution.py:312
  15.6 0.1 collective-permute-start.5
  15.7 5.3 %collective-permute-done.1.refs_1_ = f32[4,128,128]{2,1,0:T(8,128)S(1)} collective-permute-done((f32[4,128,128]{2,1,0:T(8,128)S(1)}, f32[4,128,128]{2,1,0:T(8,128)S(1)}, u32[]{:S(2)}, u32[]{:S(2)}) %collective-permute-start.1) | collective-permute-done | bytes 262176 | tf_op jit(solution)/shard_map/ppermute | solution.py:312
  21.0 0.1 collective-permute-start.2
  21.1 1.1 %collective-permute-done.5.refs_1_ = f32[4,128,128]{2,1,0:T(8,128)S(1)} collective-permute-done((f32[4,128,128]{2,1,0:T(8,128)S(1)}, f32[4,128,128]{2,1,0:T(8,128)S(1)}, u32[]{:S(2)}, u32[]{:S(2)}) %collective-permute-start.5) | collective-permute-done | bytes 262176 | tf_op jit(solution)/shard_map/ppermute | solution.py:271
  22.3 0.5 %collective-permute-start.9 = (f32[4,128,128]{2,1,0:T(8,128)S(1)}, f32[4,128,128]{2,1,0:T(8,128)S(1)}, u32[]{:S(2)}, u32[]{:S(2)}) collective-permute-start(f32[4,128,128]{2,1,0:T(8,128)S(1)} %get-tuple-element.59.refs_0_), channel_id=1, source_target_pairs={{0,1},{1,4},{2,3},{3,6},{4,5},{5,13},{6,7},{7,15},{8,0},{9,8},{10,... | collective-permute-start | bytes 786440 | tf_op jit(solution)/shard_map/ppermute | solution.py:271
  22.8 2.1 %shard_map.76 = (bf16[384,512]{1,0:T(8,128)(2,1)S(1)}, bf16[384,512]{1,0:T(8,128)(2,1)S(1)}, bf16[384,512]{1,0:T(8,128)(2,1)S(1)}) custom-call(bf16[384,1024]{1,0:T(8,128)(2,1)S(1)} %get-tuple-element.48.q_ref, bf16[384,1024]{1,0:T(8,128)(2,1)S(1)} %get-tuple-element.44.k_ref.refs_0_, bf16[384,1024]{1,0:T(8,128)(2,1)S(1)} %get-tuple-element.45.v_ref.refs_1_, ...), custom_call_target="tpu_custom_call" | custom-call | tf_op jit(solution)/shard_map/pallas_call | solution.py:182
  24.9 2.5 %collective-permute-done.2.refs_1_ = f32[4,128,128]{2,1,0:T(8,128)S(1)} collective-permute-done((f32[4,128,128]{2,1,0:T(8,128)S(1)}, f32[4,128,128]{2,1,0:T(8,128)S(1)}, u32[]{:S(2)}, u32[]{:S(2)}) %collective-permute-start.2) | collective-permute-done | bytes 262176 | tf_op jit(solution)/shard_map/ppermute | solution.py:271
  27.5 0.1 collective-permute-start.6
  27.6 2.0 %shard_map.79 = (bf16[384,512]{1,0:T(8,128)(2,1)S(1)}, bf16[384,512]{1,0:T(8,128)(2,1)S(1)}, bf16[384,512]{1,0:T(8,128)(2,1)S(1)}) custom-call(bf16[384,1024]{1,0:T(8,128)(2,1)S(1)} %get-tuple-element.48.q_ref, bf16[384,1024]{1,0:T(8,128)(2,1)S(1)} %get-tuple-element.44.k_ref.refs_0_, bf16[384,1024]{1,0:T(8,128)(2,1)S(1)} %get-tuple-element.45.v_ref.refs_1_, ...), custom_call_target="tpu_custom_call" | custom-call | tf_op jit(solution)/shard_map/pallas_call | solution.py:182
  29.7 2.8 %collective-permute-done.9.refs_2_ = f32[4,128,128]{2,1,0:T(8,128)S(1)} collective-permute-done((f32[4,128,128]{2,1,0:T(8,128)S(1)}, f32[4,128,128]{2,1,0:T(8,128)S(1)}, u32[]{:S(2)}, u32[]{:S(2)}) %collective-permute-start.9) | collective-permute-done | bytes 262176 | tf_op jit(solution)/shard_map/ppermute | solution.py:271
  32.5 0.1 shard_map.80
  32.6 1.5 %collective-permute-start.13 = (f32[4,128,128]{2,1,0:T(8,128)S(1)}, f32[4,128,128]{2,1,0:T(8,128)S(1)}, u32[]{:S(2)}, u32[]{:S(2)}) collective-permute-start(f32[4,128,128]{2,1,0:T(8,128)S(1)} %get-tuple-element.68), channel_id=1, source_target_pairs={{0,2},{1,3},{2,0},{3,1},{4,6},{5,7},{6,4},{7,5},{8,10},{9,11},{10,... | collective-permute-start | bytes 786440 | tf_op jit(solution)/shard_map/ppermute | solution.py:350
  34.2 1.2 %collective-permute-done.6.refs_2_ = f32[4,128,128]{2,1,0:T(8,128)S(1)} collective-permute-done((f32[4,128,128]{2,1,0:T(8,128)S(1)}, f32[4,128,128]{2,1,0:T(8,128)S(1)}, u32[]{:S(2)}, u32[]{:S(2)}) %collective-permute-start.6) | collective-permute-done | bytes 262176 | tf_op jit(solution)/shard_map/ppermute | solution.py:271
  35.3 0.1 shard_map.78
  35.4 1.5 %collective-permute-start.8 = (f32[4,128,128]{2,1,0:T(8,128)S(1)}, f32[4,128,128]{2,1,0:T(8,128)S(1)}, u32[]{:S(2)}, u32[]{:S(2)}) collective-permute-start(f32[4,128,128]{2,1,0:T(8,128)S(1)} %get-tuple-element.64), channel_id=1, source_target_pairs={{0,2},{1,3},{2,0},{3,1},{4,6},{5,7},{6,4},{7,5},{8,10},{9,11},{10,... | collective-permute-start | bytes 786440 | tf_op jit(solution)/shard_map/ppermute | solution.py:350
  37.0 0.5 %collective-permute-start.12 = (f32[4,128,128]{2,1,0:T(8,128)S(1)}, f32[4,128,128]{2,1,0:T(8,128)S(1)}, u32[]{:S(2)}, u32[]{:S(2)}) collective-permute-start(f32[4,128,128]{2,1,0:T(8,128)S(1)} %get-tuple-element.63.refs_4_), channel_id=1, source_target_pairs={{0,1},{1,0},{2,3},{3,2},{4,5},{5,4},{6,7},{7,6},{8,9},{9,8},{10,11... | collective-permute-start | bytes 786440 | tf_op jit(solution)/shard_map/ppermute | solution.py:351
  37.5 3.9 %collective-permute-done.13.refs_5_ = f32[4,128,128]{2,1,0:T(8,128)S(1)} collective-permute-done((f32[4,128,128]{2,1,0:T(8,128)S(1)}, f32[4,128,128]{2,1,0:T(8,128)S(1)}, u32[]{:S(2)}, u32[]{:S(2)}) %collective-permute-start.13) | collective-permute-done | bytes 262176 | tf_op jit(solution)/shard_map/ppermute | solution.py:350
  41.4 2.8 %collective-permute-done.8.refs_5_ = f32[4,128,128]{2,1,0:T(8,128)S(1)} collective-permute-done((f32[4,128,128]{2,1,0:T(8,128)S(1)}, f32[4,128,128]{2,1,0:T(8,128)S(1)}, u32[]{:S(2)}, u32[]{:S(2)}) %collective-permute-start.8) | collective-permute-done | bytes 262176 | tf_op jit(solution)/shard_map/ppermute | solution.py:350
  44.2 0.1 collective-permute-start.15
  44.3 2.1 %shard_map.81 = (bf16[384,2048]{1,0:T(8,128)(2,1)}, bf16[384,2048]{1,0:T(8,128)(2,1)}, bf16[384,2048]{1,0:T(8,128)(2,1)}) custom-call(bf16[384,1024]{1,0:T(8,128)(2,1)S(1)} %get-tuple-element.52.k_ref.refs_0_, bf16[384,1024]{1,0:T(8,128)(2,1)S(1)} %get-tuple-element.53.v_ref.refs_1_, bf16[384,1024]{1,0:T(8,128)(2,1)S(1)} %get-tuple-element.54.g_ref.refs_2_, ...), custom_call_target="tpu_custom_call" | custom-call | tf_op jit(solution)/shard_map/pallas_call | solution.py:236
  46.4 2.0 %shard_map.82 = (bf16[384,2048]{1,0:T(8,128)(2,1)}, bf16[384,2048]{1,0:T(8,128)(2,1)}, bf16[384,2048]{1,0:T(8,128)(2,1)}) custom-call(bf16[384,1024]{1,0:T(8,128)(2,1)S(1)} %get-tuple-element.44.k_ref.refs_0_, bf16[384,1024]{1,0:T(8,128)(2,1)S(1)} %get-tuple-element.45.v_ref.refs_1_, ...), custom_call_target="tpu_custom_call", output_to_operand_aliasing={{0}: (14, {}), {1}: (15, {}), {2}: (16, {})} | custom-call | tf_op jit(solution)/shard_map/pallas_call | solution.py:236
  (18 shorter events, 0.3 us)
Async XLA Ops:
  0.6 2.6 %copy-start = (bf16[384,2048]{1,0:T(8,128)(2,1)S(1)}, bf16[384,2048]{1,0:T(8,128)(2,1)}, u32[]{:S(2)}) copy-start(bf16[384,2048]{1,0:T(8,128)(2,1)} %q_ref.3) | copy-start | bytes 4718596
  2.7 2.6 %collective-permute-start.3 = (f32[8,128,128]{2,1,0:T(8,128)S(1)}, f32[8,128,128]{2,1,0:T(8,128)S(1)}, u32[]{:S(2)}, u32[]{:S(2)}) collective-permute-start(f32[8,128,128]{2,1,0:T(8,128)S(1)} %get-tuple-element.43.refs_0_), channel_id=1, source_target_pairs={{0,1},{1,0},{2,3},{3,2},{4,5},{5,4},{6,7},{7,6},{8,9},{9,8},{10,11... | collective-permute-start | bytes 1572872 | tf_op jit(solution)/shard_map/ppermute | solution.py:310
  5.1 3.5 %collective-permute-start = (f32[8,128,128]{2,1,0:T(8,128)S(1)}, f32[8,128,128]{2,1,0:T(8,128)S(1)}, u32[]{:S(2)}, u32[]{:S(2)}) collective-permute-start(f32[8,128,128]{2,1,0:T(8,128)S(1)} %get-tuple-element.47), channel_id=1, source_target_pairs={{0,1},{1,0},{2,3},{3,2},{4,5},{5,4},{6,7},{7,6},{8,9},{9,8},{10,11... | collective-permute-start | bytes 1572872 | tf_op jit(solution)/shard_map/ppermute | solution.py:310
  5.7 9.9 %collective-permute-start.4 = (f32[4,128,128]{2,1,0:T(8,128)S(1)}, f32[4,128,128]{2,1,0:T(8,128)S(1)}, u32[]{:S(2)}, u32[]{:S(2)}) collective-permute-start(f32[4,128,128]{2,1,0:T(8,128)S(1)} %get-tuple-element.56), channel_id=1, source_target_pairs={{0,2},{1,3},{2,0},{3,1},{4,6},{5,7},{6,4},{7,5},{8,10},{9,11},{10,... | collective-permute-start | bytes 786440 | tf_op jit(solution)/shard_map/ppermute | solution.py:312
  11.1 9.9 %collective-permute-start.1 = (f32[4,128,128]{2,1,0:T(8,128)S(1)}, f32[4,128,128]{2,1,0:T(8,128)S(1)}, u32[]{:S(2)}, u32[]{:S(2)}) collective-permute-start(f32[4,128,128]{2,1,0:T(8,128)S(1)} %get-tuple-element.50), channel_id=1, source_target_pairs={{0,2},{1,3},{2,0},{3,1},{4,6},{5,7},{6,4},{7,5},{8,10},{9,11},{10,... | collective-permute-start | bytes 786440 | tf_op jit(solution)/shard_map/ppermute | solution.py:312
  15.6 6.6 %collective-permute-start.5 = (f32[4,128,128]{2,1,0:T(8,128)S(1)}, f32[4,128,128]{2,1,0:T(8,128)S(1)}, u32[]{:S(2)}, u32[]{:S(2)}) collective-permute-start(f32[4,128,128]{2,1,0:T(8,128)S(1)} %shard_map.74.refs_0_), channel_id=1, source_target_pairs={{0,1},{1,5},{2,3},{3,7},{4,0},{5,4},{6,2},{7,6},{8,9},{9,13},{10,1... | collective-permute-start | bytes 786440 | tf_op jit(solution)/shard_map/ppermute | solution.py:271
  21.0 6.4 %collective-permute-start.2 = (f32[4,128,128]{2,1,0:T(8,128)S(1)}, f32[4,128,128]{2,1,0:T(8,128)S(1)}, u32[]{:S(2)}, u32[]{:S(2)}) collective-permute-start(f32[4,128,128]{2,1,0:T(8,128)S(1)} %shard_map.70.refs_2_.refs_0_), channel_id=1, source_target_pairs={{0,1},{1,5},{2,3},{3,7},{4,0},{5,4},{6,2},{7,6},{8,9},{9,13},{10,1... | collective-permute-start | bytes 786440 | tf_op jit(solution)/shard_map/ppermute | solution.py:271
  22.3 7.4 %collective-permute-start.10 = (f32[4,128,128]{2,1,0:T(8,128)S(1)}, f32[4,128,128]{2,1,0:T(8,128)S(1)}, u32[]{:S(2)}, u32[]{:S(2)}) collective-permute-start(f32[4,128,128]{2,1,0:T(8,128)S(1)} %get-tuple-element.59.refs_0_), channel_id=1, source_target_pairs={{0,1},{1,0},{2,3},{3,2},{4,5},{5,9},{6,7},{7,11},{8,4},{9,8},{10,6... | collective-permute-start | bytes 786440 | tf_op jit(solution)/shard_map/ppermute | solution.py:271
  22.3 10.2 %collective-permute-start.9 = (f32[4,128,128]{2,1,0:T(8,128)S(1)}, f32[4,128,128]{2,1,0:T(8,128)S(1)}, u32[]{:S(2)}, u32[]{:S(2)}) collective-permute-start(f32[4,128,128]{2,1,0:T(8,128)S(1)} %get-tuple-element.59.refs_0_), channel_id=1, source_target_pairs={{0,1},{1,4},{2,3},{3,6},{4,5},{5,13},{6,7},{7,15},{8,0},{9,8},{10,... | collective-permute-start | bytes 786440 | tf_op jit(solution)/shard_map/ppermute | solution.py:271
  27.5 7.8 %collective-permute-start.6 = (f32[4,128,128]{2,1,0:T(8,128)S(1)}, f32[4,128,128]{2,1,0:T(8,128)S(1)}, u32[]{:S(2)}, u32[]{:S(2)}) collective-permute-start(f32[4,128,128]{2,1,0:T(8,128)S(1)} %get-tuple-element.61.refs_0_.refs_6_), channel_id=1, source_target_pairs={{0,1},{1,4},{2,3},{3,6},{4,5},{5,13},{6,7},{7,15},{8,0},{9,8},{10,... | collective-permute-start | bytes 786440 | tf_op jit(solution)/shard_map/ppermute | solution.py:271
  27.6 7.8 %collective-permute-start.7 = (f32[4,128,128]{2,1,0:T(8,128)S(1)}, f32[4,128,128]{2,1,0:T(8,128)S(1)}, u32[]{:S(2)}, u32[]{:S(2)}) collective-permute-start(f32[4,128,128]{2,1,0:T(8,128)S(1)} %get-tuple-element.61.refs_0_.refs_6_), channel_id=1, source_target_pairs={{0,1},{1,0},{2,3},{3,2},{4,5},{5,9},{6,7},{7,11},{8,4},{9,8},{10,6... | collective-permute-start | bytes 786440 | tf_op jit(solution)/shard_map/ppermute | solution.py:271
  32.6 8.8 %collective-permute-start.13 = (f32[4,128,128]{2,1,0:T(8,128)S(1)}, f32[4,128,128]{2,1,0:T(8,128)S(1)}, u32[]{:S(2)}, u32[]{:S(2)}) collective-permute-start(f32[4,128,128]{2,1,0:T(8,128)S(1)} %get-tuple-element.68), channel_id=1, source_target_pairs={{0,2},{1,3},{2,0},{3,1},{4,6},{5,7},{6,4},{7,5},{8,10},{9,11},{10,... | collective-permute-start | bytes 786440 | tf_op jit(solution)/shard_map/ppermute | solution.py:350
  35.4 8.8 %collective-permute-start.8 = (f32[4,128,128]{2,1,0:T(8,128)S(1)}, f32[4,128,128]{2,1,0:T(8,128)S(1)}, u32[]{:S(2)}, u32[]{:S(2)}) collective-permute-start(f32[4,128,128]{2,1,0:T(8,128)S(1)} %get-tuple-element.64), channel_id=1, source_target_pairs={{0,2},{1,3},{2,0},{3,1},{4,6},{5,7},{6,4},{7,5},{8,10},{9,11},{10,... | collective-permute-start | bytes 786440 | tf_op jit(solution)/shard_map/ppermute | solution.py:350
  37.0 7.2 %collective-permute-start.11 = (f32[4,128,128]{2,1,0:T(8,128)S(1)}, f32[4,128,128]{2,1,0:T(8,128)S(1)}, u32[]{:S(2)}, u32[]{:S(2)}) collective-permute-start(f32[4,128,128]{2,1,0:T(8,128)S(1)} %get-tuple-element.67.refs_4_), channel_id=1, source_target_pairs={{0,1},{1,0},{2,3},{3,2},{4,5},{5,4},{6,7},{7,6},{8,9},{9,8},{10,11... | collective-permute-start | bytes 786440 | tf_op jit(solution)/shard_map/ppermute | solution.py:351
  37.0 7.2 %collective-permute-start.12 = (f32[4,128,128]{2,1,0:T(8,128)S(1)}, f32[4,128,128]{2,1,0:T(8,128)S(1)}, u32[]{:S(2)}, u32[]{:S(2)}) collective-permute-start(f32[4,128,128]{2,1,0:T(8,128)S(1)} %get-tuple-element.63.refs_4_), channel_id=1, source_target_pairs={{0,1},{1,0},{2,3},{3,2},{4,5},{5,4},{6,7},{7,6},{8,9},{9,8},{10,11... | collective-permute-start | bytes 786440 | tf_op jit(solution)/shard_map/ppermute | solution.py:351
  41.4 2.8 %collective-permute-start.14 = (f32[4,128,128]{2,1,0:T(8,128)S(1)}, f32[4,128,128]{2,1,0:T(8,128)S(1)}, u32[]{:S(2)}, u32[]{:S(2)}) collective-permute-start(f32[4,128,128]{2,1,0:T(8,128)S(1)} %collective-permute-done.13.refs_5_), channel_id=1, source_target_pairs={{0,1},{1,0},{2,3},{3,2},{4,5},{5,4},{6,7},{7,6},{8,9},{9,8},{10,11... | collective-permute-start | bytes 786440 | tf_op jit(solution)/shard_map/ppermute | solution.py:360
  44.2 2.1 %collective-permute-start.15 = (f32[4,128,128]{2,1,0:T(8,128)S(1)}, f32[4,128,128]{2,1,0:T(8,128)S(1)}, u32[]{:S(2)}, u32[]{:S(2)}) collective-permute-start(f32[4,128,128]{2,1,0:T(8,128)S(1)} %collective-permute-done.8.refs_5_), channel_id=1, source_target_pairs={{0,1},{1,0},{2,3},{3,2},{4,5},{5,4},{6,7},{7,6},{8,9},{9,8},{10,11... | collective-permute-start | bytes 786440 | tf_op jit(solution)/shard_map/ppermute | solution.py:360

commit v7 on v6

--- a/solution.py
+++ b/solution.py
@@ -16,7 +16,7 @@
     ((0, 0), ("kept", 1), ("plane", 0)),
     ((0, 1), ("kept", 1), ("plane", 0)),
     ((1, 0), ("window0", 0), ("window0", 1)),
-    ((1, 1), ("window0", 1), ("scan", 0)),
+    ((1, 1), ("back", 0), ("scan", 1)),
 )
 F32 = jnp.float32
 BF16 = jnp.bfloat16
@@ -323,19 +323,36 @@
         name = f"window{number}"
         for c in chunks:
 
-            def more(window, *arrived):
+            def more(window, kept, *arrived):
+                _, second = place()
                 add = masked(jnp.zeros_like(window), arrived[: len(plans)], plans)
-                return window + add, sum(arrived[len(plans) :], add)
+                total = sum(arrived[len(plans) :], add)
+                return window + add, total, total + jnp.where(second, 0.0, kept)
 
             window = made[last, c]
             arrived = [moved(window, plan) for plan in plans]
             held = [] if made["before", c] is None else [made["before", c]]
-            made[name, c], made["before", c] = sums(more, 2, [window, *arrived, *held], stage(name, c, last))
+            terms = [window, made["kept", c], *arrived, *held]
+            made[name, c], made["before", c], made["early", c] = sums(more, 3, terms, stage(name, c, last))
         last = name
 
+    needing = set().union(*levels[-1])
+    late_pairs = []
+    for i in range(seq):
+        plane = i // 4 if i % 2 else planes - 1 - i // 4
+        beside = i // 4 + (1 if (plane % 2 == 0) == (i % 2 == 1) else -1)
+        late_pairs.append((i, i ^ 2 if plane in needing else 4 * beside + i % 4))
+
+    def is_late():
+        later, _ = place()
+        plane = lax.axis_index("seq") // 4
+        plane = jnp.where(later, plane, planes - 1 - plane)
+        return functools.reduce(jnp.logical_or, [plane == to for to in needing])
+
+    early = [lax.ppermute(made["early", c], "seq", chip_pairs) for c in chunks]
     done = []
     for c in chunks:
-        plans = levels[-1]
+        plans = levels[-1][:: -1 if c else 1]
 
         def ready(kept, partner, *arrived):
             _, second = place()
@@ -346,8 +363,9 @@
         arrived = [moved(made[last, c], plan) for plan in plans]
         held = [] if made["before", c] is None else [made["before", c]]
         terms = [made["kept", c], made["partner", c], *arrived, *held]
-        made["back", c], kept_upto = sums(ready, 2, terms, stage("scan", c, last))
-        swapped = lax.ppermute(made["back", c], "seq", chip_pairs)
+        made["back", c], kept_upto = sums(ready, 2, terms, stage("scan", c, last) + [early[c]])
+        late = lax.ppermute(made["back", c], "seq", late_pairs)
+        (swapped,) = sums(lambda late, early: (jnp.where(is_late(), late, early),), 1, [late, early[c]])
         done.append((made["other", c], kept_upto, swapped, lax.ppermute(kept_upto, "seq", core_pairs)))
 
     out, others = (), []

time: 49.3 us -> 48.9 us (level)
  the two profiles are of different devices: /device:TPU:0 before, /device:TPU:9 now
where the time goes in v7:
time: 48.9 us; the launch traced here: 48.7 us
  starting transfers between devices  20.1 us (41%)
  Pallas kernels  17.5 us (36%)
  waiting for transfers between devices  10.1 us (21%)
  between operations  0.98 us (2%)
    pallas_call x4, Pallas kernels, within(): pl.pallas_call(functools.partial(within_kernel, first, heads, scale), out...  8.2 us
    ppermute x6, starting transfers between devices, moved(): return lax.ppermute(value, 'seq', sorted(pairs.items()))  7.71 us
    ppermute x2, waiting for transfers between devices, local(): made['partner', c] = lax.ppermute(sent, 'seq', chip_pairs)  5.28 us
    pallas_call x2, Pallas kernels, final(): pl.pallas_call(functools.partial(final_kernel, first, size // 2, scale),...  4.09 us
    pallas_call x2, Pallas kernels, load(): pl.pallas_call(functools.partial(load_kernel, first, size, len(after)), o...  3.81 us
    ppermute x2, starting transfers between devices, local(): lax.ppermute(kept_upto, 'seq', core_pairs)  3.26 us
    ppermute x2, starting transfers between devices, local(): given_swapped = lax.ppermute(swapped, 'seq', core_pairs)  3.2 us
    ppermute x2, waiting for transfers between devices, local(): late = lax.ppermute(made['back', c], 'seq', late_pairs)  2.56 us
  transfers between devices with their start and end apart: 18, of which 4 were waited for; matrix products, arithmetic and copies ran while one was open for 0% of the time, Pallas kernels for 28%

profile of v7, /device:TPU:9, one launch (start us, length us, event | category | flops | bytes accessed | tf_op | source)
XLA Modules:
  0.0 48.7 jit_solution(9059996588438736207)
XLA Ops:
  0.6 2.0 %shard_map.67 = (f32[8,128,128]{2,1,0:T(8,128)S(1)}, bf16[384,1024]{1,0:T(8,128)(2,1)S(1)}, bf16[384,1024]{1,0:T(8,128)(2,1)S(1)}, bf16[384,1024]{1,0:T(8,128)(2,1)S(1)}, bf16[384,1024]{1,0:T(8,128)(2,1)S(1)}) custom-call(bf16[384,2048]{1,0:T(8,128)(2,1)} %q_ref.3, bf16[384,2048]{1,0:T(8,128)(2,1)} %k_ref.3, bf16[384,2048]{1,0:T(8,128)(2,1)} %v_ref.3, ...), custom_call_target="tpu_custom_call" | custom-call | tf_op jit(solution)/shard_map/pallas_call | solution.py:91
  2.7 0.7 %collective-permute-start.3 = (f32[8,128,128]{2,1,0:T(8,128)S(1)}, f32[8,128,128]{2,1,0:T(8,128)S(1)}, u32[]{:S(2)}, u32[]{:S(2)}) collective-permute-start(f32[8,128,128]{2,1,0:T(8,128)S(1)} %get-tuple-element.45.refs_0_), channel_id=1, source_target_pairs={{0,1},{1,0},{2,3},{3,2},{4,5},{5,4},{6,7},{7,6},{8,9},{9,8},{10,11... | collective-permute-start | bytes 1572872 | tf_op jit(solution)/shard_map/ppermute | solution.py:310
  3.4 1.8 %shard_map.68 = (f32[8,128,128]{2,1,0:T(8,128)S(1)}, bf16[384,1024]{1,0:T(8,128)(2,1)S(1)}, bf16[384,1024]{1,0:T(8,128)(2,1)S(1)}, bf16[384,1024]{1,0:T(8,128)(2,1)S(1)}, bf16[384,1024]{1,0:T(8,128)(2,1)S(1)}) custom-call(bf16[384,2048]{1,0:T(8,128)(2,1)S(1)} %copy-done, bf16[384,2048]{1,0:T(8,128)(2,1)} %k_ref.3, bf16[384,2048]{1,0:T(8,128)(2,1)} %v_ref.3, ...), custom_call_target="tpu_custom_call" | custom-call | tf_op jit(solution)/shard_map/pallas_call | solution.py:91
  5.2 0.4 collective-permute-start
  5.6 0.4 shard_map.71
  6.1 1.3 %collective-permute-start.4 = (f32[4,128,128]{2,1,0:T(8,128)S(1)}, f32[4,128,128]{2,1,0:T(8,128)S(1)}, u32[]{:S(2)}, u32[]{:S(2)}) collective-permute-start(f32[4,128,128]{2,1,0:T(8,128)S(1)} %get-tuple-element.58), channel_id=1, source_target_pairs={{0,2},{1,3},{2,0},{3,1},{4,6},{5,7},{6,4},{7,5},{8,10},{9,11},{10,... | collective-permute-start | bytes 786440 | tf_op jit(solution)/shard_map/ppermute | solution.py:312
  7.3 0.4 shard_map.69
  7.8 2.1 %shard_map.73 = (bf16[384,512]{1,0:T(8,128)(2,1)S(1)}, bf16[384,512]{1,0:T(8,128)(2,1)S(1)}, bf16[384,512]{1,0:T(8,128)(2,1)S(1)}) custom-call(bf16[384,1024]{1,0:T(8,128)(2,1)S(1)} %get-tuple-element.53.q_ref, bf16[384,1024]{1,0:T(8,128)(2,1)S(1)} %get-tuple-element.54.k_ref.refs_0_, bf16[384,1024]{1,0:T(8,128)(2,1)S(1)} %get-tuple-element.55.v_ref.refs_1_, ...), custom_call_target="tpu_custom_call" | custom-call | tf_op jit(solution)/shard_map/pallas_call | solution.py:182
  9.8 2.1 %shard_map.72 = (bf16[384,512]{1,0:T(8,128)(2,1)S(1)}, bf16[384,512]{1,0:T(8,128)(2,1)S(1)}, bf16[384,512]{1,0:T(8,128)(2,1)S(1)}) custom-call(bf16[384,1024]{1,0:T(8,128)(2,1)S(1)} %get-tuple-element.53.q_ref, bf16[384,1024]{1,0:T(8,128)(2,1)S(1)} %get-tuple-element.54.k_ref.refs_0_, bf16[384,1024]{1,0:T(8,128)(2,1)S(1)} %get-tuple-element.55.v_ref.refs_1_, ...), custom_call_target="tpu_custom_call" | custom-call | tf_op jit(solution)/shard_map/pallas_call | solution.py:182
  11.9 1.1 %collective-permute-start.1 = (f32[4,128,128]{2,1,0:T(8,128)S(1)}, f32[4,128,128]{2,1,0:T(8,128)S(1)}, u32[]{:S(2)}, u32[]{:S(2)}) collective-permute-start(f32[4,128,128]{2,1,0:T(8,128)S(1)} %get-tuple-element.52), channel_id=1, source_target_pairs={{0,2},{1,3},{2,0},{3,1},{4,6},{5,7},{6,4},{7,5},{8,10},{9,11},{10,... | collective-permute-start | bytes 786440 | tf_op jit(solution)/shard_map/ppermute | solution.py:312
  13.0 0.8 %collective-permute-done.4.refs_1_ = f32[4,128,128]{2,1,0:T(8,128)S(1)} collective-permute-done((f32[4,128,128]{2,1,0:T(8,128)S(1)}, f32[4,128,128]{2,1,0:T(8,128)S(1)}, u32[]{:S(2)}, u32[]{:S(2)}) %collective-permute-start.4) | collective-permute-done | bytes 262176 | tf_op jit(solution)/shard_map/ppermute | solution.py:312
  13.9 1.0 %collective-permute-start.5 = (f32[4,128,128]{2,1,0:T(8,128)S(1)}, f32[4,128,128]{2,1,0:T(8,128)S(1)}, u32[]{:S(2)}, u32[]{:S(2)}) collective-permute-start(f32[4,128,128]{2,1,0:T(8,128)S(1)} %shard_map.74.refs_0_), channel_id=1, source_target_pairs={{0,1},{1,5},{2,3},{3,7},{4,0},{5,4},{6,2},{7,6},{8,9},{9,13},{10,1... | collective-permute-start | bytes 786440 | tf_op jit(solution)/shard_map/ppermute | solution.py:271
  14.9 4.4 %collective-permute-done.1.refs_1_ = f32[4,128,128]{2,1,0:T(8,128)S(1)} collective-permute-done((f32[4,128,128]{2,1,0:T(8,128)S(1)}, f32[4,128,128]{2,1,0:T(8,128)S(1)}, u32[]{:S(2)}, u32[]{:S(2)}) %collective-permute-start.1) | collective-permute-done | bytes 262176 | tf_op jit(solution)/shard_map/ppermute | solution.py:312
  19.4 1.4 %collective-permute-start.2 = (f32[4,128,128]{2,1,0:T(8,128)S(1)}, f32[4,128,128]{2,1,0:T(8,128)S(1)}, u32[]{:S(2)}, u32[]{:S(2)}) collective-permute-start(f32[4,128,128]{2,1,0:T(8,128)S(1)} %shard_map.70.refs_3_.refs_0_), channel_id=1, source_target_pairs={{0,1},{1,5},{2,3},{3,7},{4,0},{5,4},{6,2},{7,6},{8,9},{9,13},{10,1... | collective-permute-start | bytes 786440 | tf_op jit(solution)/shard_map/ppermute | solution.py:271
  20.9 1.1 %collective-permute-start.10 = (f32[4,128,128]{2,1,0:T(8,128)S(1)}, f32[4,128,128]{2,1,0:T(8,128)S(1)}, u32[]{:S(2)}, u32[]{:S(2)}) collective-permute-start(f32[4,128,128]{2,1,0:T(8,128)S(1)} %get-tuple-element.66), channel_id=1, source_target_pairs={{0,2},{1,3},{2,0},{3,1},{4,6},{5,7},{6,4},{7,5},{8,10},{9,11},{10,... | collective-permute-start | bytes 786440 | tf_op jit(solution)/shard_map/ppermute | solution.py:352
  22.0 1.5 %collective-permute-start.9 = (f32[4,128,128]{2,1,0:T(8,128)S(1)}, f32[4,128,128]{2,1,0:T(8,128)S(1)}, u32[]{:S(2)}, u32[]{:S(2)}) collective-permute-start(f32[4,128,128]{2,1,0:T(8,128)S(1)} %get-tuple-element.61.refs_0_), channel_id=1, source_target_pairs={{0,1},{1,0},{2,3},{3,2},{4,5},{5,9},{6,7},{7,11},{8,4},{9,8},{10,6... | collective-permute-start | bytes 786440 | tf_op jit(solution)/shard_map/ppermute | solution.py:271
  23.5 1.6 %collective-permute-start.8 = (f32[4,128,128]{2,1,0:T(8,128)S(1)}, f32[4,128,128]{2,1,0:T(8,128)S(1)}, u32[]{:S(2)}, u32[]{:S(2)}) collective-permute-start(f32[4,128,128]{2,1,0:T(8,128)S(1)} %get-tuple-element.61.refs_0_), channel_id=1, source_target_pairs={{0,1},{1,4},{2,3},{3,6},{4,5},{5,13},{6,7},{7,15},{8,0},{9,8},{10,... | collective-permute-start | bytes 786440 | tf_op jit(solution)/shard_map/ppermute | solution.py:271
  25.0 2.1 %shard_map.76 = (bf16[384,512]{1,0:T(8,128)(2,1)S(1)}, bf16[384,512]{1,0:T(8,128)(2,1)S(1)}, bf16[384,512]{1,0:T(8,128)(2,1)S(1)}) custom-call(bf16[384,1024]{1,0:T(8,128)(2,1)S(1)} %get-tuple-element.50.q_ref, bf16[384,1024]{1,0:T(8,128)(2,1)S(1)} %get-tuple-element.46.k_ref.refs_0_, bf16[384,1024]{1,0:T(8,128)(2,1)S(1)} %get-tuple-element.47.v_ref.refs_1_, ...), custom_call_target="tpu_custom_call" | custom-call | tf_op jit(solution)/shard_map/pallas_call | solution.py:182
  27.2 0.5 collective-permute-start.11
  27.7 1.0 %collective-permute-start.7 = (f32[4,128,128]{2,1,0:T(8,128)S(1)}, f32[4,128,128]{2,1,0:T(8,128)S(1)}, u32[]{:S(2)}, u32[]{:S(2)}) collective-permute-start(f32[4,128,128]{2,1,0:T(8,128)S(1)} %get-tuple-element.63.refs_5_), channel_id=1, source_target_pairs={{0,1},{1,4},{2,3},{3,6},{4,5},{5,13},{6,7},{7,15},{8,0},{9,8},{10,... | collective-permute-start | bytes 786440 | tf_op jit(solution)/shard_map/ppermute | solution.py:271
  28.7 1.2 %collective-permute-start.6 = (f32[4,128,128]{2,1,0:T(8,128)S(1)}, f32[4,128,128]{2,1,0:T(8,128)S(1)}, u32[]{:S(2)}, u32[]{:S(2)}) collective-permute-start(f32[4,128,128]{2,1,0:T(8,128)S(1)} %get-tuple-element.63.refs_5_), channel_id=1, source_target_pairs={{0,1},{1,0},{2,3},{3,2},{4,5},{5,9},{6,7},{7,11},{8,4},{9,8},{10,6... | collective-permute-start | bytes 786440 | tf_op jit(solution)/shard_map/ppermute | solution.py:271
  30.1 0.2 collective-permute-start.15
  30.3 2.0 %shard_map.79 = (bf16[384,512]{1,0:T(8,128)(2,1)S(1)}, bf16[384,512]{1,0:T(8,128)(2,1)S(1)}, bf16[384,512]{1,0:T(8,128)(2,1)S(1)}) custom-call(bf16[384,1024]{1,0:T(8,128)(2,1)S(1)} %get-tuple-element.50.q_ref, bf16[384,1024]{1,0:T(8,128)(2,1)S(1)} %get-tuple-element.46.k_ref.refs_0_, bf16[384,1024]{1,0:T(8,128)(2,1)S(1)} %get-tuple-element.47.v_ref.refs_1_, ...), custom_call_target="tpu_custom_call" | custom-call | tf_op jit(solution)/shard_map/pallas_call | solution.py:182
  32.4 1.0 %collective-permute-start.13 = (f32[4,128,128]{2,1,0:T(8,128)S(1)}, f32[4,128,128]{2,1,0:T(8,128)S(1)}, u32[]{:S(2)}, u32[]{:S(2)}) collective-permute-start(f32[4,128,128]{2,1,0:T(8,128)S(1)} %get-tuple-element.72.refs_4_), channel_id=1, source_target_pairs={{0,1},{1,0},{2,3},{3,2},{4,5},{5,4},{6,7},{7,6},{8,9},{9,8},{10,11... | collective-permute-start | bytes 786440 | tf_op jit(solution)/shard_map/ppermute | solution.py:369
  33.3 2.2 %collective-permute-done.11.refs_6_.refs_1_ = f32[4,128,128]{2,1,0:T(8,128)S(1)} collective-permute-done((f32[4,128,128]{2,1,0:T(8,128)S(1)}, f32[4,128,128]{2,1,0:T(8,128)S(1)}, u32[]{:S(2)}, u32[]{:S(2)}) %collective-permute-start.11) | collective-permute-done | bytes 262176 | tf_op jit(solution)/shard_map/ppermute | solution.py:352
  35.5 0.1 shard_map.80
  35.7 0.6 %collective-permute-start.12 = (f32[4,128,128]{2,1,0:T(8,128)S(1)}, f32[4,128,128]{2,1,0:T(8,128)S(1)}, u32[]{:S(2)}, u32[]{:S(2)}) collective-permute-start(f32[4,128,128]{2,1,0:T(8,128)S(1)} %get-tuple-element.71), channel_id=1, source_target_pairs={{0,2},{1,5},{2,0},{3,7},{4,6},{5,1},{6,4},{7,3},{8,12},{9,11},{10,... | collective-permute-start | bytes 786440 | tf_op jit(solution)/shard_map/ppermute | solution.py:367
  36.3 2.3 %collective-permute-start.14 = (f32[4,128,128]{2,1,0:T(8,128)S(1)}, f32[4,128,128]{2,1,0:T(8,128)S(1)}, u32[]{:S(2)}, u32[]{:S(2)}) collective-permute-start(f32[4,128,128]{2,1,0:T(8,128)S(1)} %get-tuple-element.70.refs_4_), channel_id=1, source_target_pairs={{0,1},{1,0},{2,3},{3,2},{4,5},{5,4},{6,7},{7,6},{8,9},{9,8},{10,11... | collective-permute-start | bytes 786440 | tf_op jit(solution)/shard_map/ppermute | solution.py:369
  38.7 2.6 %collective-permute-done.12.refs_0_ = f32[4,128,128]{2,1,0:T(8,128)S(1)} collective-permute-done((f32[4,128,128]{2,1,0:T(8,128)S(1)}, f32[4,128,128]{2,1,0:T(8,128)S(1)}, u32[]{:S(2)}, u32[]{:S(2)}) %collective-permute-start.12) | collective-permute-done | bytes 262176 | tf_op jit(solution)/shard_map/ppermute | solution.py:367
  41.3 3.1 %collective-permute-start.17 = (f32[4,128,128]{2,1,0:T(8,128)S(1)}, f32[4,128,128]{2,1,0:T(8,128)S(1)}, u32[]{:S(2)}, u32[]{:S(2)}) collective-permute-start(f32[4,128,128]{2,1,0:T(8,128)S(1)} %shard_map.81.refs_5_), channel_id=1, source_target_pairs={{0,1},{1,0},{2,3},{3,2},{4,5},{5,4},{6,7},{7,6},{8,9},{9,8},{10,11... | collective-permute-start | bytes 786440 | tf_op jit(solution)/shard_map/ppermute | solution.py:378
  44.5 2.0 %shard_map.83 = (bf16[384,2048]{1,0:T(8,128)(2,1)}, bf16[384,2048]{1,0:T(8,128)(2,1)}, bf16[384,2048]{1,0:T(8,128)(2,1)}) custom-call(bf16[384,1024]{1,0:T(8,128)(2,1)S(1)} %get-tuple-element.54.k_ref.refs_0_, bf16[384,1024]{1,0:T(8,128)(2,1)S(1)} %get-tuple-element.55.v_ref.refs_1_, bf16[384,1024]{1,0:T(8,128)(2,1)S(1)} %get-tuple-element.56.g_ref.refs_2_, ...), custom_call_target="tpu_custom_call" | custom-call | tf_op jit(solution)/shard_map/pallas_call | solution.py:236
  46.5 2.1 %shard_map.84 = (bf16[384,2048]{1,0:T(8,128)(2,1)}, bf16[384,2048]{1,0:T(8,128)(2,1)}, bf16[384,2048]{1,0:T(8,128)(2,1)}) custom-call(bf16[384,1024]{1,0:T(8,128)(2,1)S(1)} %get-tuple-element.46.k_ref.refs_0_, bf16[384,1024]{1,0:T(8,128)(2,1)S(1)} %get-tuple-element.47.v_ref.refs_1_, ...), custom_call_target="tpu_custom_call", output_to_operand_aliasing={{0}: (14, {}), {1}: (15, {}), {2}: (16, {})} | custom-call | tf_op jit(solution)/shard_map/pallas_call | solution.py:236
  (24 shorter events, 0.5 us)
Async XLA Ops:
  0.6 2.8 %copy-start = (bf16[384,2048]{1,0:T(8,128)(2,1)S(1)}, bf16[384,2048]{1,0:T(8,128)(2,1)}, u32[]{:S(2)}) copy-start(bf16[384,2048]{1,0:T(8,128)(2,1)} %q_ref.3) | copy-start | bytes 4718596
  2.7 2.9 %collective-permute-start.3 = (f32[8,128,128]{2,1,0:T(8,128)S(1)}, f32[8,128,128]{2,1,0:T(8,128)S(1)}, u32[]{:S(2)}, u32[]{:S(2)}) collective-permute-start(f32[8,128,128]{2,1,0:T(8,128)S(1)} %get-tuple-element.45.refs_0_), channel_id=1, source_target_pairs={{0,1},{1,0},{2,3},{3,2},{4,5},{5,4},{6,7},{7,6},{8,9},{9,8},{10,11... | collective-permute-start | bytes 1572872 | tf_op jit(solution)/shard_map/ppermute | solution.py:310
  5.2 2.1 %collective-permute-start = (f32[8,128,128]{2,1,0:T(8,128)S(1)}, f32[8,128,128]{2,1,0:T(8,128)S(1)}, u32[]{:S(2)}, u32[]{:S(2)}) collective-permute-start(f32[8,128,128]{2,1,0:T(8,128)S(1)} %get-tuple-element.49), channel_id=1, source_target_pairs={{0,1},{1,0},{2,3},{3,2},{4,5},{5,4},{6,7},{7,6},{8,9},{9,8},{10,11... | collective-permute-start | bytes 1572872 | tf_op jit(solution)/shard_map/ppermute | solution.py:310
  6.1 7.8 %collective-permute-start.4 = (f32[4,128,128]{2,1,0:T(8,128)S(1)}, f32[4,128,128]{2,1,0:T(8,128)S(1)}, u32[]{:S(2)}, u32[]{:S(2)}) collective-permute-start(f32[4,128,128]{2,1,0:T(8,128)S(1)} %get-tuple-element.58), channel_id=1, source_target_pairs={{0,2},{1,3},{2,0},{3,1},{4,6},{5,7},{6,4},{7,5},{8,10},{9,11},{10,... | collective-permute-start | bytes 786440 | tf_op jit(solution)/shard_map/ppermute | solution.py:312
  11.9 7.5 %collective-permute-start.1 = (f32[4,128,128]{2,1,0:T(8,128)S(1)}, f32[4,128,128]{2,1,0:T(8,128)S(1)}, u32[]{:S(2)}, u32[]{:S(2)}) collective-permute-start(f32[4,128,128]{2,1,0:T(8,128)S(1)} %get-tuple-element.52), channel_id=1, source_target_pairs={{0,2},{1,3},{2,0},{3,1},{4,6},{5,7},{6,4},{7,5},{8,10},{9,11},{10,... | collective-permute-start | bytes 786440 | tf_op jit(solution)/shard_map/ppermute | solution.py:312
  13.9 6.9 %collective-permute-start.5 = (f32[4,128,128]{2,1,0:T(8,128)S(1)}, f32[4,128,128]{2,1,0:T(8,128)S(1)}, u32[]{:S(2)}, u32[]{:S(2)}) collective-permute-start(f32[4,128,128]{2,1,0:T(8,128)S(1)} %shard_map.74.refs_0_), channel_id=1, source_target_pairs={{0,1},{1,5},{2,3},{3,7},{4,0},{5,4},{6,2},{7,6},{8,9},{9,13},{10,1... | collective-permute-start | bytes 786440 | tf_op jit(solution)/shard_map/ppermute | solution.py:271
  19.4 7.7 %collective-permute-start.2 = (f32[4,128,128]{2,1,0:T(8,128)S(1)}, f32[4,128,128]{2,1,0:T(8,128)S(1)}, u32[]{:S(2)}, u32[]{:S(2)}) collective-permute-start(f32[4,128,128]{2,1,0:T(8,128)S(1)} %shard_map.70.refs_3_.refs_0_), channel_id=1, source_target_pairs={{0,1},{1,5},{2,3},{3,7},{4,0},{5,4},{6,2},{7,6},{8,9},{9,13},{10,1... | collective-permute-start | bytes 786440 | tf_op jit(solution)/shard_map/ppermute | solution.py:271
  20.9 7.8 %collective-permute-start.10 = (f32[4,128,128]{2,1,0:T(8,128)S(1)}, f32[4,128,128]{2,1,0:T(8,128)S(1)}, u32[]{:S(2)}, u32[]{:S(2)}) collective-permute-start(f32[4,128,128]{2,1,0:T(8,128)S(1)} %get-tuple-element.66), channel_id=1, source_target_pairs={{0,2},{1,3},{2,0},{3,1},{4,6},{5,7},{6,4},{7,5},{8,10},{9,11},{10,... | collective-permute-start | bytes 786440 | tf_op jit(solution)/shard_map/ppermute | solution.py:352
  22.0 8.0 %collective-permute-start.9 = (f32[4,128,128]{2,1,0:T(8,128)S(1)}, f32[4,128,128]{2,1,0:T(8,128)S(1)}, u32[]{:S(2)}, u32[]{:S(2)}) collective-permute-start(f32[4,128,128]{2,1,0:T(8,128)S(1)} %get-tuple-element.61.refs_0_), channel_id=1, source_target_pairs={{0,1},{1,0},{2,3},{3,2},{4,5},{5,9},{6,7},{7,11},{8,4},{9,8},{10,6... | collective-permute-start | bytes 786440 | tf_op jit(solution)/shard_map/ppermute | solution.py:271
  23.5 6.5 %collective-permute-start.8 = (f32[4,128,128]{2,1,0:T(8,128)S(1)}, f32[4,128,128]{2,1,0:T(8,128)S(1)}, u32[]{:S(2)}, u32[]{:S(2)}) collective-permute-start(f32[4,128,128]{2,1,0:T(8,128)S(1)} %get-tuple-element.61.refs_0_), channel_id=1, source_target_pairs={{0,1},{1,4},{2,3},{3,6},{4,5},{5,13},{6,7},{7,15},{8,0},{9,8},{10,... | collective-permute-start | bytes 786440 | tf_op jit(solution)/shard_map/ppermute | solution.py:271
  27.2 8.3 %collective-permute-start.11 = (f32[4,128,128]{2,1,0:T(8,128)S(1)}, f32[4,128,128]{2,1,0:T(8,128)S(1)}, u32[]{:S(2)}, u32[]{:S(2)}) collective-permute-start(f32[4,128,128]{2,1,0:T(8,128)S(1)} %get-tuple-element.69), channel_id=1, source_target_pairs={{0,2},{1,3},{2,0},{3,1},{4,6},{5,7},{6,4},{7,5},{8,10},{9,11},{10,... | collective-permute-start | bytes 786440 | tf_op jit(solution)/shard_map/ppermute | solution.py:352
  27.7 7.9 %collective-permute-start.7 = (f32[4,128,128]{2,1,0:T(8,128)S(1)}, f32[4,128,128]{2,1,0:T(8,128)S(1)}, u32[]{:S(2)}, u32[]{:S(2)}) collective-permute-start(f32[4,128,128]{2,1,0:T(8,128)S(1)} %get-tuple-element.63.refs_5_), channel_id=1, source_target_pairs={{0,1},{1,4},{2,3},{3,6},{4,5},{5,13},{6,7},{7,15},{8,0},{9,8},{10,... | collective-permute-start | bytes 786440 | tf_op jit(solution)/shard_map/ppermute | solution.py:271
  28.7 6.8 %collective-permute-start.6 = (f32[4,128,128]{2,1,0:T(8,128)S(1)}, f32[4,128,128]{2,1,0:T(8,128)S(1)}, u32[]{:S(2)}, u32[]{:S(2)}) collective-permute-start(f32[4,128,128]{2,1,0:T(8,128)S(1)} %get-tuple-element.63.refs_5_), channel_id=1, source_target_pairs={{0,1},{1,0},{2,3},{3,2},{4,5},{5,9},{6,7},{7,11},{8,4},{9,8},{10,6... | collective-permute-start | bytes 786440 | tf_op jit(solution)/shard_map/ppermute | solution.py:271
  30.1 8.5 %collective-permute-start.15 = (f32[4,128,128]{2,1,0:T(8,128)S(1)}, f32[4,128,128]{2,1,0:T(8,128)S(1)}, u32[]{:S(2)}, u32[]{:S(2)}) collective-permute-start(f32[4,128,128]{2,1,0:T(8,128)S(1)} %get-tuple-element.67.refs_0_), channel_id=1, source_target_pairs={{0,2},{1,5},{2,0},{3,7},{4,6},{5,1},{6,4},{7,3},{8,12},{9,11},{10,... | collective-permute-start | bytes 786440 | tf_op jit(solution)/shard_map/ppermute | solution.py:367
  32.4 8.9 %collective-permute-start.13 = (f32[4,128,128]{2,1,0:T(8,128)S(1)}, f32[4,128,128]{2,1,0:T(8,128)S(1)}, u32[]{:S(2)}, u32[]{:S(2)}) collective-permute-start(f32[4,128,128]{2,1,0:T(8,128)S(1)} %get-tuple-element.72.refs_4_), channel_id=1, source_target_pairs={{0,1},{1,0},{2,3},{3,2},{4,5},{5,4},{6,7},{7,6},{8,9},{9,8},{10,11... | collective-permute-start | bytes 786440 | tf_op jit(solution)/shard_map/ppermute | solution.py:369
  35.7 5.6 %collective-permute-start.12 = (f32[4,128,128]{2,1,0:T(8,128)S(1)}, f32[4,128,128]{2,1,0:T(8,128)S(1)}, u32[]{:S(2)}, u32[]{:S(2)}) collective-permute-start(f32[4,128,128]{2,1,0:T(8,128)S(1)} %get-tuple-element.71), channel_id=1, source_target_pairs={{0,2},{1,5},{2,0},{3,7},{4,6},{5,1},{6,4},{7,3},{8,12},{9,11},{10,... | collective-permute-start | bytes 786440 | tf_op jit(solution)/shard_map/ppermute | solution.py:367
  36.3 5.0 %collective-permute-start.14 = (f32[4,128,128]{2,1,0:T(8,128)S(1)}, f32[4,128,128]{2,1,0:T(8,128)S(1)}, u32[]{:S(2)}, u32[]{:S(2)}) collective-permute-start(f32[4,128,128]{2,1,0:T(8,128)S(1)} %get-tuple-element.70.refs_4_), channel_id=1, source_target_pairs={{0,1},{1,0},{2,3},{3,2},{4,5},{5,4},{6,7},{7,6},{8,9},{9,8},{10,11... | collective-permute-start | bytes 786440 | tf_op jit(solution)/shard_map/ppermute | solution.py:369
  38.6 2.7 %collective-permute-start.16 = (f32[4,128,128]{2,1,0:T(8,128)S(1)}, f32[4,128,128]{2,1,0:T(8,128)S(1)}, u32[]{:S(2)}, u32[]{:S(2)}) collective-permute-start(f32[4,128,128]{2,1,0:T(8,128)S(1)} %shard_map.82.refs_5_), channel_id=1, source_target_pairs={{0,1},{1,0},{2,3},{3,2},{4,5},{5,4},{6,7},{7,6},{8,9},{9,8},{10,11... | collective-permute-start | bytes 786440 | tf_op jit(solution)/shard_map/ppermute | solution.py:378
  41.3 5.2 %collective-permute-start.17 = (f32[4,128,128]{2,1,0:T(8,128)S(1)}, f32[4,128,128]{2,1,0:T(8,128)S(1)}, u32[]{:S(2)}, u32[]{:S(2)}) collective-permute-start(f32[4,128,128]{2,1,0:T(8,128)S(1)} %shard_map.81.refs_5_), channel_id=1, source_target_pairs={{0,1},{1,0},{2,3},{3,2},{4,5},{5,4},{6,7},{7,6},{8,9},{9,8},{10,11... | collective-permute-start | bytes 786440 | tf_op jit(solution)/shard_map/ppermute | solution.py:378
